TPU v7x, 256 devices: a whole 4x4x8 slice. The times are simulated.
256 devices in a mesh: row: 16 (over x, y), col: 16 (over z, core).
Axes of the slice: x: 4, y: 4, z: 8, core: 2. Of those that a mesh axis runs over, the one named last changes fastest.
Arguments:
- iterate: float32 [6, 24576, 320], P(None, ('row', 'col')), may hold values from -6 to 6
- residual: float32 [6, 24576, 320], P(None, ('row', 'col')), may hold values from -114 to 114
- shadow: float32 [2, 24576, 320], P(None, ('row', 'col')), may hold values from -6 to 6
- res_dirs: float32 [2, 6, 24576, 320], P(None, None, ('row', 'col')), may hold values from -75 to 75
- sol_dirs: float32 [2, 6, 24576, 320], P(None, None, ('row', 'col')), may hold values from -69 to 69
- omega_step: float32 [6], replicated, may hold values from 0.3 to 1
- face_blocks: bfloat16 [24576, 4, 80, 80], P(('row', 'col')), may hold values from -1 to 1
- send_list: int32 [1024, 48], P(('row', 'col')), may hold values from 0 to 95
- neighbour_perm: int32 [256, 384], P(('row', 'col')), may hold values from 0 to 383, each once within a row
- wall_perm: int32 [256, 96], P(('row', 'col')), may hold values from 0 to 95, each once within a row
- wall_count: int32 [256], P(('row', 'col')), may hold values from 1 to 48, 6144 in all
- wall_coef: bfloat16 [3, 5, 196608], P(None, None, ('row', 'col')), may hold values from -2.5 to 2.5
- rbf_support: int32 [1536, 4], P(('row', 'col')), may hold values from 0 to 95
- rbf_weights: bfloat16 [1536, 4, 128, 128], P(('row', 'col')), may hold values from -0.25 to 0.25
Outputs:
- iterate_out: float32 [6, 24576, 320], P(None, ('row', 'col'))
- residual_out: float32 [6, 24576, 320], P(None, ('row', 'col'))
- smoothed: float32 [18, 196608], P(None, ('row', 'col'))
Inputs may be any that keep to these rules, and one draw needn't show every extreme that they name: `neighbour_perm`: each device's row lists every one of its 384 face slots once. `wall_perm`: each device's row lists every local element once. `wall_count`: some device has exactly 48 wall elements.
All inputs are finite; a program needn't handle non-finite values.
Results may differ from a plain program's by a relative error of at most 0.0065.
Values may be sent and summed in bfloat16 or wider, within the bound.
No kernel may reach another device: no remote copies, remote signals or barrier semaphores. Data moves between devices by JAX's collectives and lax.ppermute only.
A program may use at most 128 MiB of HBM per device.

v0:
```python
import functools

import jax
import jax.numpy as jnp
import numpy as np
from jax import lax
from jax.experimental import pallas as pl
from jax.experimental.pallas import tpu as pltpu
from jax.sharding import PartitionSpec as P

NVAR = 5
NOBJ = 6
E = 96
H = 48
WMAX = 48
BLOCK = 320
TRACE = 80
LANES = 128
NBLK = 6
NSUP = 4
NBAS = 3
NVEC = NOBJ * NBAS
WIDE = NVEC * LANES
STEP = NBAS * LANES
SLOTS = 4 * H
FACES = 4 * E
VPAD = 24
BPAD = 24
F32 = jnp.float32
BF16 = jnp.bfloat16


def selection():
    sel = np.zeros((BLOCK, 4 * LANES), np.float32)
    for var in range(NVAR):
        for a in range(4):
            for c in range(4):
                i = var * 16 + a * 4 + c
                base = var * 64
                sel[base + 48 + a * 4 + c, 0 * LANES + i] = 1
                sel[base + a * 4 + c, 1 * LANES + i] = 1
                sel[base + a * 16 + 12 + c, 2 * LANES + i] = 1
                sel[base + a * 16 + c, 3 * LANES + i] = 1
    return sel


def wall_spread():
    out = np.zeros((BLOCK, LANES), np.float32)
    for var in range(NVAR):
        for p in range(16):
            out[var * 64 + p * 4, p::16] = 1
    return out


def dot(a, b, dims=((1,), (0,))):
    return lax.dot_general(a, b, (dims, ((), ())), preferred_element_type=F32)


def split(x):
    high = x.astype(BF16)
    return high, (x - high.astype(F32)).astype(BF16)


def one_hot_rows(index, width):
    lane = lax.broadcasted_iota(jnp.int32, (index.shape[0], width), 1)
    return jnp.where(lane == index, 1.0, 0.0).astype(BF16)


def picker(send_row):
    row = lax.broadcasted_iota(jnp.int32, (E, H), 0)
    return jnp.where(row == send_row, 1.0, 0.0).astype(BF16)


def basis_kernel(om, send, sel, r, d, s, sh, dots, thi, tlo, outgo):
    k = pl.program_id(0)
    w = om[k]
    r0, d0, d1 = r[0], d[0, 0], d[1, 0]
    us = [w * r0, w * d0 + s[0, 0], w * d1 + s[1, 0]]
    for x, vec in enumerate([r0, d0, d1] + us):
        for i in range(2):
            dots[0, pl.ds(2 * x + i, 1), :] = jnp.sum(sh[i] * vec, axis=0, keepdims=True)
    dots[0, 12:16, :] = jnp.zeros((4, BLOCK), F32)
    picks = [picker(send[f : f + 1, :]) for f in range(4)]
    for m, u in enumerate(us):
        at = slice(m * LANES, (m + 1) * LANES)
        high, low = split(u)
        traces = dot(high, sel[...]).astype(BF16)
        rest = dot(low[H:], sel[...]).astype(BF16)
        for f in range(4):
            face = traces[:, f * LANES : (f + 1) * LANES]
            thi[f * H : (f + 1) * H, at] = face[H:]
            tlo[f * H : (f + 1) * H, at] = rest[:, f * LANES : (f + 1) * LANES]
            outgo[f, :, at] = dot(picks[f], face, ((0,), (0,))).astype(BF16)


def blocks_kernel(_, b, sh, selt, eye, wt, q, scratch, qscr):
    trsh = []
    for i in range(2):
        high, low = split(sh[i])
        nt = ((1,), (1,))
        trsh.append((dot(selt[...], high, nt) + dot(selt[...], low, nt))[:TRACE])

    def step(n, carry):
        for c in range(8):
            i = n * 8 + c
            x = b[0, i]
            scratch[pl.ds(i, E, stride=TRACE), 0:TRACE] = dot(eye[...], x, ((1,), (1,)))
            x = x.astype(F32)
            for a in range(2):
                qscr[a, pl.ds(i, 1), :] = jnp.sum(x * trsh[a], axis=0, keepdims=True)
        return carry

    lax.fori_loop(0, TRACE // 8, step, 0)

    def pack(n, carry):
        for c in range(4):
            e = n * 4 + c
            at = pl.ds(pl.multiple_of(e * TRACE, TRACE), TRACE)
            wt[0, e] = scratch[at, 0:TRACE].astype(BF16)
        return carry

    lax.fori_loop(0, E // 4, pack, 0)
    for a in range(2):
        q[a, :, 0:TRACE] = qscr[a].T
        q[a, :, TRACE:LANES] = jnp.zeros((E, LANES - TRACE), F32)


def received(flags, recv, at):
    return [jnp.where(flags[d] > 0, ref[:, at], jnp.zeros((), BF16)) for d, ref in enumerate(recv)]


def reduce_kernel(flags, cidx, thi, tlo, r0, r1, r2, r3, q, dots, out, hot, rows, acc):
    k = pl.program_id(0)

    @pl.when(k == 0)
    def _():
        hot[...] = one_hot_rows(cidx[...], 2 * SLOTS)
        rows[...] = jnp.zeros_like(rows)
        acc[...] = jnp.zeros_like(acc)

    full = slice(0, STEP)
    table = jnp.concatenate(received(flags, (r0, r1, r2, r3), full) + [thi[...]], axis=0)
    t = dot(hot[...], table) + dot(hot[:, SLOTS:], tlo[...])
    for m in range(NBAS):
        for i in range(2):
            part = t[:, m * LANES : (m + 1) * LANES] * q[i]
            rows[pl.ds(6 + 2 * m + i, 1), :] = jnp.sum(part, axis=0, keepdims=True)
    col = jnp.sum(rows[...], axis=1, keepdims=True) + jnp.sum(dots[0], axis=1, keepdims=True)
    lane = lax.broadcasted_iota(jnp.int32, (16, LANES), 1)
    acc[...] += jnp.where(lane == k, col, 0.0)
    out[...] = jnp.broadcast_to(acc[...][None], out.shape)


def merge_kernel(x, out):
    out[...] = jnp.broadcast_to(jnp.sum(x[...], axis=0, keepdims=True), out.shape)


def couple(t_ref, wt, y_ref, pad):
    def step(n, carry):
        for c in range(8):
            face = n * 8 + c
            at = pl.ds(pl.multiple_of(face * pad, 8), pad)
            y_ref[at, 0:TRACE] = dot(t_ref[at, 0:TRACE].astype(BF16), wt[face])
        return carry

    lax.fori_loop(0, FACES // 8, step, 0)


def apply_kernel(flags, cidx, send, thi, tlo, r0, r1, r2, r3, wt, cross, _, outgo, yn, t_ref, y_ref):
    hot = one_hot_rows(cidx[...], 2 * SLOTS)
    for k in range(NOBJ):
        at = slice(k * STEP, (k + 1) * STEP)
        table = jnp.concatenate(received(flags, (r0, r1, r2, r3), at) + [thi[:, at]], axis=0)
        t = dot(hot, table)
        for f in range(4):
            for m in range(NBAS):
                rows = pl.ds(f * E * VPAD + k * NBAS + m, E, stride=VPAD)
                t_ref[rows, :] = t[f * E : (f + 1) * E, m * LANES : (m + 1) * LANES]
    couple(t_ref, wt, y_ref, VPAD)
    picks = [picker(send[f : f + 1, :]) for f in range(4)]
    for v in range(NVEC):
        total = None
        for f in range(4):
            y = y_ref[pl.ds(f * E * VPAD + v, E, stride=VPAD), :][:, 0:TRACE]
            yn[v, f, :, 0:TRACE] = y
            part = dot(y.astype(BF16), cross[f * LANES : f * LANES + TRACE, :])
            total = part if total is None else total + part
        total = total.astype(BF16)
        for f in range(4):
            face = total[:, f * LANES : (f + 1) * LANES]
            outgo[f, :, v * LANES : (v + 1) * LANES] = dot(picks[f], face, ((0,), (0,))).astype(BF16)


def solve(m00, m01, m10, m11, f0, f1):
    det = m00 * m11 - m01 * m10
    return (m11 * f0 - m01 * f1) / det, (m00 * f1 - m10 * f0) / det


def step_kernel(
    red, om, r, d, s, it, yn, selt, wsel, coef, spread, itout, base, st2, coefs, payload, co, scr
):
    k = pl.program_id(0)

    @pl.when(k == 0)
    def _():
        t = jnp.sum(red[...], axis=0)
        row = lambda n: t[n : n + 1]
        w = om[...]
        c0, c1 = solve(row(2), row(4), row(3), row(5), row(0), row(1))
        n0 = -(row(6) - c0 * row(8) - c1 * row(10))
        n1 = -(row(7) - c0 * row(9) - c1 * row(11))
        e0, e1 = solve(n0, row(4), n1, row(5), row(0) + n0, row(1) + n1)
        gamma = w * (1.0 - e0)
        delta = gamma + e0
        for n, x in enumerate([w, c0, c1, 1.0 - delta, delta * c0, delta * c1 - e1, gamma]):
            co[pl.ds(n, 1), :] = x
        co[7:8, :] = jnp.zeros((1, LANES), F32)
        coefs[...] = co[...]
        scr[...] = jnp.zeros_like(scr)

    lane = lax.broadcasted_iota(jnp.int32, (8, LANES), 1)
    col = jnp.sum(jnp.where(lane == k, co[...], 0.0), axis=1, keepdims=True)
    c = [col[n : n + 1] for n in range(7)]
    r0 = r[0]
    u0 = c[0] * r0
    u1 = c[0] * d[0, 0] + s[0, 0]
    u2 = c[0] * d[1, 0] + s[1, 0]
    st1 = u0 - c[1] * u1 - c[2] * u2
    lift = None
    for f in range(4):
        y = yn[0, f] - c[1] * yn[1, f] - c[2] * yn[2, f]
        high, low = split(y[:, 0:TRACE])
        block = selt[f * LANES : f * LANES + TRACE, :]
        part = dot(high, block) + dot(low, block)
        lift = part if lift is None else lift + part
    two = c[3] * u0 + c[4] * u1 + c[5] * u2 - c[6] * lift
    new = it[0] + st1 + two
    itout[0] = new
    st2[0] = two
    base[0] = r0 - st1 - lift - two
    high, low = split(new)
    picked = dot(wsel[...], high) + dot(wsel[...], low)
    slot = lax.broadcasted_iota(jnp.int32, (WMAX, LANES), 0) % 8
    group = lax.broadcasted_iota(jnp.int32, (WMAX, LANES), 1) // 16
    for a in range(3):
        high, low = split(picked * coef[a])
        part = dot(high, spread[...]) + dot(low, spread[...])
        part = jnp.where(slot == group, part, 0.0).reshape(NBLK, 8, LANES)
        scr[pl.ds(a * NOBJ + k, NBLK, stride=BPAD), :] = jnp.sum(part, axis=1)

    @pl.when(k == NOBJ - 1)
    def _():
        payload[...] = jnp.broadcast_to(scr[...].astype(BF16)[None], payload.shape)


def last_kernel(
    flags, coefs, cidx, st2, base, a0, a1, a2, a3, b0, b1, b2, b3, wt, sel, selt, _, out, t_ref, y_ref
):
    hot = one_hot_rows(cidx[...], 2 * SLOTS)
    for k in range(NOBJ):
        c = [coefs[n : n + 1, k : k + 1] for n in range(7)]
        rows = []
        for d, (a, b) in enumerate(zip((a0, a1, a2, a3), (b0, b1, b2, b3))):
            u = [a[:, (k * NBAS + m) * LANES : (k * NBAS + m + 1) * LANES].astype(F32) for m in range(3)]
            y = [b[:, (k * NBAS + m) * LANES : (k * NBAS + m + 1) * LANES].astype(F32) for m in range(3)]
            x = c[3] * u[0] + c[4] * u[1] + c[5] * u[2] - c[6] * (y[0] - c[1] * y[1] - c[2] * y[2])
            rows.append(jnp.where(flags[d] > 0, x, 0.0).astype(BF16))
        local = dot(st2[k, H:, :].astype(BF16), sel[...]).astype(BF16)
        rows += [local[:, f * LANES : (f + 1) * LANES] for f in range(4)]
        t = dot(hot, jnp.concatenate(rows, axis=0))
        for f in range(4):
            t_ref[pl.ds(f * E * 8 + k, E, stride=8), :] = t[f * E : (f + 1) * E]
    couple(t_ref, wt, y_ref, 8)
    for k in range(NOBJ):
        lift = None
        for f in range(4):
            high, low = split(y_ref[pl.ds(f * E * 8 + k, E, stride=8), :][:, 0:TRACE])
            block = selt[f * LANES : f * LANES + TRACE, :]
            part = dot(high, block) + dot(low, block)
            lift = part if lift is None else lift + part
        out[k] = base[k] - lift


def smooth_kernel(support, sens, weights, out, scr):
    scr[...] = sens[...].astype(F32)
    for m in range(NBLK):
        acc = None
        for s in range(NSUP):
            at = pl.multiple_of(support[m, s] * BPAD, 8)
            part = dot(scr[pl.ds(at, BPAD), :].astype(BF16), weights[m, s])
            acc = part if acc is None else acc + part
        out[:, m * LANES : (m + 1) * LANES] = acc[: 3 * NOBJ]


SMEM = pl.BlockSpec(memory_space=pltpu.SMEM)
ANY = pl.BlockSpec(memory_space=pl.ANY)
VMEM = pl.BlockSpec(memory_space=pltpu.VMEM)
call = functools.partial(pl.pallas_call)


def params(mib):
    return pltpu.CompilerParams(vmem_limit_bytes=mib << 20)


def cost(us):
    return pl.CostEstimate(flops=int(us * 5e8), bytes_accessed=int(us * 3e6), transcendentals=0)


def shape(dims, dtype):
    return jax.ShapeDtypeStruct(dims, dtype)


def whole(dims):
    return pl.BlockSpec(dims, lambda *_: (0,) * len(dims))


def exchange(outgo):
    recv = []
    for d, (axis, shift) in enumerate((("row", 1), ("row", -1), ("col", 1), ("col", -1))):
        size = lax.axis_size(axis)
        recv.append(lax.ppermute(outgo[d], axis, [(i, (i + shift) % size) for i in range(size)]))
    return recv


def per_device(
    iterate,
    residual,
    shadow,
    res_dirs,
    sol_dirs,
    omega_step,
    face_blocks,
    send_list,
    neighbour_perm,
    wall_perm,
    wall_count,
    wall_coef,
    rbf_support,
    rbf_weights,
):
    n_row, n_col = lax.axis_size("row"), lax.axis_size("col")
    sel_np = selection()
    sel = jnp.asarray(sel_np, BF16)
    selt = jnp.asarray(sel_np.T, BF16)
    cross = jnp.asarray(sel_np.T @ sel_np, BF16)
    spread = jnp.asarray(wall_spread(), BF16)
    eye = jnp.asarray(np.eye(E), BF16)

    one = pl.BlockSpec((1, E, BLOCK), lambda k: (k, 0, 0))
    pair = pl.BlockSpec((2, 1, E, BLOCK), lambda k: (0, k, 0, 0))
    lanes = pl.BlockSpec((SLOTS, STEP), lambda k: (0, k))
    dots, thi, tlo, outgo = call(
        basis_kernel,
        grid=(NOBJ,),
        in_specs=[SMEM, whole((4, H)), whole(sel.shape), one, pair, pair, whole((2, E, BLOCK))],
        out_specs=[
            pl.BlockSpec((1, 16, BLOCK), lambda k: (k, 0, 0)),
            lanes,
            lanes,
            pl.BlockSpec((4, H, STEP), lambda k: (0, 0, k)),
        ],
        out_shape=[
            shape((NOBJ, 16, BLOCK), F32),
            shape((SLOTS, WIDE), BF16),
            shape((SLOTS, WIDE), BF16),
            shape((4, H, WIDE), BF16),
        ],
        compiler_params=params(16),
        cost_estimate=cost(5),
        name="basis",
    )(omega_step, send_list, sel, residual, res_dirs, sol_dirs, shadow)
    recv = exchange(outgo)

    neighbour_perm, wall_perm, wall_count, wall_coef, omega_row, dots = lax.optimization_barrier(
        (neighbour_perm, wall_perm, wall_count, wall_coef, omega_step, dots)
    )
    slot = neighbour_perm.reshape(E, 4).T.reshape(FACES, 1)
    cidx = jnp.where(slot < SLOTS, slot, SLOTS + (slot % 4) * H + slot // 4 - H)
    row, col = lax.axis_index("row"), lax.axis_index("col")
    flags = jnp.stack([row > 0, row < n_row - 1, col > 0, col < n_col - 1]).astype(jnp.int32)
    live = jnp.arange(WMAX) < wall_count[0]
    wsel = (live[:, None] & (wall_perm[0, :WMAX, None] == jnp.arange(E))).astype(BF16)
    coef = wall_coef.reshape(3, NVAR, WMAX, 16).transpose(0, 2, 1, 3)
    coef = jnp.pad(coef[..., None], ((0, 0),) * 4 + ((0, 3),)).reshape(3, WMAX, BLOCK).astype(F32)
    om_row = jnp.pad(omega_row[None], ((0, 0), (0, LANES - NOBJ)))

    wt, q = call(
        blocks_kernel,
        grid=(4,),
        in_specs=[
            ANY,
            pl.BlockSpec((1, TRACE, TRACE, E), lambda f: (f, 0, 0, 0)),
            whole((2, E, BLOCK)),
            pl.BlockSpec((LANES, BLOCK), lambda f: (f, 0)),
            whole((E, E)),
        ],
        out_specs=[
            pl.BlockSpec((1, E, TRACE, TRACE), lambda f: (f, 0, 0, 0)),
            pl.BlockSpec((2, E, LANES), lambda f: (0, f, 0)),
        ],
        out_shape=[shape((4, E, TRACE, TRACE), BF16), shape((2, FACES, LANES), F32)],
        scratch_shapes=[pltpu.VMEM((E * TRACE, LANES), F32), pltpu.VMEM((2, TRACE, E), F32)],
        compiler_params=params(24),
        cost_estimate=cost(8),
        name="blocks",
    )(dots, face_blocks.transpose(1, 2, 3, 0), shadow, selt, eye)
    wt = wt.reshape(FACES, TRACE, TRACE)

    chunk = pl.BlockSpec((H, STEP), lambda k: (0, k))
    red = call(
        reduce_kernel,
        grid=(NOBJ,),
        in_specs=[SMEM, whole((FACES, 1)), lanes, lanes]
        + [chunk] * 4
        + [whole((2, FACES, LANES)), pl.BlockSpec((1, 16, BLOCK), lambda k: (k, 0, 0))],
        out_specs=whole((n_row, 16, LANES)),
        out_shape=shape((n_row, 16, LANES), F32),
        scratch_shapes=[
            pltpu.VMEM((FACES, 2 * SLOTS), BF16),
            pltpu.VMEM((16, LANES), F32),
            pltpu.VMEM((16, LANES), F32),
        ],
        compiler_params=params(16),
        cost_estimate=cost(3),
        name="reduce",
    )(flags, cidx, thi, tlo, *recv, q, dots)
    red_row = lax.all_to_all(red, "row", 0, 0, tiled=True)

    outgo2, yn = call(
        apply_kernel,
        in_specs=[SMEM] + [VMEM] * 10 + [ANY],
        out_specs=[VMEM, VMEM],
        out_shape=[shape((4, H, WIDE), BF16), shape((NVEC, 4, E, LANES), F32)],
        scratch_shapes=[pltpu.VMEM((FACES * VPAD, LANES), F32)] * 2,
        compiler_params=params(36),
        cost_estimate=cost(8),
        name="apply",
    )(flags, cidx, send_list, thi, tlo, *recv, wt, cross, red)
    recv2 = exchange(outgo2)

    red_row = call(
        merge_kernel,
        out_shape=shape((n_col, 16, LANES), F32),
        in_specs=[VMEM],
        out_specs=VMEM,
        compiler_params=params(2),
        name="merge",
    )(red_row)
    red = lax.all_to_all(red_row, "col", 0, 0, tiled=True)

    itout, base, st2, coefs, payload = call(
        step_kernel,
        grid=(NOBJ,),
        in_specs=[
            whole((n_col, 16, LANES)),
            whole((1, LANES)),
            one,
            pair,
            pair,
            one,
            pl.BlockSpec((NBAS, 4, E, LANES), lambda k: (k, 0, 0, 0)),
            whole(selt.shape),
            whole((WMAX, E)),
            whole((3, WMAX, BLOCK)),
            whole((BLOCK, LANES)),
        ],
        out_specs=[one, one, one, whole((8, LANES)), whole((n_row, NBLK * BPAD, LANES))],
        out_shape=[
            shape((NOBJ, E, BLOCK), F32),
            shape((NOBJ, E, BLOCK), F32),
            shape((NOBJ, E, BLOCK), F32),
            shape((8, LANES), F32),
            shape((n_row, NBLK * BPAD, LANES), BF16),
        ],
        scratch_shapes=[pltpu.VMEM((8, LANES), F32), pltpu.VMEM((NBLK * BPAD, LANES), F32)],
        compiler_params=params(16),
        cost_estimate=cost(5),
        name="step",
    )(red, om_row, residual, res_dirs, sol_dirs, iterate, yn, selt, wsel, coef, spread)
    sens = lax.all_to_all(payload, "row", 0, 0, tiled=True)

    resout = call(
        last_kernel,
        in_specs=[SMEM] + [VMEM] * 15 + [ANY],
        out_specs=VMEM,
        out_shape=shape((NOBJ, E, BLOCK), F32),
        scratch_shapes=[pltpu.VMEM((FACES * 8, LANES), F32)] * 2,
        compiler_params=params(32),
        cost_estimate=cost(8),
        name="last",
    )(flags, coefs, cidx, st2, base, *recv, *recv2, wt, sel, selt, payload)

    smoothed = call(
        smooth_kernel,
        in_specs=[SMEM, VMEM, VMEM],
        out_specs=VMEM,
        out_shape=shape((3 * NOBJ, NBLK * LANES), F32),
        scratch_shapes=[pltpu.VMEM((n_row * NBLK * BPAD, LANES), F32)],
        compiler_params=params(8),
        cost_estimate=cost(3),
        name="smooth",
    )(rbf_support, sens.reshape(-1, LANES), rbf_weights)
    return (itout, resout, smoothed)


def solution(mesh):
    both = ("row", "col")
    in_specs = (
        P(None, both, None),
        P(None, both, None),
        P(None, both, None),
        P(None, None, both, None),
        P(None, None, both, None),
        P(),
        P(both, None, None, None),
        P(both, None),
        P(both, None),
        P(both, None),
        P(both),
        P(None, None, both),
        P(both, None),
        P(both, None, None, None),
    )
    out_specs = (P(None, both, None), P(None, both, None), P(None, both))
    return jax.shard_map(
        per_device, mesh=mesh, in_specs=in_specs, out_specs=out_specs, check_vma=False
    )
```

profile of v0, /device:TPU:1, one launch (start us, length us, event | category | flops | bytes accessed | tf_op | source)
XLA Modules:
  0.0 162.6 jit_solution(7435267006470634546)
XLA Ops:
  0.6 1.5 copy-done
  2.1 1.5 copy-done.2
  3.6 1.2 copy-done.4
  4.8 1.0 copy-done.28
  7.1 1.0 copy-done.52
  8.0 6.2 %basis.1 = (f32[6,16,320]{2,1,0:T(8,128)S(1)}, bf16[192,2304]{1,0:T(8,128)(2,1)S(1)}, bf16[192,2304]{1,0:T(8,128)(2,1)S(1)}, bf16[4,48,2304]{2,1,0:T(8,128)(2,1)S(1)}) custom-call(f32[6]{0:T(128)S(1)} %copy-done.46, s32[4,48]{1,0:T(4,128)S(1)} %copy-done.44, bf16[320,512]{1,0:T(8,128)(2,1)S(1)} %copy-done.52, f32[6,96,320]{2,1,0:T(8,128)S(1)} %copy-done.4, ...), custom_call_target="tpu_custom_call" | custom-call | flops 2500000000 | bytes 15000000 | tf_op jit(solution)/shard_map/basis/pallas_call | solution.py:352
  15.2 2.1 %collective-permute-start = (bf16[48,2304]{1,0:T(8,128)(2,1)}, bf16[48,2304]{1,0:T(8,128)(2,1)S(1)}, u32[]{:S(2)}, u32[]{:S(2)}) collective-permute-start(bf16[48,2304]{1,0:T(8,128)(2,1)} %get-tuple-element.48), channel_id=1, source_target_pairs={{0,16},{16,32},{32,48},{48,64},{64,80},{80,96},{96,112},{112,128},... | collective-permute-start | bytes 663560 | tf_op jit(solution)/shard_map/ppermute | solution.py:321
  17.3 3.6 %collective-permute-start.1 = (bf16[48,2304]{1,0:T(8,128)(2,1)}, bf16[48,2304]{1,0:T(8,128)(2,1)S(1)}, u32[]{:S(2)}, u32[]{:S(2)}) collective-permute-start(bf16[48,2304]{1,0:T(8,128)(2,1)} %get-tuple-element.47), channel_id=1, source_target_pairs={{0,240},{16,0},{32,16},{48,32},{64,48},{80,64},{96,80},{112,96},{1... | collective-permute-start | bytes 663560 | tf_op jit(solution)/shard_map/ppermute | solution.py:321
  21.0 2.6 %collective-permute-start.2 = (bf16[48,2304]{1,0:T(8,128)(2,1)}, bf16[48,2304]{1,0:T(8,128)(2,1)S(1)}, u32[]{:S(2)}, u32[]{:S(2)}) collective-permute-start(bf16[48,2304]{1,0:T(8,128)(2,1)} %get-tuple-element.46), channel_id=1, source_target_pairs={{0,1},{1,2},{2,3},{3,4},{4,5},{5,6},{6,7},{7,8},{8,9},{9,10},{10,1... | collective-permute-start | bytes 663560 | tf_op jit(solution)/shard_map/ppermute | solution.py:321
  25.5 1.0 copy.33
  26.5 1.9 %copy.34.coef = f32[3,48,320]{2,1,0:T(8,128)} copy(f32[3,48,320]{1,2,0:T(8,128)} %bitcast.39) | data formatting | bytes 368640 | tf_op jit(solution)/shard_map/convert_element_type | solution.py:384
  28.5 2.9 %copy-done.22 = bf16[96,4,80,80]{0,3,2,1:T(8,128)(2,1)S(1)} copy-done((bf16[96,4,80,80]{0,3,2,1:T(8,128)(2,1)S(1)}, bf16[96,4,80,80]{0,3,2,1:T(8,128)(2,1)}, u32[]{:S(2)}) %copy-start.22) | copy-done | bytes 4915224
  31.4 14.0 %blocks.1 = (bf16[4,96,80,80]{3,2,1,0:T(8,128)(2,1)S(1)}, f32[2,384,128]{2,1,0:T(8,128)S(1)}) custom-call(f32[6,16,320]{2,1,0:T(8,128)S(1)} %get-tuple-element.27._.dots, bf16[4,80,80,96]{3,2,1,0:T(8,128)(2,1)S(1)} %bitcast.35, f32[2,96,320]{2,1,0:T(8,128)S(1)} %copy-done.29, bf16[512,320]{1,0:T(8,128)(2,1)S(1)} %copy-done.12, bf16[96,96]{1,0:T(8,128)(2,1)S(1)} %copy-done.54), custom_call_target="tpu_custom_call" | custom-call | flops 4000000000 | bytes 24000000 | tf_op jit(solution)/shard_map/blocks/pallas_call | solution.py:387
  45.4 3.1 %copy-done.48 = bf16[4,96,80,80]{3,2,1,0:T(8,128)(2,1)} copy-done((bf16[4,96,80,80]{3,2,1,0:T(8,128)(2,1)}, bf16[4,96,80,80]{3,2,1,0:T(8,128)(2,1)S(1)}, u32[]{:S(2)}) %copy-start.48) | copy-done | bytes 4915224
  49.2 5.4 %reduce.2._ = f32[16,16,128]{2,1,0:T(8,128)} custom-call(s32[4]{0:T(128)S(1)} %add_convert_fusion.flags, s32[384,1]{1,0:T(8,128)S(1)} %compare_select_fusion.cidx, bf16[192,2304]{1,0:T(8,128)(2,1)S(1)} %get-tuple-element.24.thi, bf16[192,2304]{1,0:T(8,128)(2,1)S(1)} %copy-done.58, bf16[48,2304]{1,0:T(8,128)(2,1)S(1)} %collective-permute-done.r0.a0, ...), custom_call_target="tpu_custom_call" | custom-call | flops 1500000000 | bytes 9000000 | tf_op jit(solution)/shard_map/reduce/pallas_call | solution.py:410
  54.6 4.2 %all-to-all-start = ((f32[16,16,128]{2,1,0:T(8,128)}), f32[16,16,128]{2,1,0:T(8,128)}, u32[]{:S(2)}, u32[]{:S(2)}) async-start(f32[16,16,128]{2,1,0:T(8,128)} %reduce.2._), calls=%async_computation | async-start | bytes 262144 | tf_op jit(solution)/shard_map/all_to_all | solution.py:427
  60.3 0.9 copy-done.31
  61.3 0.9 copy-done.34
  62.2 0.9 copy-done.37
  63.1 0.9 copy-done.40
  64.7 3.2 %copy-done.49 = bf16[4,96,80,80]{3,2,1,0:T(8,128)(2,1)S(1)} copy-done((bf16[4,96,80,80]{3,2,1,0:T(8,128)(2,1)S(1)}, bf16[4,96,80,80]{3,2,1,0:T(8,128)(2,1)}, u32[]{:S(2)}) %copy-start.49) | copy-done | bytes 4915224
  68.0 1.0 copy-done.51
  69.0 1.2 copy-done.56
  70.2 1.2 copy-done.59
  71.4 14.8 %apply.1 = (bf16[4,48,2304]{2,1,0:T(8,128)(2,1)S(1)}, f32[18,4,96,128]{3,2,1,0:T(8,128)S(1)}) custom-call(s32[4]{0:T(128)S(1)} %copy-done.20, s32[384,1]{1,0:T(8,128)S(1)} %copy-done.16, s32[4,48]{1,0:T(4,128)S(1)} %copy-done.45, bf16[192,2304]{1,0:T(8,128)(2,1)S(1)} %copy-done.56, bf16[192,2304]{1,0:T(8,128)(2,1)S(1)} %copy-done.59, ...), custom_call_target="tpu_custom_call" | custom-call | flops 4000000000 | bytes 24000000 | tf_op jit(solution)/shard_map/apply/pallas_call | solution.py:429
  88.6 9.7 %all-to-all-start.1 = ((f32[16,16,128]{2,1,0:T(8,128)}), f32[16,16,128]{2,1,0:T(8,128)}, u32[]{:S(2)}, u32[]{:S(2)}) async-start(f32[16,16,128]{2,1,0:T(8,128)} %copy-done.11), calls=%async_computation.1 | async-start | bytes 262144 | tf_op jit(solution)/shard_map/all_to_all | solution.py:449
  98.4 2.3 %slice_bitcast_fusion = (bf16[48,2304]{1,0:T(8,128)(2,1)}, bf16[48,2304]{1,0:T(8,128)(2,1)}, bf16[48,2304]{1,0:T(8,128)(2,1)}, bf16[48,2304]{1,0:T(8,128)(2,1)}) fusion(bf16[4,48,2304]{2,1,0:T(8,128)(2,1)} %copy-done.7), kind=kLoop, calls=%fused_computation.7 | loop fusion | bytes 1769472 | tf_op jit(solution)/shard_map/squeeze | solution.py:321
  100.6 1.5 collective-permute-start.4
  102.1 3.4 %collective-permute-start.5 = (bf16[48,2304]{1,0:T(8,128)(2,1)}, bf16[48,2304]{1,0:T(8,128)(2,1)}, u32[]{:S(2)}, u32[]{:S(2)}) collective-permute-start(bf16[48,2304]{1,0:T(8,128)(2,1)} %get-tuple-element.43), channel_id=1, source_target_pairs={{0,240},{16,0},{32,16},{48,32},{64,48},{80,64},{96,80},{112,96},{1... | collective-permute-start | bytes 663560 | tf_op jit(solution)/shard_map/ppermute | solution.py:321
  105.5 2.1 %collective-permute-start.6 = (bf16[48,2304]{1,0:T(8,128)(2,1)}, bf16[48,2304]{1,0:T(8,128)(2,1)}, u32[]{:S(2)}, u32[]{:S(2)}) collective-permute-start(bf16[48,2304]{1,0:T(8,128)(2,1)} %get-tuple-element.42), channel_id=1, source_target_pairs={{0,1},{1,2},{2,3},{3,4},{4,5},{5,6},{6,7},{7,8},{8,9},{9,10},{10,1... | collective-permute-start | bytes 663560 | tf_op jit(solution)/shard_map/ppermute | solution.py:321
  107.6 1.5 copy-done.1
  109.1 1.5 copy-done.3
  110.6 1.2 copy-done.5
  111.8 1.2 copy-done.6
  112.9 0.9 copy-done.8
  113.9 1.0 copy-done.13
  115.7 7.1 %step.1 = (f32[6,96,320]{2,1,0:T(8,128)}, f32[6,96,320]{2,1,0:T(8,128)S(1)}, f32[6,96,320]{2,1,0:T(8,128)S(1)}, f32[8,128]{1,0:T(8,128)S(1)}, bf16[16,144,128]{2,1,0:T(8,128)(2,1)S(1)}) custom-call(f32[16,16,128]{2,1,0:T(8,128)} %all-to-all-done.1.red, f32[1,128]{1,0:T(1,128)S(1)} %pad.8.om, f32[6,96,320]{2,1,0:T(8,128)S(1)} %copy-done.5, ...), custom_call_target="tpu_custom_call" | custom-call | flops 2500000000 | bytes 15000000 | tf_op jit(solution)/shard_map/step/pallas_call | solution.py:451
  126.1 6.8 %all-to-all-start.2 = ((bf16[16,144,128]{2,1,0:T(8,128)(2,1)}), bf16[16,144,128]{2,1,0:T(8,128)(2,1)S(1)}, u32[]{:S(2)}, u32[]{:S(2)}) async-start(bf16[16,144,128]{2,1,0:T(8,128)(2,1)} %copy-done.9), calls=%async_computation.2 | async-start | bytes 1179648 | tf_op jit(solution)/shard_map/all_to_all | solution.py:480
  133.7 1.1 copy-done.10
  134.8 1.0 copy-done.14
  137.3 1.2 copy-done.24
  138.5 1.2 copy-done.26
  139.6 0.9 copy-done.32
  142.4 0.9 copy-done.41
  144.1 3.2 %copy-done.50 = bf16[4,96,80,80]{3,2,1,0:T(8,128)(2,1)S(1)} copy-done((bf16[4,96,80,80]{3,2,1,0:T(8,128)(2,1)S(1)}, bf16[4,96,80,80]{3,2,1,0:T(8,128)(2,1)}, u32[]{:S(2)}) %copy-start.50) | copy-done | bytes 4915224
  147.3 1.0 copy-done.53
  148.3 12.7 %last.1 = f32[6,96,320]{2,1,0:T(8,128)} custom-call(s32[4]{0:T(128)S(1)} %copy-done.21, f32[8,128]{1,0:T(8,128)S(1)} %copy-done.43, s32[384,1]{1,0:T(8,128)S(1)} %copy-done.17, f32[6,96,320]{2,1,0:T(8,128)S(1)} %copy-done.26, f32[6,96,320]{2,1,0:T(8,128)S(1)} %copy-done.24, bf16[48,2304]{1,0:T(8,128)(2,1)S(1)} %copy-done.32, ...), custom_call_target="tpu_custom_call" | custom-call | flops 4000000000 | bytes 24000000 | tf_op jit(solution)/shard_map/last/pallas_call | solution.py:482
  161.0 1.6 smooth.1
  (126 shorter events, 17.7 us)
Async XLA Ops:
  0.6 1.5 copy-start
  2.1 1.5 copy-start.2
  3.6 1.2 copy-start.4
  7.1 1.0 copy-start.52
  8.0 16.4 %copy-start.61 = (s32[1,384]{1,0:T(1,128)S(1)}, s32[1,384]{1,0:T(1,128)}, u32[]{:S(2)}) copy-start(s32[1,384]{1,0:T(1,128)} %param.27) | copy-start | bytes 4612
  8.0 17.1 %copy-start.60 = (bf16[3,5,768]{2,0,1:T(4,128)(2,1)S(1)}, bf16[3,5,768]{2,0,1:T(4,128)(2,1)}, u32[]{:S(2)}) copy-start(bf16[3,5,768]{2,0,1:T(4,128)(2,1)} %param.30) | copy-start | bytes 69124
  14.3 9.3 %copy-start.57 = (bf16[192,2304]{1,0:T(8,128)(2,1)}, bf16[192,2304]{1,0:T(8,128)(2,1)S(1)}, u32[]{:S(2)}) copy-start(bf16[192,2304]{1,0:T(8,128)(2,1)S(1)} %get-tuple-element.25.tlo) | copy-start | bytes 2654212
  14.3 34.5 %copy-start.55 = (bf16[192,2304]{1,0:T(8,128)(2,1)}, bf16[192,2304]{1,0:T(8,128)(2,1)S(1)}, u32[]{:S(2)}) copy-start(bf16[192,2304]{1,0:T(8,128)(2,1)S(1)} %get-tuple-element.24.thi) | copy-start | bytes 2654212
  14.3 14.1 %copy-start.62 = (s32[1,96]{1,0:T(1,128)S(1)}, s32[1,96]{1,0:T(1,128)}, u32[]{:S(2)}) copy-start(s32[1,96]{1,0:T(1,128)} %param.28) | copy-start | bytes 1156
  14.3 14.1 %copy-start.47 = (f32[6]{0:T(128)S(1)}, f32[6]{0:T(128)}, u32[]{:S(2)}) copy-start(f32[6]{0:T(128)} %om.1) | copy-start | bytes 76
  14.3 14.2 %copy-start.12 = (bf16[512,320]{1,0:T(8,128)(2,1)S(1)}, bf16[512,320]{1,0:T(8,128)(2,1)}, u32[]{:S(2)}) copy-start(bf16[512,320]{1,0:T(8,128)(2,1)} %constant.59.clone.selt) | copy-start | bytes 983044
  14.3 14.1 %copy-start.29 = (f32[2,96,320]{2,1,0:T(8,128)S(1)}, f32[2,96,320]{2,1,0:T(8,128)}, u32[]{:S(2)}) copy-start(f32[2,96,320]{2,1,0:T(8,128)} %sh.3) | copy-start | bytes 737284
  14.4 14.1 %copy-start.54 = (bf16[96,96]{1,0:T(8,128)(2,1)S(1)}, bf16[96,96]{1,0:T(8,128)(2,1)}, u32[]{:S(2)}) copy-start(bf16[96,96]{1,0:T(8,128)(2,1)} %constant.62.clone.eye) | copy-start | bytes 55300
  15.2 33.5 %collective-permute-start = (bf16[48,2304]{1,0:T(8,128)(2,1)}, bf16[48,2304]{1,0:T(8,128)(2,1)S(1)}, u32[]{:S(2)}, u32[]{:S(2)}) collective-permute-start(bf16[48,2304]{1,0:T(8,128)(2,1)} %get-tuple-element.48), channel_id=1, source_target_pairs={{0,16},{16,32},{32,48},{48,64},{64,80},{80,96},{96,112},{112,128},... | collective-permute-start | bytes 663560 | tf_op jit(solution)/shard_map/ppermute | solution.py:321
  17.3 31.4 %collective-permute-start.1 = (bf16[48,2304]{1,0:T(8,128)(2,1)}, bf16[48,2304]{1,0:T(8,128)(2,1)S(1)}, u32[]{:S(2)}, u32[]{:S(2)}) collective-permute-start(bf16[48,2304]{1,0:T(8,128)(2,1)} %get-tuple-element.47), channel_id=1, source_target_pairs={{0,240},{16,0},{32,16},{48,32},{64,48},{80,64},{96,80},{112,96},{1... | collective-permute-start | bytes 663560 | tf_op jit(solution)/shard_map/ppermute | solution.py:321
  21.0 27.8 %collective-permute-start.2 = (bf16[48,2304]{1,0:T(8,128)(2,1)}, bf16[48,2304]{1,0:T(8,128)(2,1)S(1)}, u32[]{:S(2)}, u32[]{:S(2)}) collective-permute-start(bf16[48,2304]{1,0:T(8,128)(2,1)} %get-tuple-element.46), channel_id=1, source_target_pairs={{0,1},{1,2},{2,3},{3,4},{4,5},{5,6},{6,7},{7,8},{8,9},{9,10},{10,1... | collective-permute-start | bytes 663560 | tf_op jit(solution)/shard_map/ppermute | solution.py:321
  23.6 25.2 %collective-permute-start.3 = (bf16[48,2304]{1,0:T(8,128)(2,1)S(1)}, bf16[48,2304]{1,0:T(8,128)(2,1)S(1)}, u32[]{:S(2)}, u32[]{:S(2)}) collective-permute-start(bf16[48,2304]{1,0:T(8,128)(2,1)S(1)} %get-tuple-element.45), channel_id=1, source_target_pairs={{0,15},{1,0},{2,1},{3,2},{4,3},{5,4},{6,5},{7,6},{8,7},{9,8},{10,9... | collective-permute-start | bytes 663560 | tf_op jit(solution)/shard_map/ppermute | solution.py:321
  25.1 23.7 %copy-start.15 = (s32[384,1]{1,0:T(8,128)}, s32[384,1]{1,0:T(8,128)S(1)}, u32[]{:S(2)}) copy-start(s32[384,1]{1,0:T(8,128)S(1)} %compare_select_fusion.cidx) | copy-start | bytes 4612
  28.5 2.9 %copy-start.22 = (bf16[96,4,80,80]{0,3,2,1:T(8,128)(2,1)S(1)}, bf16[96,4,80,80]{0,3,2,1:T(8,128)(2,1)}, u32[]{:S(2)}) copy-start(bf16[96,4,80,80]{0,3,2,1:T(8,128)(2,1)} %param.25) | copy-start | bytes 14745604
  31.4 17.8 %copy-start.58 = (bf16[192,2304]{1,0:T(8,128)(2,1)S(1)}, bf16[192,2304]{1,0:T(8,128)(2,1)}, u32[]{:S(2)}) copy-start(bf16[192,2304]{1,0:T(8,128)(2,1)} %copy-done.57) | copy-start | bytes 2654212
  45.4 3.1 %copy-start.48 = (bf16[4,96,80,80]{3,2,1,0:T(8,128)(2,1)}, bf16[4,96,80,80]{3,2,1,0:T(8,128)(2,1)S(1)}, u32[]{:S(2)}) copy-start(bf16[4,96,80,80]{3,2,1,0:T(8,128)(2,1)S(1)} %get-tuple-element.30) | copy-start | bytes 14745604
  48.7 10.0 %copy-start.30 = (bf16[48,2304]{1,0:T(8,128)(2,1)}, bf16[48,2304]{1,0:T(8,128)(2,1)S(1)}, u32[]{:S(2)}) copy-start(bf16[48,2304]{1,0:T(8,128)(2,1)S(1)} %collective-permute-done.r0.a0) | copy-start | bytes 663556
  48.8 10.0 %copy-start.33 = (bf16[48,2304]{1,0:T(8,128)(2,1)}, bf16[48,2304]{1,0:T(8,128)(2,1)S(1)}, u32[]{:S(2)}) copy-start(bf16[48,2304]{1,0:T(8,128)(2,1)S(1)} %collective-permute-done.1.r1.a1) | copy-start | bytes 663556
  48.8 10.0 %copy-start.36 = (bf16[48,2304]{1,0:T(8,128)(2,1)}, bf16[48,2304]{1,0:T(8,128)(2,1)S(1)}, u32[]{:S(2)}) copy-start(bf16[48,2304]{1,0:T(8,128)(2,1)S(1)} %collective-permute-done.2.r2.a2) | copy-start | bytes 663556
  48.8 10.0 %copy-start.39 = (bf16[48,2304]{1,0:T(8,128)(2,1)}, bf16[48,2304]{1,0:T(8,128)(2,1)S(1)}, u32[]{:S(2)}) copy-start(bf16[48,2304]{1,0:T(8,128)(2,1)S(1)} %collective-permute-done.3.r3.a3) | copy-start | bytes 663556
  54.6 32.5 %all-to-all-start = ((f32[16,16,128]{2,1,0:T(8,128)}), f32[16,16,128]{2,1,0:T(8,128)}, u32[]{:S(2)}, u32[]{:S(2)}) async-start(f32[16,16,128]{2,1,0:T(8,128)} %reduce.2._), calls=%async_computation | async-start | bytes 262144 | tf_op jit(solution)/shard_map/all_to_all | solution.py:427
  64.7 3.2 %copy-start.49 = (bf16[4,96,80,80]{3,2,1,0:T(8,128)(2,1)S(1)}, bf16[4,96,80,80]{3,2,1,0:T(8,128)(2,1)}, u32[]{:S(2)}) copy-start(bf16[4,96,80,80]{3,2,1,0:T(8,128)(2,1)} %copy-done.48) | copy-start | bytes 14745604
  68.0 1.0 copy-start.51
  69.0 1.2 copy-start.56
  70.2 1.2 copy-start.59
  88.6 19.0 %all-to-all-start.1 = ((f32[16,16,128]{2,1,0:T(8,128)}), f32[16,16,128]{2,1,0:T(8,128)}, u32[]{:S(2)}, u32[]{:S(2)}) async-start(f32[16,16,128]{2,1,0:T(8,128)} %copy-done.11), calls=%async_computation.1 | async-start | bytes 262144 | tf_op jit(solution)/shard_map/all_to_all | solution.py:449
  100.6 33.1 %collective-permute-start.4 = (bf16[48,2304]{1,0:T(8,128)(2,1)}, bf16[48,2304]{1,0:T(8,128)(2,1)}, u32[]{:S(2)}, u32[]{:S(2)}) collective-permute-start(bf16[48,2304]{1,0:T(8,128)(2,1)} %get-tuple-element.44), channel_id=1, source_target_pairs={{0,16},{16,32},{32,48},{48,64},{64,80},{80,96},{96,112},{112,128},... | collective-permute-start | bytes 663560 | tf_op jit(solution)/shard_map/ppermute | solution.py:321
  102.1 31.6 %collective-permute-start.5 = (bf16[48,2304]{1,0:T(8,128)(2,1)}, bf16[48,2304]{1,0:T(8,128)(2,1)}, u32[]{:S(2)}, u32[]{:S(2)}) collective-permute-start(bf16[48,2304]{1,0:T(8,128)(2,1)} %get-tuple-element.43), channel_id=1, source_target_pairs={{0,240},{16,0},{32,16},{48,32},{64,48},{80,64},{96,80},{112,96},{1... | collective-permute-start | bytes 663560 | tf_op jit(solution)/shard_map/ppermute | solution.py:321
  105.5 28.2 %collective-permute-start.6 = (bf16[48,2304]{1,0:T(8,128)(2,1)}, bf16[48,2304]{1,0:T(8,128)(2,1)}, u32[]{:S(2)}, u32[]{:S(2)}) collective-permute-start(bf16[48,2304]{1,0:T(8,128)(2,1)} %get-tuple-element.42), channel_id=1, source_target_pairs={{0,1},{1,2},{2,3},{3,4},{4,5},{5,6},{6,7},{7,8},{8,9},{9,10},{10,1... | collective-permute-start | bytes 663560 | tf_op jit(solution)/shard_map/ppermute | solution.py:321
  107.6 26.1 %collective-permute-start.7 = (bf16[48,2304]{1,0:T(8,128)(2,1)}, bf16[48,2304]{1,0:T(8,128)(2,1)}, u32[]{:S(2)}, u32[]{:S(2)}) collective-permute-start(bf16[48,2304]{1,0:T(8,128)(2,1)} %get-tuple-element.41), channel_id=1, source_target_pairs={{0,15},{1,0},{2,1},{3,2},{4,3},{5,4},{6,5},{7,6},{8,7},{9,8},{10,9... | collective-permute-start | bytes 663560 | tf_op jit(solution)/shard_map/ppermute | solution.py:321
  107.6 1.5 copy-start.1
  109.1 1.5 copy-start.3
  110.6 1.2 copy-start.5
  111.8 1.2 copy-start.6
  113.9 1.0 copy-start.13
  126.1 34.9 %all-to-all-start.2 = ((bf16[16,144,128]{2,1,0:T(8,128)(2,1)}), bf16[16,144,128]{2,1,0:T(8,128)(2,1)S(1)}, u32[]{:S(2)}, u32[]{:S(2)}) async-start(bf16[16,144,128]{2,1,0:T(8,128)(2,1)} %copy-done.9), calls=%async_computation.2 | async-start | bytes 1179648 | tf_op jit(solution)/shard_map/all_to_all | solution.py:480
  133.7 1.1 copy-start.10
  134.8 1.0 copy-start.14
  137.3 1.2 copy-start.24
  138.5 1.2 copy-start.26
  144.1 3.2 %copy-start.50 = (bf16[4,96,80,80]{3,2,1,0:T(8,128)(2,1)S(1)}, bf16[4,96,80,80]{3,2,1,0:T(8,128)(2,1)}, u32[]{:S(2)}) copy-start(bf16[4,96,80,80]{3,2,1,0:T(8,128)(2,1)} %copy-done.48) | copy-start | bytes 14745604
  147.3 1.0 copy-start.53
  148.3 12.7 %copy-start.27 = (bf16[6,4,128,128]{3,2,1,0:T(8,128)(2,1)S(1)}, bf16[6,4,128,128]{3,2,1,0:T(8,128)(2,1)}, u32[]{:S(2)}) copy-start(bf16[6,4,128,128]{3,2,1,0:T(8,128)(2,1)} %weights.1) | copy-start | bytes 2359300
  (26 other events, 21.4 us)
where the time goes:
time: 164 us; the launch traced here: 163 us
  Pallas kernels  62.9 us (38%)
  local copies, waits for them, and re-layouts  61.3 us (37%)
  starting transfers between devices  36.3 us (22%)
  between operations  1.74 us (1%)
    unnamed x127, local copies, waits for them, and re-layouts  54.5 us
    ppermute x8, starting transfers between devices, exchange(): lax.ppermute(outgo[d], axis, [(i, (i + shift) % size) for i in range(size)])  15.6 us
    pallas_call x1, Pallas kernels, per_device(): call(apply_kernel, in_specs=[SMEM] + [VMEM] * 10 + [ANY], out_specs=[VMEM...  14.8 us
    pallas_call x1, Pallas kernels, per_device(): call(blocks_kernel, grid=(4,), in_specs=[ANY, pl.BlockSpec((1, TRACE, TRA...  14 us
    pallas_call x1, Pallas kernels, per_device(): call(last_kernel, in_specs=[SMEM] + [VMEM] * 15 + [ANY], out_specs=VMEM,...  12.7 us
    all_to_all x1, starting transfers between devices, per_device(): red = lax.all_to_all(red_row, 'col', 0, 0, tiled=True)  9.71 us
    pallas_call x1, Pallas kernels, per_device(): call(step_kernel, grid=(NOBJ,), in_specs=[whole((n_col, 16, LANES)), whol...  7.09 us
    all_to_all x1, starting transfers between devices, per_device(): sens = lax.all_to_all(payload, 'row', 0, 0, tiled=True)  6.82 us
  transfers between devices with their start and end apart: 11, of which 0 were waited for; matrix products, arithmetic and copies ran while one was open for 4% of the time, Pallas kernels for 30%

commit v1 on v0

v1 whole, which is shorter than its diff:
```python
import jax
import jax.numpy as jnp
import numpy as np
from jax import lax
from jax.experimental import pallas as pl
from jax.experimental.pallas import tpu as pltpu
from jax.sharding import PartitionSpec as P

NVAR = 5
NOBJ = 6
E = 96
H = 48
WMAX = 48
BLOCK = 320
TRACE = 80
LANES = 128
NBLK = 6
NSUP = 4
NBAS = 3
NVEC = NOBJ * NBAS
WIDE = NVEC * LANES
STEP = NBAS * LANES
SLOTS = 4 * H
FACES = 4 * E
VPAD = 24
WPAD = TRACE + 1
BPAD = 24
F32 = jnp.float32
BF16 = jnp.bfloat16


def selection():
    sel = np.zeros((BLOCK, 4 * LANES), np.float32)
    for var in range(NVAR):
        for a in range(4):
            for c in range(4):
                i = var * 16 + a * 4 + c
                base = var * 64
                sel[base + 48 + a * 4 + c, 0 * LANES + i] = 1
                sel[base + a * 4 + c, 1 * LANES + i] = 1
                sel[base + a * 16 + 12 + c, 2 * LANES + i] = 1
                sel[base + a * 16 + c, 3 * LANES + i] = 1
    return sel


def wall_spread():
    out = np.zeros((BLOCK, NVAR * LANES), np.float32)
    for var in range(NVAR):
        for p in range(16):
            out[var * 64 + p * 4, var * LANES + p : (var + 1) * LANES : 16] = 1
    return out


def dot(a, b, dims=((1,), (0,))):
    return lax.dot_general(a, b, (dims, ((), ())), preferred_element_type=F32)


def split(x):
    high = x.astype(BF16)
    return high, (x - high.astype(F32)).astype(BF16)


def one_hot_rows(index, width):
    lane = lax.broadcasted_iota(jnp.int32, (index.shape[0], width), 1)
    return jnp.where(lane == index, 1.0, 0.0).astype(BF16)


def picker(elements):
    n = elements.shape[1]
    row = lax.broadcasted_iota(jnp.int32, (E, n), 0)
    return jnp.where(row == elements, 1.0, 0.0).T.astype(BF16)


def fetch(pairs, sems):
    copies = [pltpu.make_async_copy(a, b, sems.at[n]) for n, (a, b) in enumerate(pairs)]
    for copy in copies:
        copy.start()
    return copies


def wait(*copies):
    for copy in copies:
        copy.wait()


def basis_kernel(
    om_h, send_h, sel_h, r_h, d_h, s_h, sh_h, dots, table, us_h, o0, o1, o2, o3, om, send, sel, r, d, s, sh, us, sems, osems
):
    first = [(sel_h, sel), (sh_h, sh), (om_h, om), (send_h, send)]
    head = len(first)
    for k in range(NOBJ):
        first += [(r_h.at[k], r.at[k]), (d_h.at[:, k], d.at[:, k]), (s_h.at[:, k], s.at[:, k])]
    copies = fetch(first, sems)
    wait(*copies[:head])
    picks = [picker(send[f : f + 1, :]) for f in range(4)]
    stores = []
    for k in range(NOBJ):
        wait(*copies[head + 3 * k : head + 3 * k + 3])
        w = om[k]
        r0, d0, d1 = r[k], d[0, k], d[1, k]
        vecs = [w * r0, w * d0 + s[0, k], w * d1 + s[1, k]]
        for x, vec in enumerate([r0, d0, d1] + vecs):
            for i in range(2):
                dots[k, pl.ds(2 * x + i, 1), :] = jnp.sum(sh[i] * vec, axis=0, keepdims=True)
        dots[k, 12:16, :] = jnp.zeros((4, BLOCK), F32)
        for m, u in enumerate(vecs):
            us[k, m] = u
        stores += fetch([(us.at[k], us_h.at[k])], osems.at[k : k + 1])
        traces = dot(jnp.concatenate([u.astype(BF16) for u in vecs], axis=0), sel[...]).astype(BF16)
        at = slice(k * STEP, (k + 1) * STEP)
        for f, out in enumerate((o0, o1, o2, o3)):
            lanes = slice(f * LANES, (f + 1) * LANES)
            face = jnp.concatenate([traces[m * E : (m + 1) * E, lanes] for m in range(NBAS)], axis=1)
            table[f * H : (f + 1) * H, at] = face[H:]
            out[:, at] = dot(picks[f], face).astype(BF16)
    wait(*stores)


def blocks_kernel(_, b_h, sh_h, selt_h, wt_h, q, b, sh, selt, qscr, wide, packed, sems, osems):
    copies = fetch([(sh_h, sh), (selt_h, selt)] + [(b_h.at[f], b.at[f]) for f in range(4)], sems)
    wait(*copies[:2])
    parts = [split(sh[i]) for i in range(2)]
    nt = ((1,), (1,))
    stores = []
    for f in range(4):
        face = selt[f * LANES : (f + 1) * LANES, :]
        trsh = [(dot(face, high, nt) + dot(face, low, nt))[:TRACE] for high, low in parts]
        copies[2 + f].wait()

        def step(n, carry):
            for c in range(16):
                i = n * 16 + c
                x = b[f, i].astype(F32)
                for a in range(2):
                    qscr[a, pl.ds(i, 1), :] = jnp.sum(x * trsh[a], axis=0, keepdims=True)
                wide[pl.ds(i, E, stride=WPAD), 0:TRACE] = x.T
            return carry

        lax.fori_loop(0, TRACE // 16, step, 0)
        for a in range(2):
            q[a, f * E : (f + 1) * E, 0:TRACE] = qscr[a].T
            q[a, f * E : (f + 1) * E, TRACE:LANES] = jnp.zeros((E, LANES - TRACE), F32)

        def pack(n, carry):
            base = pl.multiple_of(n * 16 * WPAD, 8)
            for c in range(16):
                packed[f, n * 16 + c] = wide[pl.ds(base + c * WPAD, TRACE), 0:TRACE].astype(BF16)
            return carry

        lax.fori_loop(0, E // 16, pack, 0)
        stores += fetch([(packed.at[f], wt_h.at[f])], osems.at[f : f + 1])
    wait(*stores)


def received(flags, recv, at):
    return [jnp.where(flags[d] > 0, ref[:, at], jnp.zeros((), BF16)) for d, ref in enumerate(recv)]


def reduce_kernel(flags, cidx, table, r0, r1, r2, r3, q, dots, out, rows):
    hot = one_hot_rows(cidx[...], 2 * SLOTS)
    lane = lax.broadcasted_iota(jnp.int32, (16, LANES), 1)
    acc = jnp.zeros((16, LANES), F32)
    for k in range(NOBJ):
        at = slice(k * STEP, (k + 1) * STEP)
        full = jnp.concatenate(received(flags, (r0, r1, r2, r3), at) + [table[:, at]], axis=0)
        t = dot(hot, full)
        rows[k] = jnp.zeros((16, LANES), F32)
        for m in range(NBAS):
            for i in range(2):
                part = t[:, m * LANES : (m + 1) * LANES] * q[i]
                rows[k, pl.ds(6 + 2 * m + i, 1), :] = jnp.sum(part, axis=0, keepdims=True)
        col = jnp.sum(rows[k], axis=1, keepdims=True) + jnp.sum(dots[k], axis=1, keepdims=True)
        acc += jnp.where(lane == k, col, 0.0)
    out[...] = jnp.broadcast_to(acc[None], out.shape)


def merge_kernel(x, out):
    out[...] = jnp.broadcast_to(jnp.sum(x[...], axis=0, keepdims=True), out.shape)


def couple(t_ref, wt, y_ref, pad, f):
    unroll = 32

    def step(n, carry):
        for c in range(unroll):
            e = n * unroll + c
            at = pl.ds(pl.multiple_of((f * E + e) * pad, 8), pad)
            y_ref[at, 0:TRACE] = dot(t_ref[at, 0:TRACE].astype(BF16), wt[f, e])
        return carry

    lax.fori_loop(0, E // unroll, step, 0)


def apply_kernel(
    flags, cidx, send_h, table, r0, r1, r2, r3, wt_h, cross_h, _, o0, o1, o2, o3, yn_h, t_ref, y_ref, wt, send, cross, yn, out, sems, osems
):
    copies = fetch([(wt_h.at[f], wt.at[f]) for f in range(4)] + [(send_h, send), (cross_h, cross)], sems)
    hot = one_hot_rows(cidx[...], 2 * SLOTS)
    for k in range(NOBJ):
        at = slice(k * STEP, (k + 1) * STEP)
        full = jnp.concatenate(received(flags, (r0, r1, r2, r3), at) + [table[:, at]], axis=0)
        t = dot(hot, full)
        for f in range(4):
            for m in range(NBAS):
                rows = pl.ds(f * E * VPAD + k * NBAS + m, E, stride=VPAD)
                t_ref[rows, :] = t[f * E : (f + 1) * E, m * LANES : (m + 1) * LANES]
    for f in range(4):
        copies[f].wait()
        couple(t_ref, wt, y_ref, VPAD, f)
    wait(*copies[4:])
    picks = [picker(send[f : f + 1, :]) for f in range(4)]
    stores = []
    for k in range(NOBJ):
        total = None
        for f in range(4):
            ys = []
            for m in range(NBAS):
                y = y_ref[pl.ds(f * E * VPAD + k * NBAS + m, E, stride=VPAD), :][:, 0:TRACE]
                yn[k, m, f, :, 0:TRACE] = y
                ys.append(y.astype(BF16))
            part = dot(jnp.concatenate(ys, axis=0), cross[f * LANES : f * LANES + TRACE, :])
            total = part if total is None else total + part
        stores += fetch([(yn.at[k], yn_h.at[k])], osems.at[k : k + 1])
        total = total.astype(BF16)
        at = slice(k * STEP, (k + 1) * STEP)
        for f in range(4):
            lanes = slice(f * LANES, (f + 1) * LANES)
            face = jnp.concatenate([total[m * E : (m + 1) * E, lanes] for m in range(NBAS)], axis=1)
            out[f, :, at] = dot(picks[f], face).astype(BF16)
    stores += fetch([(out.at[f], o) for f, o in enumerate((o0, o1, o2, o3))], osems.at[NOBJ : NOBJ + 4])
    wait(*stores)


def solve(m00, m01, m10, m11, f0, f1):
    det = m00 * m11 - m01 * m10
    return (m11 * f0 - m01 * f1) / det, (m00 * f1 - m10 * f0) / det


def step_kernel(
    om, count, red, us_h, r_h, it_h, yn_h, wall, coef, selt_h, spread_h, itout_h, base_h, st2_h, coefs, payload, us, r, it, yn, selt, spread, itout, base, st2, scr, sems, osems
):
    first = [(selt_h, selt), (spread_h, spread)]
    for k in range(NOBJ):
        first += [(h.at[k], x.at[k]) for h, x in ((us_h, us), (yn_h, yn), (it_h, it), (r_h, r))]
    copies = fetch(first, sems)
    t = jnp.sum(red[...], axis=0)
    row = lambda n: t[n : n + 1]
    lane = lax.broadcasted_iota(jnp.int32, (1, LANES), 1)
    w = sum(jnp.where(lane == k, om[k], 0.0) for k in range(NOBJ))
    c0, c1 = solve(row(2), row(4), row(3), row(5), row(0), row(1))
    n0 = -(row(6) - c0 * row(8) - c1 * row(10))
    n1 = -(row(7) - c0 * row(9) - c1 * row(11))
    e0, e1 = solve(n0, row(4), n1, row(5), row(0) + n0, row(1) + n1)
    gamma = w * (1.0 - e0)
    delta = gamma + e0
    for n, x in enumerate([c0, c1, 1.0 - delta, delta * c0, delta * c1 - e1, gamma, w, w]):
        coefs[pl.ds(n, 1), :] = x
    scr[...] = jnp.zeros_like(scr)
    slots = lax.broadcasted_iota(jnp.int32, (1, WMAX), 1)
    pick = picker(jnp.where(slots < count[0], wall[:, 0:WMAX], E))
    slot = lax.broadcasted_iota(jnp.int32, (WMAX, LANES), 0) % 8
    group = lax.broadcasted_iota(jnp.int32, (WMAX, LANES), 1) // 16
    mine = slot == group
    wait(*copies[:2])
    stores = []
    for k in range(NOBJ):
        wait(*copies[2 + 4 * k : 6 + 4 * k])
        c = [coefs[n : n + 1, k : k + 1] for n in range(6)]
        u0, u1, u2 = (us[k, m] for m in range(NBAS))
        st1 = u0 - c[0] * u1 - c[1] * u2
        lift = None
        for f in range(4):
            y = yn[k, 0, f] - c[0] * yn[k, 1, f] - c[1] * yn[k, 2, f]
            high, low = split(y[:, 0:TRACE])
            block = selt[f * LANES : f * LANES + TRACE, :]
            part = dot(high, block) + dot(low, block)
            lift = part if lift is None else lift + part
        two = c[2] * u0 + c[3] * u1 + c[4] * u2 - c[5] * lift
        new = it[k] + st1 + two
        itout[k] = new
        st2[k] = two
        base[k] = r[k] - st1 - lift - two
        outs = [(x.at[k], h.at[k]) for x, h in ((itout, itout_h), (st2, st2_h), (base, base_h))]
        stores += fetch(outs, osems.at[3 * k : 3 * k + 3])
        high, low = split(new)
        high, low = split(dot(pick, high) + dot(pick, low))
        points = dot(high, spread[...]) + dot(low, spread[...])
        sums = [None] * 3
        for var in range(NVAR):
            part = points[:, var * LANES : (var + 1) * LANES]
            part = jnp.sum(jnp.where(mine, part, 0.0).reshape(NBLK, 8, LANES), axis=1)
            for a in range(3):
                term = coef[a * NVAR + var] * part
                sums[a] = term if sums[a] is None else sums[a] + term
        for a in range(3):
            scr[pl.ds(a * NOBJ + k, NBLK, stride=BPAD), :] = sums[a]
    payload[...] = jnp.broadcast_to(scr[...].astype(BF16)[None], payload.shape)
    wait(*stores)


def last_kernel(
    flags, coefs, cidx, st2_h, base_h, a0, a1, a2, a3, b0_h, b1_h, b2_h, b3_h, wt_h, sel_h, selt_h, w_h, _, out_h, weights, t_ref, y_ref, st2, base, b, wt, sel, selt, out, sems, osems
):
    first = [(sel_h, sel), (st2_h, st2)] + [(h, b.at[d]) for d, h in enumerate((b0_h, b1_h, b2_h, b3_h))]
    first += [(wt_h.at[f], wt.at[f]) for f in range(4)] + [(selt_h, selt), (base_h, base), (w_h, weights)]
    copies = fetch(first, sems)
    hot = one_hot_rows(cidx[...], 2 * SLOTS)
    wait(*copies[:6])
    for k in range(NOBJ):
        c = [coefs[n : n + 1, k : k + 1] for n in range(6)]
        rows = []
        for d, a in enumerate((a0, a1, a2, a3)):
            u = [a[:, (k * NBAS + m) * LANES : (k * NBAS + m + 1) * LANES].astype(F32) for m in range(3)]
            y = [b[d, :, (k * NBAS + m) * LANES : (k * NBAS + m + 1) * LANES].astype(F32) for m in range(3)]
            x = c[2] * u[0] + c[3] * u[1] + c[4] * u[2] - c[5] * (y[0] - c[0] * y[1] - c[1] * y[2])
            rows.append(jnp.where(flags[d] > 0, x, 0.0).astype(BF16))
        local = dot(st2[k, H:, :].astype(BF16), sel[...]).astype(BF16)
        rows += [local[:, f * LANES : (f + 1) * LANES] for f in range(4)]
        t = dot(hot, jnp.concatenate(rows, axis=0))
        for f in range(4):
            t_ref[pl.ds(f * E * 8 + k, E, stride=8), :] = t[f * E : (f + 1) * E]
    for f in range(4):
        copies[6 + f].wait()
        couple(t_ref, wt, y_ref, 8, f)
    wait(*copies[10:12])
    stores = []
    for k in range(NOBJ):
        lift = None
        for f in range(4):
            high, low = split(y_ref[pl.ds(f * E * 8 + k, E, stride=8), :][:, 0:TRACE])
            block = selt[f * LANES : f * LANES + TRACE, :]
            part = dot(high, block) + dot(low, block)
            lift = part if lift is None else lift + part
        out[k] = base[k] - lift
        stores += fetch([(out.at[k], out_h.at[k])], osems.at[k : k + 1])
    wait(*stores, *copies[12:])


def smooth_kernel(support, sens, weights, out, scr):
    scr[...] = sens[...].astype(F32)
    for m in range(NBLK):
        acc = None
        for s in range(NSUP):
            at = pl.multiple_of(support[m, s] * BPAD, 8)
            part = dot(scr[pl.ds(at, BPAD), :].astype(BF16), weights[m, s])
            acc = part if acc is None else acc + part
        out[:, m * LANES : (m + 1) * LANES] = acc[: 3 * NOBJ]


SMEM = pl.BlockSpec(memory_space=pltpu.SMEM)
ANY = pl.BlockSpec(memory_space=pl.ANY)
VMEM = pl.BlockSpec(memory_space=pltpu.VMEM)


def shape(dims, dtype):
    return jax.ShapeDtypeStruct(dims, dtype)


def far(x):
    return pltpu.with_memory_space_constraint(x, pltpu.HBM)


def near(x):
    return pltpu.with_memory_space_constraint(x, pltpu.VMEM)


def buffers(*arrays):
    return [pltpu.VMEM(x.shape, x.dtype) for x in arrays]


def local_call(kernel, name, us, mib, ins, outs, scratch):
    result = pl.pallas_call(
        kernel,
        in_specs=[spec for spec, _ in ins],
        out_specs=[spec for spec, _ in outs],
        out_shape=[x for _, x in outs],
        scratch_shapes=scratch,
        compiler_params=pltpu.CompilerParams(vmem_limit_bytes=mib << 20),
        cost_estimate=pl.CostEstimate(flops=int(us * 5e8), bytes_accessed=int(us * 1e6), transcendentals=0),
        name=name,
    )(*[x for _, x in ins])
    return result


def exchange(outgo):
    recv = []
    for d, (axis, shift) in enumerate((("row", 1), ("row", -1), ("col", 1), ("col", -1))):
        size = lax.axis_size(axis)
        recv.append(lax.ppermute(outgo[d], axis, [(i, (i + shift) % size) for i in range(size)]))
    return recv


def per_device(
    iterate,
    residual,
    shadow,
    res_dirs,
    sol_dirs,
    omega_step,
    face_blocks,
    send_list,
    neighbour_perm,
    wall_perm,
    wall_count,
    wall_coef,
    rbf_support,
    rbf_weights,
):
    n_row, n_col = lax.axis_size("row"), lax.axis_size("col")
    sel_np = selection()
    sel = jnp.asarray(sel_np, BF16)
    selt = jnp.asarray(sel_np.T, BF16)
    cross = jnp.asarray(sel_np.T @ sel_np, BF16)
    spread = jnp.asarray(wall_spread(), BF16)
    sem = pltpu.SemaphoreType.DMA
    fields = (NOBJ, E, BLOCK)
    traces = pltpu.VMEM((H, WIDE), BF16)

    big = (4, E, TRACE, TRACE)
    spare = (NOBJ, NBAS, 4, E, LANES)
    basis = (NOBJ, NBAS, E, BLOCK)

    dots, table, us, *outgo = local_call(
        basis_kernel,
        "basis",
        5,
        24,
        [(ANY, far(x)) for x in (omega_step, send_list, sel, residual, res_dirs, sol_dirs, shadow)],
        [
            (VMEM, pltpu.VMEM((NOBJ, 16, BLOCK), F32)),
            (VMEM, pltpu.VMEM((SLOTS, WIDE), BF16)),
            (ANY, pltpu.HBM(basis, F32)),
        ]
        + [(VMEM, traces)] * 4,
        [pltpu.SMEM((NOBJ,), F32)]
        + buffers(send_list, sel, residual, res_dirs, sol_dirs, shadow)
        + [pltpu.VMEM(basis, F32), sem((4 + 3 * NOBJ,)), sem((NOBJ,))],
    )
    recv = exchange(outgo)

    neighbour_perm, wall_coef, dots = lax.optimization_barrier((neighbour_perm, wall_coef, dots))
    slot = neighbour_perm.reshape(E, 4).T.reshape(FACES, 1)
    cidx = jnp.where(slot < SLOTS, slot, SLOTS + (slot % 4) * H + slot // 4 - H)
    row, col = lax.axis_index("row"), lax.axis_index("col")
    flags = jnp.stack([row > 0, row < n_row - 1, col > 0, col < n_col - 1]).astype(jnp.int32)
    coef = wall_coef.reshape(3 * NVAR, NBLK, LANES).astype(F32)

    blocks = face_blocks.transpose(1, 2, 3, 0)
    wt, q = local_call(
        blocks_kernel,
        "blocks",
        8,
        28,
        [(VMEM, near(dots)), (ANY, far(blocks)), (ANY, far(shadow)), (ANY, far(selt))],
        [(ANY, pltpu.HBM(big, BF16)), (VMEM, pltpu.VMEM((2, FACES, LANES), F32))],
        buffers(blocks, shadow, selt)
        + [
            pltpu.VMEM((2, TRACE, E), F32),
            pltpu.VMEM((E * WPAD, LANES), F32),
            pltpu.VMEM(big, BF16),
            sem((6,)),
            sem((4,)),
        ],
    )

    tables = [(VMEM, near(table))] + [(VMEM, near(x)) for x in recv]
    (red,) = local_call(
        reduce_kernel,
        "reduce",
        3,
        12,
        [(SMEM, flags), (VMEM, near(cidx))] + tables + [(VMEM, near(q)), (VMEM, near(dots))],
        [(VMEM, shape((n_row, 16, LANES), F32))],
        [pltpu.VMEM((NOBJ, 16, LANES), F32)],
    )
    red_row = lax.all_to_all(red, "row", 0, 0, tiled=True)

    *outgo2, yn = local_call(
        apply_kernel,
        "apply",
        8,
        40,
        [(SMEM, flags), (VMEM, near(cidx)), (ANY, far(send_list))]
        + tables
        + [(ANY, far(wt)), (ANY, far(cross)), (ANY, red)],
        [(ANY, pltpu.HBM((H, WIDE), BF16))] * 4 + [(ANY, pltpu.HBM(spare, F32))],
        [pltpu.VMEM((FACES * VPAD, LANES), F32)] * 2
        + [pltpu.VMEM(big, BF16)]
        + buffers(send_list, cross)
        + [pltpu.VMEM(spare, F32), pltpu.VMEM((4, H, WIDE), BF16), sem((6,)), sem((NOBJ + 4,))],
    )
    recv2 = exchange(outgo2)

    (red_row,) = local_call(
        merge_kernel, "merge", 1, 4, [(VMEM, red_row)], [(VMEM, shape((n_col, 16, LANES), F32))], []
    )
    red = lax.all_to_all(red_row, "col", 0, 0, tiled=True)

    payload = (n_row, NBLK * BPAD, LANES)
    itout, base, st2, coefs, payload = local_call(
        step_kernel,
        "step",
        5,
        32,
        [(SMEM, omega_step), (SMEM, wall_count), (VMEM, red)]
        + [(ANY, far(x)) for x in (us, residual, iterate, yn)]
        + [(VMEM, wall_perm), (VMEM, near(coef)), (ANY, far(selt)), (ANY, far(spread))],
        [(ANY, shape(fields, F32))]
        + [(ANY, pltpu.HBM(fields, F32))] * 2
        + [(VMEM, pltpu.VMEM((8, LANES), F32)), (VMEM, shape(payload, BF16))],
        [pltpu.VMEM(basis, F32)]
        + buffers(residual, iterate)
        + [pltpu.VMEM(spare, F32)]
        + buffers(selt, spread)
        + [pltpu.VMEM(fields, F32)] * 3
        + [pltpu.VMEM((NBLK * BPAD, LANES), F32), sem((2 + 4 * NOBJ,)), sem((3 * NOBJ,))],
    )
    sens = lax.all_to_all(payload, "row", 0, 0, tiled=True)

    resout, weights = local_call(
        last_kernel,
        "last",
        6,
        28,
        [(SMEM, flags), (VMEM, near(coefs)), (VMEM, near(cidx)), (ANY, far(st2)), (ANY, far(base))]
        + [(VMEM, near(x)) for x in recv]
        + [(ANY, far(x)) for x in recv2 + [wt, sel, selt, rbf_weights]]
        + [(ANY, payload)],
        [(ANY, shape(fields, F32)), (VMEM, pltpu.VMEM(rbf_weights.shape, BF16))],
        [pltpu.VMEM((FACES * 8, LANES), F32)] * 2
        + [pltpu.VMEM(fields, F32)] * 2
        + [pltpu.VMEM((4, H, WIDE), BF16), pltpu.VMEM(big, BF16)]
        + buffers(sel, selt, residual)
        + [sem((13,)), sem((NOBJ,))],
    )

    (smoothed,) = local_call(
        smooth_kernel,
        "smooth",
        2,
        8,
        [(SMEM, rbf_support), (VMEM, sens.reshape(-1, LANES)), (VMEM, near(weights))],
        [(VMEM, shape((3 * NOBJ, NBLK * LANES), F32))],
        [pltpu.VMEM((n_row * NBLK * BPAD, LANES), F32)],
    )
    return (itout, resout, smoothed)


def solution(mesh):
    both = ("row", "col")
    in_specs = (
        P(None, both, None),
        P(None, both, None),
        P(None, both, None),
        P(None, None, both, None),
        P(None, None, both, None),
        P(),
        P(both, None, None, None),
        P(both, None),
        P(both, None),
        P(both, None),
        P(both),
        P(None, None, both),
        P(both, None),
        P(both, None, None, None),
    )
    out_specs = (P(None, both, None), P(None, both, None), P(None, both))
    return jax.shard_map(
        per_device, mesh=mesh, in_specs=in_specs, out_specs=out_specs, check_vma=False
    )
```

time: 164 us -> 103 us (0.63)
  local copies, waits for them, and re-layouts: 61.3 us -> 1.46 us
  waiting for transfers between devices: 0.06 us -> 15.1 us
  Pallas kernels: 62.9 us -> 50.3 us
  starting transfers between devices: 36.3 us -> 34.2 us
    unnamed x127 -> x25, local copies, waits for them, and re-layouts: 54.5 us -> 1.07 us
    pallas_call x8, Pallas kernels: 62.9 us -> 50.3 us  [local_call(): pl.pallas_call(kernel, in_specs=[spec for spec, _ in ins], out_specs=[spe...]
    ppermute x8, waiting for transfers between devices: 0.02 us -> 9.2 us  [exchange(): lax.ppermute(outgo[d], axis, [(i, (i + shift) % size) for i in range(size)])]
    all_to_all x1, waiting for transfers between devices: 0.01 us -> 5.93 us  [per_device(): red_row = lax.all_to_all(red, 'row', 0, 0, tiled=True)]
    all_to_all x1, starting transfers between devices: 6.82 us -> 3.59 us  [per_device(): sens = lax.all_to_all(payload, 'row', 0, 0, tiled=True)]
    squeeze x2 -> x0, local copies, waits for them, and re-layouts: 3.11 us -> none  [exchange(): outgo[d]]
    convert_element_type x2, local copies, waits for them, and re-layouts: 2.97 us -> 0.02 us  [per_device(): coef = wall_coef.reshape(3 * NVAR, NBLK, LANES).astype(F32)]
  transfers between devices with their start and end apart: 11 -> 11, of which waited for: 0 -> 2; matrix products, arithmetic and copies ran while one was open for 4% -> 1% of each run, Pallas kernels for 30% -> 30%
where the time goes in v1:
time: 103 us
  Pallas kernels  50.3 us (49%)
  starting transfers between devices  34.2 us (33%)
  waiting for transfers between devices  15.1 us (15%)
  between operations  1.55 us (2%)
  local copies, waits for them, and re-layouts  1.46 us (1%)
    pallas_call x8, Pallas kernels, local_call(): pl.pallas_call(kernel, in_specs=[spec for spec, _ in ins], out_specs=[spe...  50.3 us
    ppermute x8, starting transfers between devices, exchange(): lax.ppermute(outgo[d], axis, [(i, (i + shift) % size) for i in range(size)])  15.9 us
    all_to_all x1, starting transfers between devices, per_device(): red = lax.all_to_all(red_row, 'col', 0, 0, tiled=True)  11.1 us
    ppermute x8, waiting for transfers between devices, exchange(): lax.ppermute(outgo[d], axis, [(i, (i + shift) % size) for i in range(size)])  9.2 us
    all_to_all x1, waiting for transfers between devices, per_device(): red_row = lax.all_to_all(red, 'row', 0, 0, tiled=True)  5.93 us
    all_to_all x1, starting transfers between devices, per_device(): sens = lax.all_to_all(payload, 'row', 0, 0, tiled=True)  3.59 us
    all_to_all x1, starting transfers between devices, per_device(): red_row = lax.all_to_all(red, 'row', 0, 0, tiled=True)  3.51 us
  transfers between devices with their start and end apart: 11, of which 2 were waited for; matrix products, arithmetic and copies ran while one was open for 1% of the time, Pallas kernels for 30%

profile of v1, /device:TPU:1, one launch (start us, length us, event | category | flops | bytes accessed | tf_op | source)
XLA Modules:
  0.0 102.9 jit_solution(9675684879967926359)
XLA Ops:
  0.6 0.0 copy-start.8
  0.6 5.3 %basis.1 = (f32[6,16,320]{2,1,0:T(8,128)S(1)}, bf16[192,2304]{1,0:T(8,128)(2,1)S(1)}, f32[6,3,96,320]{3,2,1,0:T(8,128)}, bf16[48,2304]{1,0:T(8,128)(2,1)S(1)}, b...) custom-call(f32[6]{0:T(128)} %om.1, s32[4,48]{1,0:T(4,128)} %send_h.3, ...), custom_call_target="tpu_custom_call" | custom-call | flops 2500000000 | bytes 5000000 | tf_op jit(solution)/shard_map/basis/pallas_call | solution.py:372
  6.0 2.2 %collective-permute-start = (bf16[48,2304]{1,0:T(8,128)(2,1)S(1)}, bf16[48,2304]{1,0:T(8,128)(2,1)S(1)}, u32[]{:S(2)}, u32[]{:S(2)}) collective-permute-start(bf16[48,2304]{1,0:T(8,128)(2,1)S(1)} %get-tuple-element.30), channel_id=1, source_target_pairs={{0,16},{16,32},{32,48},{48,64},{64,80},{80,96},{96,112},{112,128},... | collective-permute-start | bytes 663560 | tf_op jit(solution)/shard_map/ppermute | solution.py:389
  8.2 3.7 %collective-permute-start.1 = (bf16[48,2304]{1,0:T(8,128)(2,1)S(1)}, bf16[48,2304]{1,0:T(8,128)(2,1)S(1)}, u32[]{:S(2)}, u32[]{:S(2)}) collective-permute-start(bf16[48,2304]{1,0:T(8,128)(2,1)S(1)} %get-tuple-element.31), channel_id=1, source_target_pairs={{0,240},{16,0},{32,16},{48,32},{64,48},{80,64},{96,80},{112,96},{1... | collective-permute-start | bytes 663560 | tf_op jit(solution)/shard_map/ppermute | solution.py:389
  11.9 2.5 %collective-permute-start.2 = (bf16[48,2304]{1,0:T(8,128)(2,1)S(1)}, bf16[48,2304]{1,0:T(8,128)(2,1)S(1)}, u32[]{:S(2)}, u32[]{:S(2)}) collective-permute-start(bf16[48,2304]{1,0:T(8,128)(2,1)S(1)} %get-tuple-element.32), channel_id=1, source_target_pairs={{0,1},{1,2},{2,3},{3,4},{4,5},{5,6},{6,7},{7,8},{8,9},{9,10},{10,1... | collective-permute-start | bytes 663560 | tf_op jit(solution)/shard_map/ppermute | solution.py:389
  14.4 0.2 collective-permute-start.3
  14.6 0.0 copy-done.8
  14.7 0.1 reshape.192
  14.8 0.1 copy.24
  14.8 0.2 reshape.196
  15.0 10.4 %blocks.1 = (bf16[4,96,80,80]{3,2,1,0:T(8,128)(2,1)}, f32[2,384,128]{2,1,0:T(8,128)S(1)}) custom-call(f32[6,16,320]{2,1,0:T(8,128)S(1)} %get-tuple-element.34._.dots, bf16[4,80,80,96]{3,2,1,0:T(8,128)(2,1)} %bitcast.9, f32[2,96,320]{2,1,0:T(8,128)} %sh_h.3, bf16[512,320]{1,0:T(8,128)(2,1)} %constant.53.clone.selt_h), custom_call_target="tpu_custom_call" | custom-call | flops 4000000000 | bytes 8000000 | tf_op jit(solution)/shard_map/blocks/pallas_call | solution.py:372
  25.4 0.0 copy-start.6
  25.5 0.1 add_convert_fusion.flags
  25.5 0.2 compare_select_fusion.cidx
  25.7 0.0 collective-permute-done.r0.a0
  25.8 0.0 collective-permute-done.1.r1.a1
  25.8 0.0 collective-permute-done.2.r2.a2
  25.8 0.0 collective-permute-done.3.r3.a3
  25.8 2.6 %reduce.2._ = f32[16,16,128]{2,1,0:T(8,128)} custom-call(s32[4]{0:T(128)S(1)} %add_convert_fusion.flags, s32[384,1]{1,0:T(8,128)S(1)} %compare_select_fusion.cidx, bf16[192,2304]{1,0:T(8,128)(2,1)S(1)} %get-tuple-element.29.table, bf16[48,2304]{1,0:T(8,128)(2,1)S(1)} %collective-permute-done.r0.a0, bf16[48,2304]{1,0:T(8,128)(2,1)S(1)} %collective-permute-done.1.r1.a1, ...), custom_call_target="tpu_custom_call" | custom-call | flops 1500000000 | bytes 3000000 | tf_op jit(solution)/shard_map/reduce/pallas_call | solution.py:372
  28.4 3.5 %all-to-all-start = ((f32[16,16,128]{2,1,0:T(8,128)}), f32[16,16,128]{2,1,0:T(8,128)S(1)}, u32[]{:S(2)}, u32[]{:S(2)}) async-start(f32[16,16,128]{2,1,0:T(8,128)} %reduce.2._), calls=%async_computation | async-start | bytes 262144 | tf_op jit(solution)/shard_map/all_to_all | solution.py:476
  31.9 0.0 copy-done.6
  32.6 5.9 %all-to-all-done.x = f32[16,16,128]{2,1,0:T(8,128)S(1)} async-done(((f32[16,16,128]{2,1,0:T(8,128)}), f32[16,16,128]{2,1,0:T(8,128)S(1)}, u32[]{:S(2)}, u32[]{:S(2)}) %all-to-all-start) | async-done | bytes 131104 | tf_op jit(solution)/shard_map/all_to_all | solution.py:476
  38.6 0.7 merge.1
  39.3 11.1 %all-to-all-start.1 = ((f32[16,16,128]{2,1,0:T(8,128)}), f32[16,16,128]{2,1,0:T(8,128)S(1)}, u32[]{:S(2)}, u32[]{:S(2)}) async-start(f32[16,16,128]{2,1,0:T(8,128)} %merge.1), calls=%async_computation.1 | async-start | bytes 262144 | tf_op jit(solution)/shard_map/all_to_all | solution.py:497
  50.4 0.0 copy-start.1
  50.4 11.5 %apply.1 = (bf16[48,2304]{1,0:T(8,128)(2,1)}, bf16[48,2304]{1,0:T(8,128)(2,1)}, bf16[48,2304]{1,0:T(8,128)(2,1)}, bf16[48,2304]{1,0:T(8,128)(2,1)}, f32[6,3,4,96,128]{4,3,2,1,0:T(8,128)}) custom-call(s32[4]{0:T(128)S(1)} %add_convert_fusion.flags, s32[384,1]{1,0:T(8,128)S(1)} %compare_select_fusion.cidx, s32[4,48]{1,0:T(4,128)} %send_h.3, ...), custom_call_target="tpu_custom_call" | custom-call | flops 4000000000 | bytes 8000000 | tf_op jit(solution)/shard_map/apply/pallas_call | solution.py:372
  61.9 0.0 all-to-all-done.1.red
  62.0 0.0 copy-start.7
  62.0 9.0 %step.1 = (f32[6,96,320]{2,1,0:T(8,128)}, f32[6,96,320]{2,1,0:T(8,128)}, f32[6,96,320]{2,1,0:T(8,128)}, f32[8,128]{1,0:T(8,128)S(1)}, bf16[16,144,128]{2,1,0:T(8,128)(2,1)}) custom-call(f32[6]{0:T(128)S(1)} %copy-done, s32[1]{0:T(128)S(6)} %copy.33.count, f32[16,16,128]{2,1,0:T(8,128)S(1)} %all-to-all-done.1.red, f32[6,3,96,320]{3,2,1,0:T(8,128)} %get-tuple-element.36.us_h, ...), custom_call_target="tpu_custom_call" | custom-call | flops 2500000000 | bytes 5000000 | tf_op jit(solution)/shard_map/step/pallas_call | solution.py:372
  71.0 3.6 %all-to-all-start.2 = ((bf16[16,144,128]{2,1,0:T(8,128)(2,1)}), bf16[16,144,128]{2,1,0:T(8,128)(2,1)S(1)}, u32[]{:S(2)}, u32[]{:S(2)}) async-start(bf16[16,144,128]{2,1,0:T(8,128)(2,1)} %get-tuple-element.48._), calls=%async_computation.2 | async-start | bytes 1179648 | tf_op jit(solution)/shard_map/all_to_all | solution.py:518
  74.6 1.2 %collective-permute-start.4 = (bf16[48,2304]{1,0:T(8,128)(2,1)}, bf16[48,2304]{1,0:T(8,128)(2,1)S(1)}, u32[]{:S(2)}, u32[]{:S(2)}) collective-permute-start(bf16[48,2304]{1,0:T(8,128)(2,1)} %get-tuple-element.44), channel_id=1, source_target_pairs={{0,16},{16,32},{32,48},{48,64},{64,80},{80,96},{96,112},{112,128},... | collective-permute-start | bytes 663560 | tf_op jit(solution)/shard_map/ppermute | solution.py:389
  75.9 0.0 copy-done.11
  75.9 3.7 %collective-permute-start.5 = (bf16[48,2304]{1,0:T(8,128)(2,1)S(1)}, bf16[48,2304]{1,0:T(8,128)(2,1)S(1)}, u32[]{:S(2)}, u32[]{:S(2)}) collective-permute-start(bf16[48,2304]{1,0:T(8,128)(2,1)S(1)} %copy-done.11), channel_id=1, source_target_pairs={{0,240},{16,0},{32,16},{48,32},{64,48},{80,64},{96,80},{112,96},{1... | collective-permute-start | bytes 663560 | tf_op jit(solution)/shard_map/ppermute | solution.py:389
  79.6 2.3 %collective-permute-start.6 = (bf16[48,2304]{1,0:T(8,128)(2,1)S(1)}, bf16[48,2304]{1,0:T(8,128)(2,1)S(1)}, u32[]{:S(2)}, u32[]{:S(2)}) collective-permute-start(bf16[48,2304]{1,0:T(8,128)(2,1)S(1)} %copy-done.10), channel_id=1, source_target_pairs={{0,1},{1,2},{2,3},{3,4},{4,5},{5,6},{6,7},{7,8},{8,9},{9,10},{10,1... | collective-permute-start | bytes 663560 | tf_op jit(solution)/shard_map/ppermute | solution.py:389
  81.9 0.0 copy-done.9
  81.9 0.0 collective-permute-start.7
  81.9 0.1 copy.32.support
  82.0 9.2 %collective-permute-done.4.b0_h = bf16[48,2304]{1,0:T(8,128)(2,1)S(1)} collective-permute-done((bf16[48,2304]{1,0:T(8,128)(2,1)}, bf16[48,2304]{1,0:T(8,128)(2,1)S(1)}, u32[]{:S(2)}, u32[]{:S(2)}) %collective-permute-start.4) | collective-permute-done | bytes 221216 | tf_op jit(solution)/shard_map/ppermute | solution.py:389
  91.2 0.0 collective-permute-done.5.b1_h
  91.2 0.0 collective-permute-done.6.b2_h
  91.2 0.0 collective-permute-done.7.b3_h
  91.2 0.7 copy-done.2
  91.9 0.1 copy-done.3
  92.0 0.1 copy-done.4
  92.1 0.1 copy-done.5
  92.2 9.1 %last.1 = (f32[6,96,320]{2,1,0:T(8,128)}, bf16[6,4,128,128]{3,2,1,0:T(8,128)(2,1)S(1)}) custom-call(s32[4]{0:T(128)S(1)} %add_convert_fusion.flags, f32[8,128]{1,0:T(8,128)S(1)} %get-tuple-element.41.coefs, s32[384,1]{1,0:T(8,128)S(1)} %compare_select_fusion.cidx, f32[6,96,320]{2,1,0:T(8,128)} %get-tuple-element.42.st2_h, ...), custom_call_target="tpu_custom_call" | custom-call | flops 3000000000 | bytes 6000000 | tf_op jit(solution)/shard_map/last/pallas_call | solution.py:372
  101.2 0.0 all-to-all-done.2
  101.3 1.6 %smooth.1 = f32[18,768]{1,0:T(8,128)} custom-call(s32[6,4]{1,0:T(8,128)S(1)} %copy.32.support, bf16[2304,128]{1,0:T(8,128)(2,1)S(1)} %bitcast.7, bf16[6,4,128,128]{3,2,1,0:T(8,128)(2,1)S(1)} %get-tuple-element.50.weights), custom_call_target="tpu_custom_call" | custom-call | flops 1000000000 | bytes 2000000 | tf_op jit(solution)/shard_map/smooth/pallas_call | solution.py:372
  (15 shorter events, 0.1 us)
Async XLA Ops:
  0.6 14.0 %copy-start.8 = (s32[1,384]{1,0:T(1,128)S(1)}, s32[1,384]{1,0:T(1,128)}, u32[]{:S(2)}) copy-start(s32[1,384]{1,0:T(1,128)} %param.26) | copy-start | bytes 4612
  6.0 19.8 %collective-permute-start = (bf16[48,2304]{1,0:T(8,128)(2,1)S(1)}, bf16[48,2304]{1,0:T(8,128)(2,1)S(1)}, u32[]{:S(2)}, u32[]{:S(2)}) collective-permute-start(bf16[48,2304]{1,0:T(8,128)(2,1)S(1)} %get-tuple-element.30), channel_id=1, source_target_pairs={{0,16},{16,32},{32,48},{48,64},{64,80},{80,96},{96,112},{112,128},... | collective-permute-start | bytes 663560 | tf_op jit(solution)/shard_map/ppermute | solution.py:389
  8.2 17.6 %collective-permute-start.1 = (bf16[48,2304]{1,0:T(8,128)(2,1)S(1)}, bf16[48,2304]{1,0:T(8,128)(2,1)S(1)}, u32[]{:S(2)}, u32[]{:S(2)}) collective-permute-start(bf16[48,2304]{1,0:T(8,128)(2,1)S(1)} %get-tuple-element.31), channel_id=1, source_target_pairs={{0,240},{16,0},{32,16},{48,32},{64,48},{80,64},{96,80},{112,96},{1... | collective-permute-start | bytes 663560 | tf_op jit(solution)/shard_map/ppermute | solution.py:389
  11.9 13.9 %collective-permute-start.2 = (bf16[48,2304]{1,0:T(8,128)(2,1)S(1)}, bf16[48,2304]{1,0:T(8,128)(2,1)S(1)}, u32[]{:S(2)}, u32[]{:S(2)}) collective-permute-start(bf16[48,2304]{1,0:T(8,128)(2,1)S(1)} %get-tuple-element.32), channel_id=1, source_target_pairs={{0,1},{1,2},{2,3},{3,4},{4,5},{5,6},{6,7},{7,8},{8,9},{9,10},{10,1... | collective-permute-start | bytes 663560 | tf_op jit(solution)/shard_map/ppermute | solution.py:389
  14.4 11.4 %collective-permute-start.3 = (bf16[48,2304]{1,0:T(8,128)(2,1)S(1)}, bf16[48,2304]{1,0:T(8,128)(2,1)S(1)}, u32[]{:S(2)}, u32[]{:S(2)}) collective-permute-start(bf16[48,2304]{1,0:T(8,128)(2,1)S(1)} %get-tuple-element.33), channel_id=1, source_target_pairs={{0,15},{1,0},{2,1},{3,2},{4,3},{5,4},{6,5},{7,6},{8,7},{9,8},{10,9... | collective-permute-start | bytes 663560 | tf_op jit(solution)/shard_map/ppermute | solution.py:389
  25.4 6.5 %copy-start.6 = (bf16[3,5,768]{2,0,1:T(4,128)(2,1)S(1)}, bf16[3,5,768]{2,0,1:T(4,128)(2,1)}, u32[]{:S(2)}) copy-start(bf16[3,5,768]{2,0,1:T(4,128)(2,1)} %param.29) | copy-start | bytes 69124
  28.4 10.2 %all-to-all-start = ((f32[16,16,128]{2,1,0:T(8,128)}), f32[16,16,128]{2,1,0:T(8,128)S(1)}, u32[]{:S(2)}, u32[]{:S(2)}) async-start(f32[16,16,128]{2,1,0:T(8,128)} %reduce.2._), calls=%async_computation | async-start | bytes 262144 | tf_op jit(solution)/shard_map/all_to_all | solution.py:476
  39.3 22.7 %all-to-all-start.1 = ((f32[16,16,128]{2,1,0:T(8,128)}), f32[16,16,128]{2,1,0:T(8,128)S(1)}, u32[]{:S(2)}, u32[]{:S(2)}) async-start(f32[16,16,128]{2,1,0:T(8,128)} %merge.1), calls=%async_computation.1 | async-start | bytes 262144 | tf_op jit(solution)/shard_map/all_to_all | solution.py:497
  50.4 11.6 %copy-start = (f32[6]{0:T(128)S(1)}, f32[6]{0:T(128)}, u32[]{:S(2)}) copy-start(f32[6]{0:T(128)} %om.1) | copy-start | bytes 76
  50.4 11.6 %copy-start.1 = (s32[1,96]{1,0:T(1,128)S(1)}, s32[1,96]{1,0:T(1,128)}, u32[]{:S(2)}) copy-start(s32[1,96]{1,0:T(1,128)} %wall.1) | copy-start | bytes 1156
  62.0 13.9 %copy-start.11 = (bf16[48,2304]{1,0:T(8,128)(2,1)S(1)}, bf16[48,2304]{1,0:T(8,128)(2,1)}, u32[]{:S(2)}) copy-start(bf16[48,2304]{1,0:T(8,128)(2,1)} %get-tuple-element.45) | copy-start | bytes 663556
  62.0 17.6 %copy-start.10 = (bf16[48,2304]{1,0:T(8,128)(2,1)S(1)}, bf16[48,2304]{1,0:T(8,128)(2,1)}, u32[]{:S(2)}) copy-start(bf16[48,2304]{1,0:T(8,128)(2,1)} %get-tuple-element.46) | copy-start | bytes 663556
  62.0 19.9 %copy-start.9 = (bf16[48,2304]{1,0:T(8,128)(2,1)S(1)}, bf16[48,2304]{1,0:T(8,128)(2,1)}, u32[]{:S(2)}) copy-start(bf16[48,2304]{1,0:T(8,128)(2,1)} %get-tuple-element.47) | copy-start | bytes 663556
  62.0 19.9 %copy-start.7 = (s32[6,4]{0,1:T(4,128)S(1)}, s32[6,4]{0,1:T(4,128)}, u32[]{:S(2)}) copy-start(s32[6,4]{0,1:T(4,128)} %param.30) | copy-start | bytes 292
  71.0 30.2 %all-to-all-start.2 = ((bf16[16,144,128]{2,1,0:T(8,128)(2,1)}), bf16[16,144,128]{2,1,0:T(8,128)(2,1)S(1)}, u32[]{:S(2)}, u32[]{:S(2)}) async-start(bf16[16,144,128]{2,1,0:T(8,128)(2,1)} %get-tuple-element.48._), calls=%async_computation.2 | async-start | bytes 1179648 | tf_op jit(solution)/shard_map/all_to_all | solution.py:518
  74.6 16.6 %collective-permute-start.4 = (bf16[48,2304]{1,0:T(8,128)(2,1)}, bf16[48,2304]{1,0:T(8,128)(2,1)S(1)}, u32[]{:S(2)}, u32[]{:S(2)}) collective-permute-start(bf16[48,2304]{1,0:T(8,128)(2,1)} %get-tuple-element.44), channel_id=1, source_target_pairs={{0,16},{16,32},{32,48},{48,64},{64,80},{80,96},{96,112},{112,128},... | collective-permute-start | bytes 663560 | tf_op jit(solution)/shard_map/ppermute | solution.py:389
  75.9 15.3 %collective-permute-start.5 = (bf16[48,2304]{1,0:T(8,128)(2,1)S(1)}, bf16[48,2304]{1,0:T(8,128)(2,1)S(1)}, u32[]{:S(2)}, u32[]{:S(2)}) collective-permute-start(bf16[48,2304]{1,0:T(8,128)(2,1)S(1)} %copy-done.11), channel_id=1, source_target_pairs={{0,240},{16,0},{32,16},{48,32},{64,48},{80,64},{96,80},{112,96},{1... | collective-permute-start | bytes 663560 | tf_op jit(solution)/shard_map/ppermute | solution.py:389
  79.6 11.6 %collective-permute-start.6 = (bf16[48,2304]{1,0:T(8,128)(2,1)S(1)}, bf16[48,2304]{1,0:T(8,128)(2,1)S(1)}, u32[]{:S(2)}, u32[]{:S(2)}) collective-permute-start(bf16[48,2304]{1,0:T(8,128)(2,1)S(1)} %copy-done.10), channel_id=1, source_target_pairs={{0,1},{1,2},{2,3},{3,4},{4,5},{5,6},{6,7},{7,8},{8,9},{9,10},{10,1... | collective-permute-start | bytes 663560 | tf_op jit(solution)/shard_map/ppermute | solution.py:389
  81.9 9.3 %collective-permute-start.7 = (bf16[48,2304]{1,0:T(8,128)(2,1)S(1)}, bf16[48,2304]{1,0:T(8,128)(2,1)S(1)}, u32[]{:S(2)}, u32[]{:S(2)}) collective-permute-start(bf16[48,2304]{1,0:T(8,128)(2,1)S(1)} %copy-done.9), channel_id=1, source_target_pairs={{0,15},{1,0},{2,1},{3,2},{4,3},{5,4},{6,5},{7,6},{8,7},{9,8},{10,9... | collective-permute-start | bytes 663560 | tf_op jit(solution)/shard_map/ppermute | solution.py:389
  91.2 0.7 copy-start.2
  91.2 0.8 copy-start.3
  91.2 0.9 copy-start.4
  91.2 0.9 copy-start.5

commit v2 on v1

v2 whole, which is shorter than its diff:
```python
import jax
import jax.numpy as jnp
import numpy as np
from jax import lax
from jax.experimental import pallas as pl
from jax.experimental.pallas import tpu as pltpu
from jax.sharding import PartitionSpec as P

NVAR = 5
NOBJ = 6
E = 96
H = 48
WMAX = 48
BLOCK = 320
TRACE = 80
LANES = 128
NBLK = 6
NSUP = 4
NBAS = 3
NVEC = NOBJ * NBAS
WIDE = NVEC * LANES
STEP = NBAS * LANES
SLOTS = 4 * H
FACES = 4 * E
VPAD = 24
WPAD = TRACE + 1
BPAD = 24
F32 = jnp.float32
BF16 = jnp.bfloat16


def selection():
    sel = np.zeros((BLOCK, 4 * LANES), np.float32)
    for var in range(NVAR):
        for a in range(4):
            for c in range(4):
                i = var * 16 + a * 4 + c
                base = var * 64
                sel[base + 48 + a * 4 + c, 0 * LANES + i] = 1
                sel[base + a * 4 + c, 1 * LANES + i] = 1
                sel[base + a * 16 + 12 + c, 2 * LANES + i] = 1
                sel[base + a * 16 + c, 3 * LANES + i] = 1
    return sel


def wall_spread():
    out = np.zeros((BLOCK, NVAR * LANES), np.float32)
    for var in range(NVAR):
        for p in range(16):
            out[var * 64 + p * 4, var * LANES + p : (var + 1) * LANES : 16] = 1
    return out


def dot(a, b, dims=((1,), (0,))):
    return lax.dot_general(a, b, (dims, ((), ())), preferred_element_type=F32)


def split(x):
    high = x.astype(BF16)
    return high, (x - high.astype(F32)).astype(BF16)


def picker(elements):
    n = elements.shape[1]
    row = lax.broadcasted_iota(jnp.int32, (E, n), 0)
    return jnp.where(row == elements, 1.0, 0.0).T.astype(BF16)


def fetch(pairs, sems):
    copies = [pltpu.make_async_copy(a, b, sems.at[n]) for n, (a, b) in enumerate(pairs)]
    for copy in copies:
        copy.start()
    return copies


def wait(*copies):
    for copy in copies:
        copy.wait()


def basis_kernel(
    flags, om_h, send_h, sel_h, r_h, d_h, s_h, sh_h, dots, table, us_h, o0, o1, o2, o3, om, send, sel, r, d, s, sh, us, sems, osems
):
    first = [(sel_h, sel), (sh_h, sh), (om_h, om), (send_h, send)]
    head = len(first)
    for k in range(NOBJ):
        first += [(r_h.at[k], r.at[k]), (d_h.at[:, k], d.at[:, k]), (s_h.at[:, k], s.at[:, k])]
    copies = fetch(first, sems)
    wait(*copies[:head])
    picks = [picker(send[f : f + 1, :]) for f in range(4)]
    stores = []
    for k in range(NOBJ):
        wait(*copies[head + 3 * k : head + 3 * k + 3])
        w = om[k]
        r0, d0, d1 = r[k], d[0, k], d[1, k]
        vecs = [w * r0, w * d0 + s[0, k], w * d1 + s[1, k]]
        for x, vec in enumerate([r0, d0, d1] + vecs):
            for i in range(2):
                dots[k, pl.ds(2 * x + i, 1), :] = jnp.sum(sh[i] * vec, axis=0, keepdims=True)
        dots[k, 12:16, :] = jnp.zeros((4, BLOCK), F32)
        for m, u in enumerate(vecs):
            us[k, m] = u
        stores += fetch([(us.at[k], us_h.at[k])], osems.at[k : k + 1])
        traces = dot(jnp.concatenate([u.astype(BF16) for u in vecs], axis=0), sel[...]).astype(BF16)
        at = slice(k * STEP, (k + 1) * STEP)
        for f, out in enumerate((o0, o1, o2, o3)):
            lanes = slice(f * LANES, (f + 1) * LANES)
            face = jnp.concatenate([traces[m * E : (m + 1) * E, lanes] for m in range(NBAS)], axis=1)
            table[f * H : (f + 1) * H, at] = face[H:]
            out[:, at] = dot(picks[f], face).astype(BF16)
    wait(*stores)


def relayout(b, f, wt, base, i, each=None):
    x = b[f, i].astype(F32)
    if each is not None:
        each(i, x)
    wt[pl.ds(base + i, E, stride=WPAD), 0:TRACE] = x.T


def blocks_kernel(_, perm_h, b_h, sh_h, selt_h, wt, q, hot, b, sh, selt, perm, qscr, square, sems):
    first = [(sh_h, sh), (selt_h, selt), (perm_h, perm)]
    copies = fetch(first + [(b_h.at[f], b.at[f]) for f in range(4)], sems)
    wait(*copies[:3])
    slot = perm[...]
    entry = jnp.where(slot < SLOTS, slot, SLOTS + (slot & 3) * H + (slot >> 2) - H)
    row = lax.broadcasted_iota(jnp.int32, (2 * SLOTS, FACES), 0)
    marks = jnp.where(row == entry, 1.0, 0.0).T
    for n in range(3):
        square[n] = marks[:, n * LANES : (n + 1) * LANES]
    parts = [split(sh[i]) for i in range(2)]
    nt = ((1,), (1,))
    for f in range(4):
        for n in range(3):
            lanes = slice(n * LANES, (n + 1) * LANES)
            hot[f * E : (f + 1) * E, lanes] = square[n, pl.ds(f, E, stride=4), :].astype(BF16)
        face = selt[f * LANES : (f + 1) * LANES, :]
        trsh = [(dot(face, high, nt) + dot(face, low, nt))[:TRACE] for high, low in parts]
        copies[3 + f].wait()

        def couple_shadow(i, x):
            for a in range(2):
                qscr[a, pl.ds(i, 1), :] = jnp.sum(x * trsh[a], axis=0, keepdims=True)

        for i in range(TRACE):
            relayout(b, f, wt, f * E * WPAD, i, couple_shadow)
        for a in range(2):
            q[a, f * E : (f + 1) * E, 0:TRACE] = qscr[a].T
            q[a, f * E : (f + 1) * E, TRACE:LANES] = jnp.zeros((E, LANES - TRACE), F32)


def received(flags, recv, at):
    return [jnp.where(flags[d] > 0, ref[:, at], jnp.zeros((), BF16)) for d, ref in enumerate(recv)]


def merge_kernel(x, _, out):
    out[...] = jnp.broadcast_to(jnp.sum(x[...], axis=0, keepdims=True), out.shape)


def couple(t_ref, wt, base, y_ref, pad, face, e):
    at = pl.ds(face * pad, pad)
    block = wt[pl.ds(base + e * WPAD, TRACE), 0:TRACE].astype(BF16)
    y_ref[at, 0:TRACE] = dot(t_ref[at, 0:TRACE].astype(BF16), block)


def face_rows(y_ref, row, pad):
    return jnp.concatenate([y_ref[pl.ds(f * E * pad + row, E, stride=pad), :] for f in range(4)], axis=1)


def lifted(y, selt):
    high, low = split(y)
    both = dot(jnp.concatenate([high, low], axis=0), selt[...])
    return both[:E] + both[E:]


def apply_kernel(
    flags, hot, table, r0, r1, r2, r3, q, dots, wt, red, yn_h, rows, t_ref, y_ref, yn, osems
):
    y_ref[...] = jnp.zeros_like(y_ref)
    lane = lax.broadcasted_iota(jnp.int32, (16, LANES), 1)
    acc = jnp.zeros((16, LANES), F32)
    for k in range(NOBJ):
        at = slice(k * STEP, (k + 1) * STEP)
        full = jnp.concatenate(received(flags, (r0, r1, r2, r3), at) + [table[:, at]], axis=0)
        t = dot(hot[...], full)
        rows[k] = jnp.zeros((16, LANES), F32)
        for m in range(NBAS):
            part = t[:, m * LANES : (m + 1) * LANES]
            for f in range(4):
                to = pl.ds(f * E * VPAD + k * NBAS + m, E, stride=VPAD)
                t_ref[to, :] = part[f * E : (f + 1) * E]
            for i in range(2):
                rows[k, pl.ds(6 + 2 * m + i, 1), :] = jnp.sum(part * q[i], axis=0, keepdims=True)
        col = jnp.sum(rows[k], axis=1, keepdims=True) + jnp.sum(dots[k], axis=1, keepdims=True)
        acc += jnp.where(lane == k, col, 0.0)
    red[...] = jnp.broadcast_to(acc[None], red.shape)
    for face in range(FACES):
        couple(t_ref, wt, face // E * E * WPAD, y_ref, VPAD, face, face % E)
    stores = []
    for k in range(NOBJ):
        for m in range(NBAS):
            y = face_rows(y_ref, k * NBAS + m, VPAD)
            for f in range(4):
                yn[k, m, f] = y[:, f * LANES : (f + 1) * LANES]
        stores += fetch([(yn.at[k], yn_h.at[k])], osems.at[k : k + 1])
    wait(*stores)


def outgo_kernel(_, yn_h, send_h, cross_h, o0, o1, o2, o3, yn, send, cross, out, sems, osems):
    first = [(send_h, send), (cross_h, cross)] + [(yn_h.at[k], yn.at[k]) for k in range(NOBJ)]
    copies = fetch(first, sems)
    wait(*copies[:2])
    picks = [picker(send[f : f + 1, :]) for f in range(4)]
    for k in range(NOBJ):
        copies[2 + k].wait()
        ys = [jnp.concatenate([yn[k, m, f].astype(BF16) for f in range(4)], axis=1) for m in range(NBAS)]
        total = dot(jnp.concatenate(ys, axis=0), cross[...]).astype(BF16)
        at = slice(k * STEP, (k + 1) * STEP)
        for f in range(4):
            lanes = slice(f * LANES, (f + 1) * LANES)
            face = jnp.concatenate([total[m * E : (m + 1) * E, lanes] for m in range(NBAS)], axis=1)
            out[f, :, at] = dot(picks[f], face).astype(BF16)
    wait(*fetch([(out.at[f], o) for f, o in enumerate((o0, o1, o2, o3))], osems))


def solve(m00, m01, m10, m11, f0, f1):
    det = m00 * m11 - m01 * m10
    return (m11 * f0 - m01 * f1) / det, (m00 * f1 - m10 * f0) / det


def step_kernel(
    om, count, red, us_h, it_h, yn_h, wall, coef, selt_h, spread_h, itout_h, base_h, st2_h, coefs, payload, us, it, yn, selt, spread, itout, base, st2, points, scr, sems, osems
):
    first = [(selt_h, selt)]
    for k in range(NOBJ):
        first += [(h.at[k], x.at[k]) for h, x in ((us_h, us), (yn_h, yn), (it_h, it))]
    copies = fetch(first + [(spread_h, spread)], sems)
    t = jnp.sum(red[...], axis=0)
    row = lambda n: t[n : n + 1]
    lane = lax.broadcasted_iota(jnp.int32, (1, LANES), 1)
    w = sum(jnp.where(lane == k, om[k], 0.0) for k in range(NOBJ))
    c0, c1 = solve(row(2), row(4), row(3), row(5), row(0), row(1))
    n0 = -(row(6) - c0 * row(8) - c1 * row(10))
    n1 = -(row(7) - c0 * row(9) - c1 * row(11))
    e0, e1 = solve(n0, row(4), n1, row(5), row(0) + n0, row(1) + n1)
    gamma = w * (1.0 - e0)
    delta = gamma + e0
    for n, x in enumerate([c0, c1, 1.0 - delta, delta * c0, delta * c1 - e1, gamma, 1.0 / w, w]):
        coefs[pl.ds(n, 1), :] = x
    scr[...] = jnp.zeros_like(scr)
    slots = lax.broadcasted_iota(jnp.int32, (1, WMAX), 1)
    pick = picker(jnp.where(slots < count[0], wall[:, 0:WMAX], E))
    slot = lax.broadcasted_iota(jnp.int32, (WMAX, LANES), 0) % 8
    group = lax.broadcasted_iota(jnp.int32, (WMAX, LANES), 1) // 16
    mine = slot == group
    copies[0].wait()
    stores = []
    half = NOBJ * WMAX
    for k in range(NOBJ):
        wait(*copies[1 + 3 * k : 4 + 3 * k])
        c = [coefs[n : n + 1, k : k + 1] for n in range(7)]
        u0, u1, u2 = (us[k, m] for m in range(NBAS))
        st1 = u0 - c[0] * u1 - c[1] * u2
        y = [yn[k, 0, f] - c[0] * yn[k, 1, f] - c[1] * yn[k, 2, f] for f in range(4)]
        lift = lifted(jnp.concatenate(y, axis=1), selt)
        two = c[2] * u0 + c[3] * u1 + c[4] * u2 - c[5] * lift
        both = st1 + two
        new = it[k] + both
        itout[k] = new
        st2[k] = two[H:]
        base[k] = c[6] * u0 - both - lift
        outs = [(x.at[k], h.at[k]) for x, h in ((itout, itout_h), (st2, st2_h), (base, base_h))]
        stores += fetch(outs, osems.at[3 * k : 3 * k + 3])
        high, low = split(new)
        high, low = split(dot(pick, high) + dot(pick, low))
        points[k * WMAX : (k + 1) * WMAX, :] = high
        points[half + k * WMAX : half + (k + 1) * WMAX, :] = low
    copies[-1].wait()
    every = dot(points[...], spread[...])
    for k in range(NOBJ):
        at = slice(k * WMAX, (k + 1) * WMAX)
        below = slice(half + k * WMAX, half + (k + 1) * WMAX)
        wide = every[at] + every[below]
        sums = [None] * 3
        for var in range(NVAR):
            part = wide[:, var * LANES : (var + 1) * LANES]
            part = jnp.sum(jnp.where(mine, part, 0.0).reshape(NBLK, 8, LANES), axis=1)
            for a in range(3):
                term = coef[a * NVAR + var] * part
                sums[a] = term if sums[a] is None else sums[a] + term
        for a in range(3):
            scr[pl.ds(a * NOBJ + k, NBLK, stride=BPAD), :] = sums[a]
    payload[...] = jnp.broadcast_to(scr[...].astype(BF16)[None], payload.shape)
    wait(*stores)


def last_kernel(
    flags, coefs, hot, st2_h, base_h, a0, a1, a2, a3, b0_h, b1_h, b2_h, b3_h, blocks_h, sel_h, selt_h, w_h, _, out_h, weights, t_ref, y_ref, st2, base, b, blocks, w0, w1, w2, w3, sel, selt, out, sems, osems
):
    first = [(sel_h, sel), (st2_h, st2)] + [(h, b.at[d]) for d, h in enumerate((b0_h, b1_h, b2_h, b3_h))]
    first += [(blocks_h.at[f], blocks.at[f]) for f in range(4)] + [(selt_h, selt), (base_h, base), (w_h, weights)]
    copies = fetch(first, sems)
    y_ref[...] = jnp.zeros_like(y_ref)
    wait(*copies[:6])
    for k in range(NOBJ):
        c = [coefs[n : n + 1, k : k + 1] for n in range(6)]
        rows = []
        for d, a in enumerate((a0, a1, a2, a3)):
            u = [a[:, (k * NBAS + m) * LANES : (k * NBAS + m + 1) * LANES].astype(F32) for m in range(3)]
            y = [b[d, :, (k * NBAS + m) * LANES : (k * NBAS + m + 1) * LANES].astype(F32) for m in range(3)]
            x = c[2] * u[0] + c[3] * u[1] + c[4] * u[2] - c[5] * (y[0] - c[0] * y[1] - c[1] * y[2])
            rows.append(jnp.where(flags[d] > 0, x, 0.0).astype(BF16))
        local = dot(st2[k].astype(BF16), sel[...]).astype(BF16)
        rows += [local[:, f * LANES : (f + 1) * LANES] for f in range(4)]
        t = dot(hot[...], jnp.concatenate(rows, axis=0))
        for f in range(4):
            t_ref[pl.ds(f * E * 8 + k, E, stride=8), :] = t[f * E : (f + 1) * E]
    wts = (w0, w1, w2, w3)
    rounds = 16
    for f in range(5):
        if f < 4:
            copies[6 + f].wait()
        for n in range(rounds):
            for c in range(TRACE // rounds):
                if f < 4:
                    relayout(blocks, f, wts[f], 0, n * (TRACE // rounds) + c)
            for c in range(E // rounds):
                if f > 0:
                    e = n * (E // rounds) + c
                    couple(t_ref, wts[f - 1], 0, y_ref, 8, (f - 1) * E + e, e)
    wait(*copies[10:12])
    stores = []
    for k in range(NOBJ):
        out[k] = base[k] - lifted(face_rows(y_ref, k, 8), selt)
        stores += fetch([(out.at[k], out_h.at[k])], osems.at[k : k + 1])
    wait(*stores, *copies[12:])


def smooth_kernel(support, sens, weights, out, scr):
    scr[...] = sens[...].astype(F32)
    for m in range(NBLK):
        acc = None
        for s in range(NSUP):
            at = pl.multiple_of(support[m, s] * BPAD, 8)
            part = dot(scr[pl.ds(at, BPAD), :].astype(BF16), weights[m, s])
            acc = part if acc is None else acc + part
        out[:, m * LANES : (m + 1) * LANES] = acc[: 3 * NOBJ]


SMEM = pl.BlockSpec(memory_space=pltpu.SMEM)
ANY = pl.BlockSpec(memory_space=pl.ANY)
VMEM = pl.BlockSpec(memory_space=pltpu.VMEM)


def shape(dims, dtype):
    return jax.ShapeDtypeStruct(dims, dtype)


def far(x):
    return pltpu.with_memory_space_constraint(x, pltpu.HBM)


def near(x):
    return pltpu.with_memory_space_constraint(x, pltpu.VMEM)


def buffers(*arrays):
    return [pltpu.VMEM(x.shape, x.dtype) for x in arrays]


def local_call(kernel, name, us, mib, ins, outs, scratch):
    result = pl.pallas_call(
        kernel,
        in_specs=[spec for spec, _ in ins],
        out_specs=[spec for spec, _ in outs],
        out_shape=[x for _, x in outs],
        scratch_shapes=scratch,
        compiler_params=pltpu.CompilerParams(vmem_limit_bytes=mib << 20),
        cost_estimate=pl.CostEstimate(flops=int(us * 5e8), bytes_accessed=int(us * 1e6), transcendentals=0),
        name=name,
    )(*[x for _, x in ins])
    return result


def exchange(outgo):
    recv = []
    for d, (axis, shift) in enumerate((("row", 1), ("row", -1), ("col", 1), ("col", -1))):
        size = lax.axis_size(axis)
        recv.append(lax.ppermute(outgo[d], axis, [(i, (i + shift) % size) for i in range(size)]))
    return recv


def per_device(
    iterate,
    residual,
    shadow,
    res_dirs,
    sol_dirs,
    omega_step,
    face_blocks,
    send_list,
    neighbour_perm,
    wall_perm,
    wall_count,
    wall_coef,
    rbf_support,
    rbf_weights,
):
    n_row, n_col = lax.axis_size("row"), lax.axis_size("col")
    sel_np = selection()
    sel = jnp.asarray(sel_np, BF16)
    selt = jnp.asarray(sel_np.T, BF16)
    cross = jnp.asarray(sel_np.T @ sel_np, BF16)
    spread = jnp.asarray(wall_spread(), BF16)
    sem = pltpu.SemaphoreType.DMA
    fields = (NOBJ, E, BLOCK)
    traces = pltpu.VMEM((H, WIDE), BF16)

    spare = (NOBJ, NBAS, 4, E, LANES)
    basis = (NOBJ, NBAS, E, BLOCK)

    row, col = lax.axis_index("row"), lax.axis_index("col")
    flags = jnp.stack([row > 0, row < n_row - 1, col > 0, col < n_col - 1]).astype(jnp.int32)
    dots, table, us, *outgo = local_call(
        basis_kernel,
        "basis",
        5,
        24,
        [(SMEM, flags)]
        + [(ANY, far(x)) for x in (omega_step, send_list, sel, residual, res_dirs, sol_dirs, shadow)],
        [
            (VMEM, pltpu.VMEM((NOBJ, 16, BLOCK), F32)),
            (VMEM, pltpu.VMEM((SLOTS, WIDE), BF16)),
            (ANY, pltpu.HBM(basis, F32)),
        ]
        + [(VMEM, traces)] * 4,
        [pltpu.SMEM((NOBJ,), F32)]
        + buffers(send_list, sel, residual, res_dirs, sol_dirs, shadow)
        + [pltpu.VMEM(basis, F32), sem((4 + 3 * NOBJ,)), sem((NOBJ,))],
    )
    recv = exchange(outgo)

    blocks = face_blocks.transpose(1, 2, 3, 0)
    wt, q, hot = local_call(
        blocks_kernel,
        "blocks",
        6,
        12,
        [(VMEM, near(dots))] + [(ANY, far(x)) for x in (neighbour_perm, blocks, shadow, selt)],
        [
            (VMEM, pltpu.VMEM((FACES * WPAD, LANES), F32)),
            (VMEM, pltpu.VMEM((2, FACES, LANES), F32)),
            (VMEM, pltpu.VMEM((FACES, 2 * SLOTS), BF16)),
        ],
        buffers(blocks, shadow, selt, neighbour_perm)
        + [pltpu.VMEM((2, TRACE, E), F32), pltpu.VMEM((3, FACES, LANES), F32), sem((7,))],
    )

    red, yn = local_call(
        apply_kernel,
        "apply",
        7,
        24,
        [(SMEM, flags), (VMEM, near(hot)), (VMEM, near(table))]
        + [(VMEM, near(x)) for x in recv + [q, dots, wt]],
        [(VMEM, shape((n_row, 16, LANES), F32)), (ANY, pltpu.HBM(spare, F32))],
        [pltpu.VMEM((NOBJ, 16, LANES), F32)]
        + [pltpu.VMEM((FACES * VPAD, LANES), F32)] * 2
        + [pltpu.VMEM(spare, F32), sem((NOBJ,))],
    )
    outgo2 = local_call(
        outgo_kernel,
        "outgo",
        4,
        12,
        [(ANY, red)] + [(ANY, far(x)) for x in (yn, send_list, cross)],
        [(ANY, pltpu.HBM((H, WIDE), BF16))] * 4,
        [pltpu.VMEM(spare, F32)]
        + buffers(send_list, cross)
        + [pltpu.VMEM((4, H, WIDE), BF16), sem((2 + NOBJ,)), sem((4,))],
    )
    recv2 = exchange(outgo2)
    red_row = lax.all_to_all(red, "row", 0, 0, tiled=True)
    wall_coef, wall_perm, wall_count, rbf_support, red = lax.optimization_barrier(
        (wall_coef, wall_perm, wall_count, rbf_support, red)
    )
    coef = wall_coef.reshape(3 * NVAR, NBLK, LANES).astype(F32)
    (red_row,) = local_call(
        merge_kernel, "merge", 1, 4, [(VMEM, red_row), (ANY, far(outgo2[0]))], [(VMEM, shape((n_col, 16, LANES), F32))], []
    )
    red = lax.all_to_all(red_row, "col", 0, 0, tiled=True)

    payload = (n_row, NBLK * BPAD, LANES)
    upper = (NOBJ, E - H, BLOCK)
    itout, base, st2, coefs, payload = local_call(
        step_kernel,
        "step",
        6,
        32,
        [(SMEM, omega_step), (SMEM, wall_count), (VMEM, red)]
        + [(ANY, far(x)) for x in (us, iterate, yn)]
        + [(VMEM, wall_perm), (VMEM, near(coef)), (ANY, far(selt)), (ANY, far(spread))],
        [(ANY, shape(fields, F32)), (ANY, pltpu.HBM(fields, F32)), (ANY, pltpu.HBM(upper, F32))]
        + [(VMEM, pltpu.VMEM((8, LANES), F32)), (VMEM, shape(payload, BF16))],
        [pltpu.VMEM(basis, F32)]
        + buffers(iterate)
        + [pltpu.VMEM(spare, F32)]
        + buffers(selt, spread)
        + [pltpu.VMEM(fields, F32)] * 2
        + [pltpu.VMEM(upper, F32), pltpu.VMEM((2 * NOBJ * WMAX, BLOCK), BF16)]
        + [pltpu.VMEM((NBLK * BPAD, LANES), F32), sem((2 + 3 * NOBJ,)), sem((3 * NOBJ,))],
    )
    payload, *recv2 = lax.optimization_barrier((payload, *recv2))
    sens = lax.all_to_all(payload, "row", 0, 0, tiled=True)

    resout, weights = local_call(
        last_kernel,
        "last",
        8,
        40,
        [(SMEM, flags), (VMEM, near(coefs)), (VMEM, near(hot)), (ANY, far(st2)), (ANY, far(base))]
        + [(VMEM, near(x)) for x in recv]
        + [(ANY, far(x)) for x in recv2 + [blocks, sel, selt, rbf_weights]]
        + [(ANY, payload)],
        [(ANY, shape(fields, F32)), (VMEM, pltpu.VMEM(rbf_weights.shape, BF16))],
        [pltpu.VMEM((FACES * 8, LANES), F32)] * 2
        + [pltpu.VMEM(upper, F32), pltpu.VMEM(fields, F32), pltpu.VMEM((4, H, WIDE), BF16)]
        + buffers(blocks)
        + [pltpu.VMEM((E * WPAD, LANES), F32)] * 4
        + buffers(sel, selt, residual)
        + [sem((13,)), sem((NOBJ,))],
    )

    (smoothed,) = local_call(
        smooth_kernel,
        "smooth",
        2,
        8,
        [(SMEM, rbf_support), (VMEM, sens.reshape(-1, LANES)), (VMEM, near(weights))],
        [(VMEM, shape((3 * NOBJ, NBLK * LANES), F32))],
        [pltpu.VMEM((n_row * NBLK * BPAD, LANES), F32)],
    )
    return (itout, resout, smoothed)


def solution(mesh):
    both = ("row", "col")
    in_specs = (
        P(None, both, None),
        P(None, both, None),
        P(None, both, None),
        P(None, None, both, None),
        P(None, None, both, None),
        P(),
        P(both, None, None, None),
        P(both, None),
        P(both, None),
        P(both, None),
        P(both),
        P(None, None, both),
        P(both, None),
        P(both, None, None, None),
    )
    out_specs = (P(None, both, None), P(None, both, None), P(None, both))
    return jax.shard_map(
        per_device, mesh=mesh, in_specs=in_specs, out_specs=out_specs, check_vma=False
    )
```

time: 103 us -> 86 us (0.83)
  waiting for transfers between devices: 15.1 us -> 6.57 us
  Pallas kernels: 50.3 us -> 42.5 us
  local copies, waits for them, and re-layouts: 1.46 us -> 0.15 us
    ppermute x8, waiting for transfers between devices: 9.2 us -> 0.02 us  [exchange(): lax.ppermute(outgo[d], axis, [(i, (i + shift) % size) for i in range(size)])]
    pallas_call x8, Pallas kernels: 50.3 us -> 42.5 us  [local_call(): pl.pallas_call(kernel, in_specs=[spec for spec, _ in ins], out_specs=[spe...]
    all_to_all x1, waiting for transfers between devices: 5.93 us -> 1.32 us  [per_device(): red_row = lax.all_to_all(red, 'row', 0, 0, tiled=True)]
    all_to_all x1, waiting for transfers between devices: 0.01 us -> 3.89 us  [per_device(): sens = lax.all_to_all(payload, 'row', 0, 0, tiled=True)]
    all_to_all x1, waiting for transfers between devices: 0.01 us -> 1.35 us  [per_device(): red = lax.all_to_all(red_row, 'col', 0, 0, tiled=True)]
    unnamed x25 -> x16, local copies, waits for them, and re-layouts: 1.07 us -> 0.04 us
  transfers between devices with their start and end apart: 11 -> 11, of which waited for: 2 -> 3; matrix products, arithmetic and copies ran while one was open for 1% -> 0% of each run, Pallas kernels for 30% -> 31%
where the time goes in v2:
time: 86 us; the launch traced here: 85.7 us
  Pallas kernels  42.5 us (49%)
  starting transfers between devices  34.9 us (41%)
  waiting for transfers between devices  6.57 us (8%)
  between operations  1.51 us (2%)
    pallas_call x8, Pallas kernels, local_call(): pl.pallas_call(kernel, in_specs=[spec for spec, _ in ins], out_specs=[spe...  42.5 us
    ppermute x8, starting transfers between devices, exchange(): lax.ppermute(outgo[d], axis, [(i, (i + shift) % size) for i in range(size)])  15.8 us
    all_to_all x1, starting transfers between devices, per_device(): red = lax.all_to_all(red_row, 'col', 0, 0, tiled=True)  11.1 us
    all_to_all x1, starting transfers between devices, per_device(): sens = lax.all_to_all(payload, 'row', 0, 0, tiled=True)  4.45 us
    all_to_all x1, waiting for transfers between devices, per_device(): sens = lax.all_to_all(payload, 'row', 0, 0, tiled=True)  3.89 us
    all_to_all x1, starting transfers between devices, per_device(): red_row = lax.all_to_all(red, 'row', 0, 0, tiled=True)  3.52 us
  transfers between devices with their start and end apart: 11, of which 3 were waited for; matrix products, arithmetic and copies ran while one was open for 0% of the time, Pallas kernels for 31%

profile of v2, /device:TPU:1, one launch (start us, length us, event | category | flops | bytes accessed | tf_op | source)
XLA Modules:
  0.0 85.7 jit_solution(12059687526053833436)
XLA Ops:
  0.6 0.1 add_convert_fusion.flags
  0.7 5.9 %basis.1 = (f32[6,16,320]{2,1,0:T(8,128)S(1)}, bf16[192,2304]{1,0:T(8,128)(2,1)S(1)}, f32[6,3,96,320]{3,2,1,0:T(8,128)}, bf16[48,2304]{1,0:T(8,128)(2,1)S(1)}, b...) custom-call(s32[4]{0:T(128)S(1)} %add_convert_fusion.flags, f32[6]{0:T(128)} %om.1, ...), custom_call_target="tpu_custom_call" | custom-call | flops 2500000000 | bytes 5000000 | tf_op jit(solution)/shard_map/basis/pallas_call | solution.py:372
  6.6 2.2 %collective-permute-start = (bf16[48,2304]{1,0:T(8,128)(2,1)S(1)}, bf16[48,2304]{1,0:T(8,128)(2,1)S(1)}, u32[]{:S(2)}, u32[]{:S(2)}) collective-permute-start(bf16[48,2304]{1,0:T(8,128)(2,1)S(1)} %get-tuple-element.38), channel_id=1, source_target_pairs={{0,16},{16,32},{32,48},{48,64},{64,80},{80,96},{96,112},{112,128},... | collective-permute-start | bytes 663560 | tf_op jit(solution)/shard_map/ppermute | solution.py:389
  8.8 3.9 %collective-permute-start.1 = (bf16[48,2304]{1,0:T(8,128)(2,1)S(1)}, bf16[48,2304]{1,0:T(8,128)(2,1)S(1)}, u32[]{:S(2)}, u32[]{:S(2)}) collective-permute-start(bf16[48,2304]{1,0:T(8,128)(2,1)S(1)} %get-tuple-element.39), channel_id=1, source_target_pairs={{0,240},{16,0},{32,16},{48,32},{64,48},{80,64},{96,80},{112,96},{1... | collective-permute-start | bytes 663560 | tf_op jit(solution)/shard_map/ppermute | solution.py:389
  12.7 2.5 %collective-permute-start.2 = (bf16[48,2304]{1,0:T(8,128)(2,1)S(1)}, bf16[48,2304]{1,0:T(8,128)(2,1)S(1)}, u32[]{:S(2)}, u32[]{:S(2)}) collective-permute-start(bf16[48,2304]{1,0:T(8,128)(2,1)S(1)} %get-tuple-element.40), channel_id=1, source_target_pairs={{0,1},{1,2},{2,3},{3,4},{4,5},{5,6},{6,7},{7,8},{8,9},{9,10},{10,1... | collective-permute-start | bytes 663560 | tf_op jit(solution)/shard_map/ppermute | solution.py:389
  15.2 0.1 collective-permute-start.3
  15.3 6.2 %blocks.1 = (f32[31104,128]{1,0:T(8,128)S(1)}, f32[2,384,128]{2,1,0:T(8,128)S(1)}, bf16[384,384]{1,0:T(8,128)(2,1)S(1)}) custom-call(f32[6,16,320]{2,1,0:T(8,128)S(1)} %get-tuple-element.35._.dots, s32[1,384]{1,0:T(1,128)} %perm_h.1, bf16[4,80,80,96]{3,2,1,0:T(8,128)(2,1)} %bitcast.7, f32[2,96,320]{2,1,0:T(8,128)} %sh_h.3, ...), custom_call_target="tpu_custom_call" | custom-call | flops 3000000000 | bytes 6000000 | tf_op jit(solution)/shard_map/blocks/pallas_call | solution.py:372
  21.5 0.0 collective-permute-done.r0.a0
  21.5 0.0 collective-permute-done.1.r1.a1
  21.6 0.0 collective-permute-done.2.r2.a2
  21.6 0.0 collective-permute-done.3.r3.a3
  21.6 7.5 %apply.1 = (f32[16,16,128]{2,1,0:T(8,128)}, f32[6,3,4,96,128]{4,3,2,1,0:T(8,128)}) custom-call(s32[4]{0:T(128)S(1)} %add_convert_fusion.flags, bf16[384,384]{1,0:T(8,128)(2,1)S(1)} %get-tuple-element.36.hot, bf16[192,2304]{1,0:T(8,128)(2,1)S(1)} %get-tuple-element.37.table, bf16[48,2304]{1,0:T(8,128)(2,1)S(1)} %collective-permute-done.r0.a0, ...), custom_call_target="tpu_custom_call" | custom-call | flops 3500000000 | bytes 7000000 | tf_op jit(solution)/shard_map/apply/pallas_call | solution.py:372
  29.1 3.5 %all-to-all-start = ((f32[16,16,128]{2,1,0:T(8,128)}), f32[16,16,128]{2,1,0:T(8,128)S(1)}, u32[]{:S(2)}, u32[]{:S(2)}) async-start(f32[16,16,128]{2,1,0:T(8,128)} %get-tuple-element.44._), calls=%async_computation | async-start | bytes 262144 | tf_op jit(solution)/shard_map/all_to_all | solution.py:483
  32.6 0.0 copy-start.2
  32.6 0.0 copy-start
  32.7 0.0 copy-start.1
  32.7 5.3 %outgo.1 = (bf16[48,2304]{1,0:T(8,128)(2,1)}, bf16[48,2304]{1,0:T(8,128)(2,1)}, bf16[48,2304]{1,0:T(8,128)(2,1)}, bf16[48,2304]{1,0:T(8,128)(2,1)}) custom-call(f32[16,16,128]{2,1,0:T(8,128)} %get-tuple-element.44._, f32[6,3,4,96,128]{4,3,2,1,0:T(8,128)} %get-tuple-element.46.yn_h, s32[4,48]{1,0:T(4,128)} %send_h.3, bf16[512,512]{1,0:T(8,128)(2,1)} %constant.21.clone.cross_h), custom_call_target="tpu_custom_call" | custom-call | flops 2000000000 | bytes 4000000 | tf_op jit(solution)/shard_map/outgo/pallas_call | solution.py:372
  37.9 1.3 %all-to-all-done.x = f32[16,16,128]{2,1,0:T(8,128)S(1)} async-done(((f32[16,16,128]{2,1,0:T(8,128)}), f32[16,16,128]{2,1,0:T(8,128)S(1)}, u32[]{:S(2)}, u32[]{:S(2)}) %all-to-all-start) | async-done | bytes 131104 | tf_op jit(solution)/shard_map/all_to_all | solution.py:483
  39.3 0.7 merge.1
  39.9 11.1 %all-to-all-start.1 = ((f32[16,16,128]{2,1,0:T(8,128)}), f32[16,16,128]{2,1,0:T(8,128)S(1)}, u32[]{:S(2)}, u32[]{:S(2)}) async-start(f32[16,16,128]{2,1,0:T(8,128)} %merge.1), calls=%async_computation.1 | async-start | bytes 262144 | tf_op jit(solution)/shard_map/all_to_all | solution.py:491
  51.7 0.3 collective-permute-start.4
  52.0 0.0 copy-done.2
  52.0 4.7 %collective-permute-start.5 = (bf16[48,2304]{1,0:T(8,128)(2,1)}, bf16[48,2304]{1,0:T(8,128)(2,1)S(1)}, u32[]{:S(2)}, u32[]{:S(2)}) collective-permute-start(bf16[48,2304]{1,0:T(8,128)(2,1)} %get-tuple-element.56), channel_id=1, source_target_pairs={{0,240},{16,0},{32,16},{48,32},{64,48},{80,64},{96,80},{112,96},{1... | collective-permute-start | bytes 663560 | tf_op jit(solution)/shard_map/ppermute | solution.py:389
  56.7 2.2 %collective-permute-start.6 = (bf16[48,2304]{1,0:T(8,128)(2,1)}, bf16[48,2304]{1,0:T(8,128)(2,1)S(1)}, u32[]{:S(2)}, u32[]{:S(2)}) collective-permute-start(bf16[48,2304]{1,0:T(8,128)(2,1)} %get-tuple-element.57), channel_id=1, source_target_pairs={{0,1},{1,2},{2,3},{3,4},{4,5},{5,6},{6,7},{7,8},{8,9},{9,10},{10,1... | collective-permute-start | bytes 663560 | tf_op jit(solution)/shard_map/ppermute | solution.py:389
  58.9 0.0 collective-permute-start.7
  58.9 1.3 %all-to-all-done.1.red = f32[16,16,128]{2,1,0:T(8,128)S(1)} async-done(((f32[16,16,128]{2,1,0:T(8,128)}), f32[16,16,128]{2,1,0:T(8,128)S(1)}, u32[]{:S(2)}, u32[]{:S(2)}) %all-to-all-start.1) | async-done | bytes 131104 | tf_op jit(solution)/shard_map/all_to_all | solution.py:491
  60.2 0.0 copy-done
  60.2 0.0 copy-done.1
  60.2 0.0 copy-start.3
  60.2 7.0 %step.1 = (f32[6,96,320]{2,1,0:T(8,128)}, f32[6,96,320]{2,1,0:T(8,128)}, f32[6,48,320]{2,1,0:T(8,128)}, f32[8,128]{1,0:T(8,128)S(1)}, bf16[16,144,128]{2,1,0:T(8,128)(2,1)}) custom-call(f32[6]{0:T(128)S(1)} %copy-done, s32[1]{0:T(128)S(6)} %copy.25.count, f32[16,16,128]{2,1,0:T(8,128)S(1)} %all-to-all-done.1.red, f32[6,3,96,320]{3,2,1,0:T(8,128)} %get-tuple-element.48.us_h, ...), custom_call_target="tpu_custom_call" | custom-call | flops 3000000000 | bytes 6000000 | tf_op jit(solution)/shard_map/step/pallas_call | solution.py:372
  67.2 0.0 collective-permute-done.4.b0_h
  67.3 0.0 copy-start.4
  67.3 0.0 collective-permute-done.5.b1_h
  67.3 0.0 copy-start.5
  67.3 0.0 collective-permute-done.6.b2_h
  67.3 0.0 copy-start.6
  67.3 0.0 collective-permute-done.7.b3_h
  67.3 0.0 copy-start.7
  67.3 4.4 %all-to-all-start.2 = ((bf16[16,144,128]{2,1,0:T(8,128)(2,1)}), bf16[16,144,128]{2,1,0:T(8,128)(2,1)S(1)}, u32[]{:S(2)}, u32[]{:S(2)}) async-start(bf16[16,144,128]{2,1,0:T(8,128)(2,1)} %get-tuple-element.63._), calls=%async_computation.2 | async-start | bytes 1179648 | tf_op jit(solution)/shard_map/all_to_all | solution.py:514
  71.8 0.0 copy-done.3
  71.8 0.1 copy.24.support
  71.9 0.0 copy-done.4
  71.9 0.0 copy-done.5
  71.9 0.0 copy-done.6
  71.9 0.0 copy-done.7
  71.9 8.3 %last.1 = (f32[6,96,320]{2,1,0:T(8,128)}, bf16[6,4,128,128]{3,2,1,0:T(8,128)(2,1)S(1)}) custom-call(s32[4]{0:T(128)S(1)} %add_convert_fusion.flags, f32[8,128]{1,0:T(8,128)S(1)} %get-tuple-element.52.coefs, bf16[384,384]{1,0:T(8,128)(2,1)S(1)} %get-tuple-element.36.hot, f32[6,48,320]{2,1,0:T(8,128)} %get-tuple-element.53.st2_h, ...), custom_call_target="tpu_custom_call" | custom-call | flops 4000000000 | bytes 8000000 | tf_op jit(solution)/shard_map/last/pallas_call | solution.py:372
  80.2 3.9 %all-to-all-done.2 = bf16[16,144,128]{2,1,0:T(8,128)(2,1)S(1)} async-done(((bf16[16,144,128]{2,1,0:T(8,128)(2,1)}), bf16[16,144,128]{2,1,0:T(8,128)(2,1)S(1)}, u32[]{:S(2)}, u32[]{:S(2)}) %all-to-all-start.2) | async-done | bytes 589856 | tf_op jit(solution)/shard_map/all_to_all | solution.py:514
  84.1 1.6 %smooth.1 = f32[18,768]{1,0:T(8,128)} custom-call(s32[6,4]{1,0:T(8,128)S(1)} %copy.24.support, bf16[2304,128]{1,0:T(8,128)(2,1)S(1)} %bitcast.6, bf16[6,4,128,128]{3,2,1,0:T(8,128)(2,1)S(1)} %get-tuple-element.66.weights), custom_call_target="tpu_custom_call" | custom-call | flops 1000000000 | bytes 2000000 | tf_op jit(solution)/shard_map/smooth/pallas_call | solution.py:372
  (2 shorter events, 0.0 us)
Async XLA Ops:
  6.6 14.9 %collective-permute-start = (bf16[48,2304]{1,0:T(8,128)(2,1)S(1)}, bf16[48,2304]{1,0:T(8,128)(2,1)S(1)}, u32[]{:S(2)}, u32[]{:S(2)}) collective-permute-start(bf16[48,2304]{1,0:T(8,128)(2,1)S(1)} %get-tuple-element.38), channel_id=1, source_target_pairs={{0,16},{16,32},{32,48},{48,64},{64,80},{80,96},{96,112},{112,128},... | collective-permute-start | bytes 663560 | tf_op jit(solution)/shard_map/ppermute | solution.py:389
  8.8 12.7 %collective-permute-start.1 = (bf16[48,2304]{1,0:T(8,128)(2,1)S(1)}, bf16[48,2304]{1,0:T(8,128)(2,1)S(1)}, u32[]{:S(2)}, u32[]{:S(2)}) collective-permute-start(bf16[48,2304]{1,0:T(8,128)(2,1)S(1)} %get-tuple-element.39), channel_id=1, source_target_pairs={{0,240},{16,0},{32,16},{48,32},{64,48},{80,64},{96,80},{112,96},{1... | collective-permute-start | bytes 663560 | tf_op jit(solution)/shard_map/ppermute | solution.py:389
  12.7 8.8 %collective-permute-start.2 = (bf16[48,2304]{1,0:T(8,128)(2,1)S(1)}, bf16[48,2304]{1,0:T(8,128)(2,1)S(1)}, u32[]{:S(2)}, u32[]{:S(2)}) collective-permute-start(bf16[48,2304]{1,0:T(8,128)(2,1)S(1)} %get-tuple-element.40), channel_id=1, source_target_pairs={{0,1},{1,2},{2,3},{3,4},{4,5},{5,6},{6,7},{7,8},{8,9},{9,10},{10,1... | collective-permute-start | bytes 663560 | tf_op jit(solution)/shard_map/ppermute | solution.py:389
  15.2 6.4 %collective-permute-start.3 = (bf16[48,2304]{1,0:T(8,128)(2,1)S(1)}, bf16[48,2304]{1,0:T(8,128)(2,1)S(1)}, u32[]{:S(2)}, u32[]{:S(2)}) collective-permute-start(bf16[48,2304]{1,0:T(8,128)(2,1)S(1)} %get-tuple-element.41), channel_id=1, source_target_pairs={{0,15},{1,0},{2,1},{3,2},{4,3},{5,4},{6,5},{7,6},{8,7},{9,8},{10,9... | collective-permute-start | bytes 663560 | tf_op jit(solution)/shard_map/ppermute | solution.py:389
  29.1 10.2 %all-to-all-start = ((f32[16,16,128]{2,1,0:T(8,128)}), f32[16,16,128]{2,1,0:T(8,128)S(1)}, u32[]{:S(2)}, u32[]{:S(2)}) async-start(f32[16,16,128]{2,1,0:T(8,128)} %get-tuple-element.44._), calls=%async_computation | async-start | bytes 262144 | tf_op jit(solution)/shard_map/all_to_all | solution.py:483
  32.6 19.4 %copy-start.2 = (bf16[3,5,768]{2,0,1:T(4,128)(2,1)S(1)}, bf16[3,5,768]{2,0,1:T(4,128)(2,1)}, u32[]{:S(2)}) copy-start(bf16[3,5,768]{2,0,1:T(4,128)(2,1)} %param.29) | copy-start | bytes 69124
  32.6 27.6 %copy-start = (f32[6]{0:T(128)S(1)}, f32[6]{0:T(128)}, u32[]{:S(2)}) copy-start(f32[6]{0:T(128)} %om.1) | copy-start | bytes 76
  32.7 27.6 %copy-start.1 = (s32[1,96]{1,0:T(1,128)S(1)}, s32[1,96]{1,0:T(1,128)}, u32[]{:S(2)}) copy-start(s32[1,96]{1,0:T(1,128)} %wall) | copy-start | bytes 1156
  39.9 20.3 %all-to-all-start.1 = ((f32[16,16,128]{2,1,0:T(8,128)}), f32[16,16,128]{2,1,0:T(8,128)S(1)}, u32[]{:S(2)}, u32[]{:S(2)}) async-start(f32[16,16,128]{2,1,0:T(8,128)} %merge.1), calls=%async_computation.1 | async-start | bytes 262144 | tf_op jit(solution)/shard_map/all_to_all | solution.py:491
  51.7 15.5 %collective-permute-start.4 = (bf16[48,2304]{1,0:T(8,128)(2,1)}, bf16[48,2304]{1,0:T(8,128)(2,1)S(1)}, u32[]{:S(2)}, u32[]{:S(2)}) collective-permute-start(bf16[48,2304]{1,0:T(8,128)(2,1)} %get-tuple-element.47._), channel_id=1, source_target_pairs={{0,16},{16,32},{32,48},{48,64},{64,80},{80,96},{96,112},{112,128},... | collective-permute-start | bytes 663560 | tf_op jit(solution)/shard_map/ppermute | solution.py:389
  52.0 15.2 %collective-permute-start.5 = (bf16[48,2304]{1,0:T(8,128)(2,1)}, bf16[48,2304]{1,0:T(8,128)(2,1)S(1)}, u32[]{:S(2)}, u32[]{:S(2)}) collective-permute-start(bf16[48,2304]{1,0:T(8,128)(2,1)} %get-tuple-element.56), channel_id=1, source_target_pairs={{0,240},{16,0},{32,16},{48,32},{64,48},{80,64},{96,80},{112,96},{1... | collective-permute-start | bytes 663560 | tf_op jit(solution)/shard_map/ppermute | solution.py:389
  56.7 10.6 %collective-permute-start.6 = (bf16[48,2304]{1,0:T(8,128)(2,1)}, bf16[48,2304]{1,0:T(8,128)(2,1)S(1)}, u32[]{:S(2)}, u32[]{:S(2)}) collective-permute-start(bf16[48,2304]{1,0:T(8,128)(2,1)} %get-tuple-element.57), channel_id=1, source_target_pairs={{0,1},{1,2},{2,3},{3,4},{4,5},{5,6},{6,7},{7,8},{8,9},{9,10},{10,1... | collective-permute-start | bytes 663560 | tf_op jit(solution)/shard_map/ppermute | solution.py:389
  58.9 8.4 %collective-permute-start.7 = (bf16[48,2304]{1,0:T(8,128)(2,1)}, bf16[48,2304]{1,0:T(8,128)(2,1)S(1)}, u32[]{:S(2)}, u32[]{:S(2)}) collective-permute-start(bf16[48,2304]{1,0:T(8,128)(2,1)} %get-tuple-element.58), channel_id=1, source_target_pairs={{0,15},{1,0},{2,1},{3,2},{4,3},{5,4},{6,5},{7,6},{8,7},{9,8},{10,9... | collective-permute-start | bytes 663560 | tf_op jit(solution)/shard_map/ppermute | solution.py:389
  60.2 11.6 %copy-start.3 = (s32[6,4]{0,1:T(4,128)S(1)}, s32[6,4]{0,1:T(4,128)}, u32[]{:S(2)}) copy-start(s32[6,4]{0,1:T(4,128)} %param.30) | copy-start | bytes 292
  67.3 4.6 %copy-start.4 = (bf16[48,2304]{1,0:T(8,128)(2,1)}, bf16[48,2304]{1,0:T(8,128)(2,1)S(1)}, u32[]{:S(2)}) copy-start(bf16[48,2304]{1,0:T(8,128)(2,1)S(1)} %collective-permute-done.4.b0_h) | copy-start | bytes 663556
  67.3 4.6 %copy-start.5 = (bf16[48,2304]{1,0:T(8,128)(2,1)}, bf16[48,2304]{1,0:T(8,128)(2,1)S(1)}, u32[]{:S(2)}) copy-start(bf16[48,2304]{1,0:T(8,128)(2,1)S(1)} %collective-permute-done.5.b1_h) | copy-start | bytes 663556
  67.3 4.6 %copy-start.6 = (bf16[48,2304]{1,0:T(8,128)(2,1)}, bf16[48,2304]{1,0:T(8,128)(2,1)S(1)}, u32[]{:S(2)}) copy-start(bf16[48,2304]{1,0:T(8,128)(2,1)S(1)} %collective-permute-done.6.b2_h) | copy-start | bytes 663556
  67.3 4.6 %copy-start.7 = (bf16[48,2304]{1,0:T(8,128)(2,1)}, bf16[48,2304]{1,0:T(8,128)(2,1)S(1)}, u32[]{:S(2)}) copy-start(bf16[48,2304]{1,0:T(8,128)(2,1)S(1)} %collective-permute-done.7.b3_h) | copy-start | bytes 663556
  67.3 16.7 %all-to-all-start.2 = ((bf16[16,144,128]{2,1,0:T(8,128)(2,1)}), bf16[16,144,128]{2,1,0:T(8,128)(2,1)S(1)}, u32[]{:S(2)}, u32[]{:S(2)}) async-start(bf16[16,144,128]{2,1,0:T(8,128)(2,1)} %get-tuple-element.63._), calls=%async_computation.2 | async-start | bytes 1179648 | tf_op jit(solution)/shard_map/all_to_all | solution.py:514

commit v3 on v2

--- a/solution.py
+++ b/solution.py
@@ -140,12 +140,13 @@
 
         def couple_shadow(i, x):
             for a in range(2):
-                qscr[a, pl.ds(i, 1), :] = jnp.sum(x * trsh[a], axis=0, keepdims=True)
+                qscr[a, i * 8 : i * 8 + 8, 0:E] = jnp.sum((x * trsh[a]).reshape(TRACE // 8, 8, E), axis=0)
 
         for i in range(TRACE):
             relayout(b, f, wt, f * E * WPAD, i, couple_shadow)
         for a in range(2):
-            q[a, f * E : (f + 1) * E, 0:TRACE] = qscr[a].T
+            total = sum(qscr[a, pl.ds(n, TRACE, stride=8), :] for n in range(8))
+            q[a, f * E : (f + 1) * E, 0:TRACE] = total[:, 0:E].T
             q[a, f * E : (f + 1) * E, TRACE:LANES] = jnp.zeros((E, LANES - TRACE), F32)
 
 
@@ -194,26 +195,25 @@
         col = jnp.sum(rows[k], axis=1, keepdims=True) + jnp.sum(dots[k], axis=1, keepdims=True)
         acc += jnp.where(lane == k, col, 0.0)
     red[...] = jnp.broadcast_to(acc[None], red.shape)
-    for face in range(FACES):
-        couple(t_ref, wt, face // E * E * WPAD, y_ref, VPAD, face, face % E)
     stores = []
-    for k in range(NOBJ):
-        for m in range(NBAS):
-            y = face_rows(y_ref, k * NBAS + m, VPAD)
-            for f in range(4):
-                yn[k, m, f] = y[:, f * LANES : (f + 1) * LANES]
-        stores += fetch([(yn.at[k], yn_h.at[k])], osems.at[k : k + 1])
+    for f in range(4):
+        for e in range(E):
+            couple(t_ref, wt, f * E * WPAD, y_ref, VPAD, f * E + e, e)
+        for k in range(NOBJ):
+            for m in range(NBAS):
+                yn[f, k, m] = y_ref[pl.ds(f * E * VPAD + k * NBAS + m, E, stride=VPAD), :]
+        stores += fetch([(yn.at[f], yn_h.at[f])], osems.at[f : f + 1])
     wait(*stores)
 
 
 def outgo_kernel(_, yn_h, send_h, cross_h, o0, o1, o2, o3, yn, send, cross, out, sems, osems):
-    first = [(send_h, send), (cross_h, cross)] + [(yn_h.at[k], yn.at[k]) for k in range(NOBJ)]
+    first = [(send_h, send), (cross_h, cross)] + [(yn_h.at[:, k], yn.at[:, k]) for k in range(NOBJ)]
     copies = fetch(first, sems)
     wait(*copies[:2])
     picks = [picker(send[f : f + 1, :]) for f in range(4)]
     for k in range(NOBJ):
         copies[2 + k].wait()
-        ys = [jnp.concatenate([yn[k, m, f].astype(BF16) for f in range(4)], axis=1) for m in range(NBAS)]
+        ys = [jnp.concatenate([yn[f, k, m].astype(BF16) for f in range(4)], axis=1) for m in range(NBAS)]
         total = dot(jnp.concatenate(ys, axis=0), cross[...]).astype(BF16)
         at = slice(k * STEP, (k + 1) * STEP)
         for f in range(4):
@@ -233,7 +233,7 @@
 ):
     first = [(selt_h, selt)]
     for k in range(NOBJ):
-        first += [(h.at[k], x.at[k]) for h, x in ((us_h, us), (yn_h, yn), (it_h, it))]
+        first += [(us_h.at[k], us.at[k]), (yn_h.at[:, k], yn.at[:, k]), (it_h.at[k], it.at[k])]
     copies = fetch(first + [(spread_h, spread)], sems)
     t = jnp.sum(red[...], axis=0)
     row = lambda n: t[n : n + 1]
@@ -261,7 +261,7 @@
         c = [coefs[n : n + 1, k : k + 1] for n in range(7)]
         u0, u1, u2 = (us[k, m] for m in range(NBAS))
         st1 = u0 - c[0] * u1 - c[1] * u2
-        y = [yn[k, 0, f] - c[0] * yn[k, 1, f] - c[1] * yn[k, 2, f] for f in range(4)]
+        y = [yn[f, k, 0] - c[0] * yn[f, k, 1] - c[1] * yn[f, k, 2] for f in range(4)]
         lift = lifted(jnp.concatenate(y, axis=1), selt)
         two = c[2] * u0 + c[3] * u1 + c[4] * u2 - c[5] * lift
         both = st1 + two
@@ -416,7 +416,7 @@
     fields = (NOBJ, E, BLOCK)
     traces = pltpu.VMEM((H, WIDE), BF16)
 
-    spare = (NOBJ, NBAS, 4, E, LANES)
+    spare = (4, NOBJ, NBAS, E, LANES)
     basis = (NOBJ, NBAS, E, BLOCK)
 
     row, col = lax.axis_index("row"), lax.axis_index("col")
@@ -453,7 +453,7 @@
             (VMEM, pltpu.VMEM((FACES, 2 * SLOTS), BF16)),
         ],
         buffers(blocks, shadow, selt, neighbour_perm)
-        + [pltpu.VMEM((2, TRACE, E), F32), pltpu.VMEM((3, FACES, LANES), F32), sem((7,))],
+        + [pltpu.VMEM((2, TRACE * 8, LANES), F32), pltpu.VMEM((3, FACES, LANES), F32), sem((7,))],
     )
 
     red, yn = local_call(
@@ -466,7 +466,7 @@
         [(VMEM, shape((n_row, 16, LANES), F32)), (ANY, pltpu.HBM(spare, F32))],
         [pltpu.VMEM((NOBJ, 16, LANES), F32)]
         + [pltpu.VMEM((FACES * VPAD, LANES), F32)] * 2
-        + [pltpu.VMEM(spare, F32), sem((NOBJ,))],
+        + [pltpu.VMEM(spare, F32), sem((4,))],
     )
     outgo2 = local_call(
         outgo_kernel,

time: 86 us -> 84.9 us (0.987)
  Pallas kernels: 42.5 us -> 41.4 us
    pallas_call x8, Pallas kernels: 42.5 us -> 41.4 us  [local_call(): pl.pallas_call(kernel, in_specs=[spec for spec, _ in ins], out_specs=[spe...]
  transfers between devices with their start and end apart: 11 -> 11, of which waited for: 3 -> 3; matrix products, arithmetic and copies ran while one was open for 0% -> 0% of each run, Pallas kernels for 31% -> 32%
where the time goes in v3:
time: 84.9 us; the launch traced here: 84.5 us
  Pallas kernels  41.4 us (49%)
  starting transfers between devices  35.1 us (41%)
  waiting for transfers between devices  6.32 us (7%)
  between operations  1.51 us (2%)
    pallas_call x8, Pallas kernels, local_call(): pl.pallas_call(kernel, in_specs=[spec for spec, _ in ins], out_specs=[spe...  41.4 us
    ppermute x8, starting transfers between devices, exchange(): lax.ppermute(outgo[d], axis, [(i, (i + shift) % size) for i in range(size)])  16 us
    all_to_all x1, starting transfers between devices, per_device(): red = lax.all_to_all(red_row, 'col', 0, 0, tiled=True)  11.1 us
    all_to_all x1, starting transfers between devices, per_device(): sens = lax.all_to_all(payload, 'row', 0, 0, tiled=True)  4.43 us
    all_to_all x1, waiting for transfers between devices, per_device(): sens = lax.all_to_all(payload, 'row', 0, 0, tiled=True)  3.85 us
    all_to_all x1, starting transfers between devices, per_device(): red_row = lax.all_to_all(red, 'row', 0, 0, tiled=True)  3.52 us
  transfers between devices with their start and end apart: 11, of which 3 were waited for; matrix products, arithmetic and copies ran while one was open for 0% of the time, Pallas kernels for 32%

profile of v3, /device:TPU:1, one launch (start us, length us, event | category | flops | bytes accessed | tf_op | source)
XLA Modules:
  0.0 84.5 jit_solution(459367458484153526)
XLA Ops:
  0.6 0.1 add_convert_fusion.flags
  0.7 5.9 %basis.1 = (f32[6,16,320]{2,1,0:T(8,128)S(1)}, bf16[192,2304]{1,0:T(8,128)(2,1)S(1)}, f32[6,3,96,320]{3,2,1,0:T(8,128)}, bf16[48,2304]{1,0:T(8,128)(2,1)S(1)}, b...) custom-call(s32[4]{0:T(128)S(1)} %add_convert_fusion.flags, f32[6]{0:T(128)} %om.1, ...), custom_call_target="tpu_custom_call" | custom-call | flops 2500000000 | bytes 5000000 | tf_op jit(solution)/shard_map/basis/pallas_call | solution.py:372
  6.6 2.2 %collective-permute-start = (bf16[48,2304]{1,0:T(8,128)(2,1)S(1)}, bf16[48,2304]{1,0:T(8,128)(2,1)S(1)}, u32[]{:S(2)}, u32[]{:S(2)}) collective-permute-start(bf16[48,2304]{1,0:T(8,128)(2,1)S(1)} %get-tuple-element.38), channel_id=1, source_target_pairs={{0,16},{16,32},{32,48},{48,64},{64,80},{80,96},{96,112},{112,128},... | collective-permute-start | bytes 663560 | tf_op jit(solution)/shard_map/ppermute | solution.py:389
  8.8 3.9 %collective-permute-start.1 = (bf16[48,2304]{1,0:T(8,128)(2,1)S(1)}, bf16[48,2304]{1,0:T(8,128)(2,1)S(1)}, u32[]{:S(2)}, u32[]{:S(2)}) collective-permute-start(bf16[48,2304]{1,0:T(8,128)(2,1)S(1)} %get-tuple-element.39), channel_id=1, source_target_pairs={{0,240},{16,0},{32,16},{48,32},{64,48},{80,64},{96,80},{112,96},{1... | collective-permute-start | bytes 663560 | tf_op jit(solution)/shard_map/ppermute | solution.py:389
  12.7 2.5 %collective-permute-start.2 = (bf16[48,2304]{1,0:T(8,128)(2,1)S(1)}, bf16[48,2304]{1,0:T(8,128)(2,1)S(1)}, u32[]{:S(2)}, u32[]{:S(2)}) collective-permute-start(bf16[48,2304]{1,0:T(8,128)(2,1)S(1)} %get-tuple-element.40), channel_id=1, source_target_pairs={{0,1},{1,2},{2,3},{3,4},{4,5},{5,6},{6,7},{7,8},{8,9},{9,10},{10,1... | collective-permute-start | bytes 663560 | tf_op jit(solution)/shard_map/ppermute | solution.py:389
  15.2 0.1 collective-permute-start.3
  15.3 6.2 %blocks.1 = (f32[31104,128]{1,0:T(8,128)S(1)}, f32[2,384,128]{2,1,0:T(8,128)S(1)}, bf16[384,384]{1,0:T(8,128)(2,1)S(1)}) custom-call(f32[6,16,320]{2,1,0:T(8,128)S(1)} %get-tuple-element.35._.dots, s32[1,384]{1,0:T(1,128)} %perm_h.1, bf16[4,80,80,96]{3,2,1,0:T(8,128)(2,1)} %bitcast.7, f32[2,96,320]{2,1,0:T(8,128)} %sh_h.3, ...), custom_call_target="tpu_custom_call" | custom-call | flops 3000000000 | bytes 6000000 | tf_op jit(solution)/shard_map/blocks/pallas_call | solution.py:372
  21.5 0.0 collective-permute-done.r0.a0
  21.5 0.0 collective-permute-done.1.r1.a1
  21.5 0.0 collective-permute-done.2.r2.a2
  21.5 0.0 collective-permute-done.3.r3.a3
  21.5 6.5 %apply.1 = (f32[16,16,128]{2,1,0:T(8,128)}, f32[4,6,3,96,128]{4,3,2,1,0:T(8,128)}) custom-call(s32[4]{0:T(128)S(1)} %add_convert_fusion.flags, bf16[384,384]{1,0:T(8,128)(2,1)S(1)} %get-tuple-element.36.hot, bf16[192,2304]{1,0:T(8,128)(2,1)S(1)} %get-tuple-element.37.table, bf16[48,2304]{1,0:T(8,128)(2,1)S(1)} %collective-permute-done.r0.a0, ...), custom_call_target="tpu_custom_call" | custom-call | flops 3500000000 | bytes 7000000 | tf_op jit(solution)/shard_map/apply/pallas_call | solution.py:372
  28.0 3.5 %all-to-all-start = ((f32[16,16,128]{2,1,0:T(8,128)}), f32[16,16,128]{2,1,0:T(8,128)S(1)}, u32[]{:S(2)}, u32[]{:S(2)}) async-start(f32[16,16,128]{2,1,0:T(8,128)} %get-tuple-element.44._), calls=%async_computation | async-start | bytes 262144 | tf_op jit(solution)/shard_map/all_to_all | solution.py:483
  31.5 0.0 copy-start.2
  31.5 0.0 copy-start
  31.6 0.0 copy-start.1
  31.6 5.3 %outgo.1 = (bf16[48,2304]{1,0:T(8,128)(2,1)}, bf16[48,2304]{1,0:T(8,128)(2,1)}, bf16[48,2304]{1,0:T(8,128)(2,1)}, bf16[48,2304]{1,0:T(8,128)(2,1)}) custom-call(f32[16,16,128]{2,1,0:T(8,128)} %get-tuple-element.44._, f32[4,6,3,96,128]{4,3,2,1,0:T(8,128)} %get-tuple-element.46.yn_h, s32[4,48]{1,0:T(4,128)} %send_h.3, bf16[512,512]{1,0:T(8,128)(2,1)} %constant.21.clone.cross_h), custom_call_target="tpu_custom_call" | custom-call | flops 2000000000 | bytes 4000000 | tf_op jit(solution)/shard_map/outgo/pallas_call | solution.py:372
  36.8 1.3 %all-to-all-done.x = f32[16,16,128]{2,1,0:T(8,128)S(1)} async-done(((f32[16,16,128]{2,1,0:T(8,128)}), f32[16,16,128]{2,1,0:T(8,128)S(1)}, u32[]{:S(2)}, u32[]{:S(2)}) %all-to-all-start) | async-done | bytes 131104 | tf_op jit(solution)/shard_map/all_to_all | solution.py:483
  38.2 0.7 merge.1
  38.8 11.1 %all-to-all-start.1 = ((f32[16,16,128]{2,1,0:T(8,128)}), f32[16,16,128]{2,1,0:T(8,128)S(1)}, u32[]{:S(2)}, u32[]{:S(2)}) async-start(f32[16,16,128]{2,1,0:T(8,128)} %merge.1), calls=%async_computation.1 | async-start | bytes 262144 | tf_op jit(solution)/shard_map/all_to_all | solution.py:491
  50.6 0.3 collective-permute-start.4
  50.9 0.0 copy-done.2
  50.9 4.9 %collective-permute-start.5 = (bf16[48,2304]{1,0:T(8,128)(2,1)}, bf16[48,2304]{1,0:T(8,128)(2,1)S(1)}, u32[]{:S(2)}, u32[]{:S(2)}) collective-permute-start(bf16[48,2304]{1,0:T(8,128)(2,1)} %get-tuple-element.56), channel_id=1, source_target_pairs={{0,240},{16,0},{32,16},{48,32},{64,48},{80,64},{96,80},{112,96},{1... | collective-permute-start | bytes 663560 | tf_op jit(solution)/shard_map/ppermute | solution.py:389
  55.8 2.2 %collective-permute-start.6 = (bf16[48,2304]{1,0:T(8,128)(2,1)}, bf16[48,2304]{1,0:T(8,128)(2,1)S(1)}, u32[]{:S(2)}, u32[]{:S(2)}) collective-permute-start(bf16[48,2304]{1,0:T(8,128)(2,1)} %get-tuple-element.57), channel_id=1, source_target_pairs={{0,1},{1,2},{2,3},{3,4},{4,5},{5,6},{6,7},{7,8},{8,9},{9,10},{10,1... | collective-permute-start | bytes 663560 | tf_op jit(solution)/shard_map/ppermute | solution.py:389
  58.0 0.0 collective-permute-start.7
  58.0 1.1 %all-to-all-done.1.red = f32[16,16,128]{2,1,0:T(8,128)S(1)} async-done(((f32[16,16,128]{2,1,0:T(8,128)}), f32[16,16,128]{2,1,0:T(8,128)S(1)}, u32[]{:S(2)}, u32[]{:S(2)}) %all-to-all-start.1) | async-done | bytes 131104 | tf_op jit(solution)/shard_map/all_to_all | solution.py:491
  59.1 0.0 copy-done
  59.1 0.0 copy-done.1
  59.1 0.0 copy-start.3
  59.1 7.0 %step.1 = (f32[6,96,320]{2,1,0:T(8,128)}, f32[6,96,320]{2,1,0:T(8,128)}, f32[6,48,320]{2,1,0:T(8,128)}, f32[8,128]{1,0:T(8,128)S(1)}, bf16[16,144,128]{2,1,0:T(8,128)(2,1)}) custom-call(f32[6]{0:T(128)S(1)} %copy-done, s32[1]{0:T(128)S(6)} %copy.25.count, f32[16,16,128]{2,1,0:T(8,128)S(1)} %all-to-all-done.1.red, f32[6,3,96,320]{3,2,1,0:T(8,128)} %get-tuple-element.48.us_h, ...), custom_call_target="tpu_custom_call" | custom-call | flops 3000000000 | bytes 6000000 | tf_op jit(solution)/shard_map/step/pallas_call | solution.py:372
  66.1 0.0 collective-permute-done.4.b0_h
  66.2 0.0 copy-start.4
  66.2 0.0 collective-permute-done.5.b1_h
  66.2 0.0 copy-start.5
  66.2 0.0 collective-permute-done.6.b2_h
  66.2 0.0 copy-start.6
  66.2 0.0 collective-permute-done.7.b3_h
  66.2 0.0 copy-start.7
  66.2 4.4 %all-to-all-start.2 = ((bf16[16,144,128]{2,1,0:T(8,128)(2,1)}), bf16[16,144,128]{2,1,0:T(8,128)(2,1)S(1)}, u32[]{:S(2)}, u32[]{:S(2)}) async-start(bf16[16,144,128]{2,1,0:T(8,128)(2,1)} %get-tuple-element.63._), calls=%async_computation.2 | async-start | bytes 1179648 | tf_op jit(solution)/shard_map/all_to_all | solution.py:514
  70.7 0.0 copy-done.3
  70.7 0.1 copy.24.support
  70.8 0.0 copy-done.4
  70.8 0.0 copy-done.5
  70.8 0.0 copy-done.6
  70.8 0.0 copy-done.7
  70.8 8.3 %last.1 = (f32[6,96,320]{2,1,0:T(8,128)}, bf16[6,4,128,128]{3,2,1,0:T(8,128)(2,1)S(1)}) custom-call(s32[4]{0:T(128)S(1)} %add_convert_fusion.flags, f32[8,128]{1,0:T(8,128)S(1)} %get-tuple-element.52.coefs, bf16[384,384]{1,0:T(8,128)(2,1)S(1)} %get-tuple-element.36.hot, f32[6,48,320]{2,1,0:T(8,128)} %get-tuple-element.53.st2_h, ...), custom_call_target="tpu_custom_call" | custom-call | flops 4000000000 | bytes 8000000 | tf_op jit(solution)/shard_map/last/pallas_call | solution.py:372
  79.1 3.9 %all-to-all-done.2 = bf16[16,144,128]{2,1,0:T(8,128)(2,1)S(1)} async-done(((bf16[16,144,128]{2,1,0:T(8,128)(2,1)}), bf16[16,144,128]{2,1,0:T(8,128)(2,1)S(1)}, u32[]{:S(2)}, u32[]{:S(2)}) %all-to-all-start.2) | async-done | bytes 589856 | tf_op jit(solution)/shard_map/all_to_all | solution.py:514
  82.9 1.6 %smooth.1 = f32[18,768]{1,0:T(8,128)} custom-call(s32[6,4]{1,0:T(8,128)S(1)} %copy.24.support, bf16[2304,128]{1,0:T(8,128)(2,1)S(1)} %bitcast.6, bf16[6,4,128,128]{3,2,1,0:T(8,128)(2,1)S(1)} %get-tuple-element.66.weights), custom_call_target="tpu_custom_call" | custom-call | flops 1000000000 | bytes 2000000 | tf_op jit(solution)/shard_map/smooth/pallas_call | solution.py:372
  (2 shorter events, 0.0 us)
Async XLA Ops:
  6.6 14.9 %collective-permute-start = (bf16[48,2304]{1,0:T(8,128)(2,1)S(1)}, bf16[48,2304]{1,0:T(8,128)(2,1)S(1)}, u32[]{:S(2)}, u32[]{:S(2)}) collective-permute-start(bf16[48,2304]{1,0:T(8,128)(2,1)S(1)} %get-tuple-element.38), channel_id=1, source_target_pairs={{0,16},{16,32},{32,48},{48,64},{64,80},{80,96},{96,112},{112,128},... | collective-permute-start | bytes 663560 | tf_op jit(solution)/shard_map/ppermute | solution.py:389
  8.8 12.7 %collective-permute-start.1 = (bf16[48,2304]{1,0:T(8,128)(2,1)S(1)}, bf16[48,2304]{1,0:T(8,128)(2,1)S(1)}, u32[]{:S(2)}, u32[]{:S(2)}) collective-permute-start(bf16[48,2304]{1,0:T(8,128)(2,1)S(1)} %get-tuple-element.39), channel_id=1, source_target_pairs={{0,240},{16,0},{32,16},{48,32},{64,48},{80,64},{96,80},{112,96},{1... | collective-permute-start | bytes 663560 | tf_op jit(solution)/shard_map/ppermute | solution.py:389
  12.7 8.8 %collective-permute-start.2 = (bf16[48,2304]{1,0:T(8,128)(2,1)S(1)}, bf16[48,2304]{1,0:T(8,128)(2,1)S(1)}, u32[]{:S(2)}, u32[]{:S(2)}) collective-permute-start(bf16[48,2304]{1,0:T(8,128)(2,1)S(1)} %get-tuple-element.40), channel_id=1, source_target_pairs={{0,1},{1,2},{2,3},{3,4},{4,5},{5,6},{6,7},{7,8},{8,9},{9,10},{10,1... | collective-permute-start | bytes 663560 | tf_op jit(solution)/shard_map/ppermute | solution.py:389
  15.2 6.3 %collective-permute-start.3 = (bf16[48,2304]{1,0:T(8,128)(2,1)S(1)}, bf16[48,2304]{1,0:T(8,128)(2,1)S(1)}, u32[]{:S(2)}, u32[]{:S(2)}) collective-permute-start(bf16[48,2304]{1,0:T(8,128)(2,1)S(1)} %get-tuple-element.41), channel_id=1, source_target_pairs={{0,15},{1,0},{2,1},{3,2},{4,3},{5,4},{6,5},{7,6},{8,7},{9,8},{10,9... | collective-permute-start | bytes 663560 | tf_op jit(solution)/shard_map/ppermute | solution.py:389
  28.0 10.2 %all-to-all-start = ((f32[16,16,128]{2,1,0:T(8,128)}), f32[16,16,128]{2,1,0:T(8,128)S(1)}, u32[]{:S(2)}, u32[]{:S(2)}) async-start(f32[16,16,128]{2,1,0:T(8,128)} %get-tuple-element.44._), calls=%async_computation | async-start | bytes 262144 | tf_op jit(solution)/shard_map/all_to_all | solution.py:483
  31.5 19.4 %copy-start.2 = (bf16[3,5,768]{2,0,1:T(4,128)(2,1)S(1)}, bf16[3,5,768]{2,0,1:T(4,128)(2,1)}, u32[]{:S(2)}) copy-start(bf16[3,5,768]{2,0,1:T(4,128)(2,1)} %param.29) | copy-start | bytes 69124
  31.5 27.6 %copy-start = (f32[6]{0:T(128)S(1)}, f32[6]{0:T(128)}, u32[]{:S(2)}) copy-start(f32[6]{0:T(128)} %om.1) | copy-start | bytes 76
  31.6 27.6 %copy-start.1 = (s32[1,96]{1,0:T(1,128)S(1)}, s32[1,96]{1,0:T(1,128)}, u32[]{:S(2)}) copy-start(s32[1,96]{1,0:T(1,128)} %wall) | copy-start | bytes 1156
  38.8 20.3 %all-to-all-start.1 = ((f32[16,16,128]{2,1,0:T(8,128)}), f32[16,16,128]{2,1,0:T(8,128)S(1)}, u32[]{:S(2)}, u32[]{:S(2)}) async-start(f32[16,16,128]{2,1,0:T(8,128)} %merge.1), calls=%async_computation.1 | async-start | bytes 262144 | tf_op jit(solution)/shard_map/all_to_all | solution.py:491
  50.6 15.5 %collective-permute-start.4 = (bf16[48,2304]{1,0:T(8,128)(2,1)}, bf16[48,2304]{1,0:T(8,128)(2,1)S(1)}, u32[]{:S(2)}, u32[]{:S(2)}) collective-permute-start(bf16[48,2304]{1,0:T(8,128)(2,1)} %get-tuple-element.47._), channel_id=1, source_target_pairs={{0,16},{16,32},{32,48},{48,64},{64,80},{80,96},{96,112},{112,128},... | collective-permute-start | bytes 663560 | tf_op jit(solution)/shard_map/ppermute | solution.py:389
  50.9 15.2 %collective-permute-start.5 = (bf16[48,2304]{1,0:T(8,128)(2,1)}, bf16[48,2304]{1,0:T(8,128)(2,1)S(1)}, u32[]{:S(2)}, u32[]{:S(2)}) collective-permute-start(bf16[48,2304]{1,0:T(8,128)(2,1)} %get-tuple-element.56), channel_id=1, source_target_pairs={{0,240},{16,0},{32,16},{48,32},{64,48},{80,64},{96,80},{112,96},{1... | collective-permute-start | bytes 663560 | tf_op jit(solution)/shard_map/ppermute | solution.py:389
  55.8 10.4 %collective-permute-start.6 = (bf16[48,2304]{1,0:T(8,128)(2,1)}, bf16[48,2304]{1,0:T(8,128)(2,1)S(1)}, u32[]{:S(2)}, u32[]{:S(2)}) collective-permute-start(bf16[48,2304]{1,0:T(8,128)(2,1)} %get-tuple-element.57), channel_id=1, source_target_pairs={{0,1},{1,2},{2,3},{3,4},{4,5},{5,6},{6,7},{7,8},{8,9},{9,10},{10,1... | collective-permute-start | bytes 663560 | tf_op jit(solution)/shard_map/ppermute | solution.py:389
  58.0 8.2 %collective-permute-start.7 = (bf16[48,2304]{1,0:T(8,128)(2,1)}, bf16[48,2304]{1,0:T(8,128)(2,1)S(1)}, u32[]{:S(2)}, u32[]{:S(2)}) collective-permute-start(bf16[48,2304]{1,0:T(8,128)(2,1)} %get-tuple-element.58), channel_id=1, source_target_pairs={{0,15},{1,0},{2,1},{3,2},{4,3},{5,4},{6,5},{7,6},{8,7},{9,8},{10,9... | collective-permute-start | bytes 663560 | tf_op jit(solution)/shard_map/ppermute | solution.py:389
  59.1 11.5 %copy-start.3 = (s32[6,4]{0,1:T(4,128)S(1)}, s32[6,4]{0,1:T(4,128)}, u32[]{:S(2)}) copy-start(s32[6,4]{0,1:T(4,128)} %param.30) | copy-start | bytes 292
  66.2 4.6 %copy-start.4 = (bf16[48,2304]{1,0:T(8,128)(2,1)}, bf16[48,2304]{1,0:T(8,128)(2,1)S(1)}, u32[]{:S(2)}) copy-start(bf16[48,2304]{1,0:T(8,128)(2,1)S(1)} %collective-permute-done.4.b0_h) | copy-start | bytes 663556
  66.2 4.6 %copy-start.5 = (bf16[48,2304]{1,0:T(8,128)(2,1)}, bf16[48,2304]{1,0:T(8,128)(2,1)S(1)}, u32[]{:S(2)}) copy-start(bf16[48,2304]{1,0:T(8,128)(2,1)S(1)} %collective-permute-done.5.b1_h) | copy-start | bytes 663556
  66.2 4.6 %copy-start.6 = (bf16[48,2304]{1,0:T(8,128)(2,1)}, bf16[48,2304]{1,0:T(8,128)(2,1)S(1)}, u32[]{:S(2)}) copy-start(bf16[48,2304]{1,0:T(8,128)(2,1)S(1)} %collective-permute-done.6.b2_h) | copy-start | bytes 663556
  66.2 4.6 %copy-start.7 = (bf16[48,2304]{1,0:T(8,128)(2,1)}, bf16[48,2304]{1,0:T(8,128)(2,1)S(1)}, u32[]{:S(2)}) copy-start(bf16[48,2304]{1,0:T(8,128)(2,1)S(1)} %collective-permute-done.7.b3_h) | copy-start | bytes 663556
  66.2 16.7 %all-to-all-start.2 = ((bf16[16,144,128]{2,1,0:T(8,128)(2,1)}), bf16[16,144,128]{2,1,0:T(8,128)(2,1)S(1)}, u32[]{:S(2)}, u32[]{:S(2)}) async-start(bf16[16,144,128]{2,1,0:T(8,128)(2,1)} %get-tuple-element.63._), calls=%async_computation.2 | async-start | bytes 1179648 | tf_op jit(solution)/shard_map/all_to_all | solution.py:514

commit v4 on v3

--- a/solution.py
+++ b/solution.py
@@ -211,6 +211,7 @@
     copies = fetch(first, sems)
     wait(*copies[:2])
     picks = [picker(send[f : f + 1, :]) for f in range(4)]
+    stores = []
     for k in range(NOBJ):
         copies[2 + k].wait()
         ys = [jnp.concatenate([yn[f, k, m].astype(BF16) for f in range(4)], axis=1) for m in range(NBAS)]
@@ -220,7 +221,9 @@
             lanes = slice(f * LANES, (f + 1) * LANES)
             face = jnp.concatenate([total[m * E : (m + 1) * E, lanes] for m in range(NBAS)], axis=1)
             out[f, :, at] = dot(picks[f], face).astype(BF16)
-    wait(*fetch([(out.at[f], o) for f, o in enumerate((o0, o1, o2, o3))], osems))
+        outs = [(out.at[f, :, at], o.at[:, at]) for f, o in enumerate((o0, o1, o2, o3))]
+        stores += fetch(outs, osems.at[4 * k : 4 * k + 4])
+    wait(*stores)
 
 
 def solve(m00, m01, m10, m11, f0, f1):
@@ -477,7 +480,7 @@
         [(ANY, pltpu.HBM((H, WIDE), BF16))] * 4,
         [pltpu.VMEM(spare, F32)]
         + buffers(send_list, cross)
-        + [pltpu.VMEM((4, H, WIDE), BF16), sem((2 + NOBJ,)), sem((4,))],
+        + [pltpu.VMEM((4, H, WIDE), BF16), sem((2 + NOBJ,)), sem((4 * NOBJ,))],
     )
     recv2 = exchange(outgo2)
     red_row = lax.all_to_all(red, "row", 0, 0, tiled=True)

time: 84.9 us -> 84.8 us (level)
  no operation moved by 1% of the time
where the time goes in v4:
time: 84.8 us; the launch traced here: 84.4 us
  Pallas kernels  41.3 us (49%)
  starting transfers between devices  35 us (41%)
  waiting for transfers between devices  6.38 us (8%)
  between operations  1.51 us (2%)
    pallas_call x8, Pallas kernels, local_call(): pl.pallas_call(kernel, in_specs=[spec for spec, _ in ins], out_specs=[spe...  41.3 us
    ppermute x8, starting transfers between devices, exchange(): lax.ppermute(outgo[d], axis, [(i, (i + shift) % size) for i in range(size)])  16 us
    all_to_all x1, starting transfers between devices, per_device(): red = lax.all_to_all(red_row, 'col', 0, 0, tiled=True)  11.1 us
    all_to_all x1, starting transfers between devices, per_device(): sens = lax.all_to_all(payload, 'row', 0, 0, tiled=True)  4.36 us
    all_to_all x1, waiting for transfers between devices, per_device(): sens = lax.all_to_all(payload, 'row', 0, 0, tiled=True)  3.85 us
    all_to_all x1, starting transfers between devices, per_device(): red_row = lax.all_to_all(red, 'row', 0, 0, tiled=True)  3.52 us
  transfers between devices with their start and end apart: 11, of which 3 were waited for; matrix products, arithmetic and copies ran while one was open for 0% of the time, Pallas kernels for 32%

profile of v4, /device:TPU:1, one launch (start us, length us, event | category | flops | bytes accessed | tf_op | source)
XLA Modules:
  0.0 84.4 jit_solution(15722649280990225897)
XLA Ops:
  0.6 0.1 add_convert_fusion.flags
  0.7 5.9 %basis.1 = (f32[6,16,320]{2,1,0:T(8,128)S(1)}, bf16[192,2304]{1,0:T(8,128)(2,1)S(1)}, f32[6,3,96,320]{3,2,1,0:T(8,128)}, bf16[48,2304]{1,0:T(8,128)(2,1)S(1)}, b...) custom-call(s32[4]{0:T(128)S(1)} %add_convert_fusion.flags, f32[6]{0:T(128)} %om.1, ...), custom_call_target="tpu_custom_call" | custom-call | flops 2500000000 | bytes 5000000 | tf_op jit(solution)/shard_map/basis/pallas_call | solution.py:375
  6.6 2.2 %collective-permute-start = (bf16[48,2304]{1,0:T(8,128)(2,1)S(1)}, bf16[48,2304]{1,0:T(8,128)(2,1)S(1)}, u32[]{:S(2)}, u32[]{:S(2)}) collective-permute-start(bf16[48,2304]{1,0:T(8,128)(2,1)S(1)} %get-tuple-element.38), channel_id=1, source_target_pairs={{0,16},{16,32},{32,48},{48,64},{64,80},{80,96},{96,112},{112,128},... | collective-permute-start | bytes 663560 | tf_op jit(solution)/shard_map/ppermute | solution.py:392
  8.8 3.9 %collective-permute-start.1 = (bf16[48,2304]{1,0:T(8,128)(2,1)S(1)}, bf16[48,2304]{1,0:T(8,128)(2,1)S(1)}, u32[]{:S(2)}, u32[]{:S(2)}) collective-permute-start(bf16[48,2304]{1,0:T(8,128)(2,1)S(1)} %get-tuple-element.39), channel_id=1, source_target_pairs={{0,240},{16,0},{32,16},{48,32},{64,48},{80,64},{96,80},{112,96},{1... | collective-permute-start | bytes 663560 | tf_op jit(solution)/shard_map/ppermute | solution.py:392
  12.7 2.5 %collective-permute-start.2 = (bf16[48,2304]{1,0:T(8,128)(2,1)S(1)}, bf16[48,2304]{1,0:T(8,128)(2,1)S(1)}, u32[]{:S(2)}, u32[]{:S(2)}) collective-permute-start(bf16[48,2304]{1,0:T(8,128)(2,1)S(1)} %get-tuple-element.40), channel_id=1, source_target_pairs={{0,1},{1,2},{2,3},{3,4},{4,5},{5,6},{6,7},{7,8},{8,9},{9,10},{10,1... | collective-permute-start | bytes 663560 | tf_op jit(solution)/shard_map/ppermute | solution.py:392
  15.2 0.1 collective-permute-start.3
  15.3 6.2 %blocks.1 = (f32[31104,128]{1,0:T(8,128)S(1)}, f32[2,384,128]{2,1,0:T(8,128)S(1)}, bf16[384,384]{1,0:T(8,128)(2,1)S(1)}) custom-call(f32[6,16,320]{2,1,0:T(8,128)S(1)} %get-tuple-element.35._.dots, s32[1,384]{1,0:T(1,128)} %perm_h.1, bf16[4,80,80,96]{3,2,1,0:T(8,128)(2,1)} %bitcast.7, f32[2,96,320]{2,1,0:T(8,128)} %sh_h.3, ...), custom_call_target="tpu_custom_call" | custom-call | flops 3000000000 | bytes 6000000 | tf_op jit(solution)/shard_map/blocks/pallas_call | solution.py:375
  21.5 0.0 collective-permute-done.r0.a0
  21.5 0.0 collective-permute-done.1.r1.a1
  21.5 0.0 collective-permute-done.2.r2.a2
  21.5 0.0 collective-permute-done.3.r3.a3
  21.5 6.5 %apply.1 = (f32[16,16,128]{2,1,0:T(8,128)}, f32[4,6,3,96,128]{4,3,2,1,0:T(8,128)}) custom-call(s32[4]{0:T(128)S(1)} %add_convert_fusion.flags, bf16[384,384]{1,0:T(8,128)(2,1)S(1)} %get-tuple-element.36.hot, bf16[192,2304]{1,0:T(8,128)(2,1)S(1)} %get-tuple-element.37.table, bf16[48,2304]{1,0:T(8,128)(2,1)S(1)} %collective-permute-done.r0.a0, ...), custom_call_target="tpu_custom_call" | custom-call | flops 3500000000 | bytes 7000000 | tf_op jit(solution)/shard_map/apply/pallas_call | solution.py:375
  28.0 3.5 %all-to-all-start = ((f32[16,16,128]{2,1,0:T(8,128)}), f32[16,16,128]{2,1,0:T(8,128)S(1)}, u32[]{:S(2)}, u32[]{:S(2)}) async-start(f32[16,16,128]{2,1,0:T(8,128)} %get-tuple-element.44._), calls=%async_computation | async-start | bytes 262144 | tf_op jit(solution)/shard_map/all_to_all | solution.py:486
  31.5 0.0 copy-start.2
  31.5 0.0 copy-start
  31.6 0.0 copy-start.1
  31.6 5.2 %outgo.1 = (bf16[48,2304]{1,0:T(8,128)(2,1)}, bf16[48,2304]{1,0:T(8,128)(2,1)}, bf16[48,2304]{1,0:T(8,128)(2,1)}, bf16[48,2304]{1,0:T(8,128)(2,1)}) custom-call(f32[16,16,128]{2,1,0:T(8,128)} %get-tuple-element.44._, f32[4,6,3,96,128]{4,3,2,1,0:T(8,128)} %get-tuple-element.46.yn_h, s32[4,48]{1,0:T(4,128)} %send_h.3, bf16[512,512]{1,0:T(8,128)(2,1)} %constant.21.clone.cross_h), custom_call_target="tpu_custom_call" | custom-call | flops 2000000000 | bytes 4000000 | tf_op jit(solution)/shard_map/outgo/pallas_call | solution.py:375
  36.8 1.4 %all-to-all-done.x = f32[16,16,128]{2,1,0:T(8,128)S(1)} async-done(((f32[16,16,128]{2,1,0:T(8,128)}), f32[16,16,128]{2,1,0:T(8,128)S(1)}, u32[]{:S(2)}, u32[]{:S(2)}) %all-to-all-start) | async-done | bytes 131104 | tf_op jit(solution)/shard_map/all_to_all | solution.py:486
  38.2 0.7 merge.1
  38.8 11.1 %all-to-all-start.1 = ((f32[16,16,128]{2,1,0:T(8,128)}), f32[16,16,128]{2,1,0:T(8,128)S(1)}, u32[]{:S(2)}, u32[]{:S(2)}) async-start(f32[16,16,128]{2,1,0:T(8,128)} %merge.1), calls=%async_computation.1 | async-start | bytes 262144 | tf_op jit(solution)/shard_map/all_to_all | solution.py:494
  50.6 0.3 collective-permute-start.4
  50.9 0.0 copy-done.2
  50.9 4.9 %collective-permute-start.5 = (bf16[48,2304]{1,0:T(8,128)(2,1)}, bf16[48,2304]{1,0:T(8,128)(2,1)S(1)}, u32[]{:S(2)}, u32[]{:S(2)}) collective-permute-start(bf16[48,2304]{1,0:T(8,128)(2,1)} %get-tuple-element.56), channel_id=1, source_target_pairs={{0,240},{16,0},{32,16},{48,32},{64,48},{80,64},{96,80},{112,96},{1... | collective-permute-start | bytes 663560 | tf_op jit(solution)/shard_map/ppermute | solution.py:392
  55.8 2.2 %collective-permute-start.6 = (bf16[48,2304]{1,0:T(8,128)(2,1)}, bf16[48,2304]{1,0:T(8,128)(2,1)S(1)}, u32[]{:S(2)}, u32[]{:S(2)}) collective-permute-start(bf16[48,2304]{1,0:T(8,128)(2,1)} %get-tuple-element.57), channel_id=1, source_target_pairs={{0,1},{1,2},{2,3},{3,4},{4,5},{5,6},{6,7},{7,8},{8,9},{9,10},{10,1... | collective-permute-start | bytes 663560 | tf_op jit(solution)/shard_map/ppermute | solution.py:392
  58.0 0.0 collective-permute-start.7
  58.0 1.1 %all-to-all-done.1.red = f32[16,16,128]{2,1,0:T(8,128)S(1)} async-done(((f32[16,16,128]{2,1,0:T(8,128)}), f32[16,16,128]{2,1,0:T(8,128)S(1)}, u32[]{:S(2)}, u32[]{:S(2)}) %all-to-all-start.1) | async-done | bytes 131104 | tf_op jit(solution)/shard_map/all_to_all | solution.py:494
  59.1 0.0 copy-done
  59.1 0.0 copy-done.1
  59.1 0.0 copy-start.3
  59.1 7.0 %step.1 = (f32[6,96,320]{2,1,0:T(8,128)}, f32[6,96,320]{2,1,0:T(8,128)}, f32[6,48,320]{2,1,0:T(8,128)}, f32[8,128]{1,0:T(8,128)S(1)}, bf16[16,144,128]{2,1,0:T(8,128)(2,1)}) custom-call(f32[6]{0:T(128)S(1)} %copy-done, s32[1]{0:T(128)S(6)} %copy.25.count, f32[16,16,128]{2,1,0:T(8,128)S(1)} %all-to-all-done.1.red, f32[6,3,96,320]{3,2,1,0:T(8,128)} %get-tuple-element.48.us_h, ...), custom_call_target="tpu_custom_call" | custom-call | flops 3000000000 | bytes 6000000 | tf_op jit(solution)/shard_map/step/pallas_call | solution.py:375
  66.1 0.0 collective-permute-done.4.b0_h
  66.2 0.0 copy-start.4
  66.2 0.0 collective-permute-done.5.b1_h
  66.2 0.0 copy-start.5
  66.2 0.0 collective-permute-done.6.b2_h
  66.2 0.0 copy-start.6
  66.2 0.0 collective-permute-done.7.b3_h
  66.2 0.0 copy-start.7
  66.2 4.4 %all-to-all-start.2 = ((bf16[16,144,128]{2,1,0:T(8,128)(2,1)}), bf16[16,144,128]{2,1,0:T(8,128)(2,1)S(1)}, u32[]{:S(2)}, u32[]{:S(2)}) async-start(bf16[16,144,128]{2,1,0:T(8,128)(2,1)} %get-tuple-element.63._), calls=%async_computation.2 | async-start | bytes 1179648 | tf_op jit(solution)/shard_map/all_to_all | solution.py:517
  70.6 0.0 copy-done.3
  70.6 0.1 copy.24.support
  70.7 0.0 copy-done.4
  70.7 0.0 copy-done.5
  70.7 0.0 copy-done.6
  70.7 0.0 copy-done.7
  70.7 8.3 %last.1 = (f32[6,96,320]{2,1,0:T(8,128)}, bf16[6,4,128,128]{3,2,1,0:T(8,128)(2,1)S(1)}) custom-call(s32[4]{0:T(128)S(1)} %add_convert_fusion.flags, f32[8,128]{1,0:T(8,128)S(1)} %get-tuple-element.52.coefs, bf16[384,384]{1,0:T(8,128)(2,1)S(1)} %get-tuple-element.36.hot, f32[6,48,320]{2,1,0:T(8,128)} %get-tuple-element.53.st2_h, ...), custom_call_target="tpu_custom_call" | custom-call | flops 4000000000 | bytes 8000000 | tf_op jit(solution)/shard_map/last/pallas_call | solution.py:375
  79.0 3.9 %all-to-all-done.2 = bf16[16,144,128]{2,1,0:T(8,128)(2,1)S(1)} async-done(((bf16[16,144,128]{2,1,0:T(8,128)(2,1)}), bf16[16,144,128]{2,1,0:T(8,128)(2,1)S(1)}, u32[]{:S(2)}, u32[]{:S(2)}) %all-to-all-start.2) | async-done | bytes 589856 | tf_op jit(solution)/shard_map/all_to_all | solution.py:517
  82.8 1.6 %smooth.1 = f32[18,768]{1,0:T(8,128)} custom-call(s32[6,4]{1,0:T(8,128)S(1)} %copy.24.support, bf16[2304,128]{1,0:T(8,128)(2,1)S(1)} %bitcast.6, bf16[6,4,128,128]{3,2,1,0:T(8,128)(2,1)S(1)} %get-tuple-element.66.weights), custom_call_target="tpu_custom_call" | custom-call | flops 1000000000 | bytes 2000000 | tf_op jit(solution)/shard_map/smooth/pallas_call | solution.py:375
  (2 shorter events, 0.0 us)
Async XLA Ops:
  6.6 14.9 %collective-permute-start = (bf16[48,2304]{1,0:T(8,128)(2,1)S(1)}, bf16[48,2304]{1,0:T(8,128)(2,1)S(1)}, u32[]{:S(2)}, u32[]{:S(2)}) collective-permute-start(bf16[48,2304]{1,0:T(8,128)(2,1)S(1)} %get-tuple-element.38), channel_id=1, source_target_pairs={{0,16},{16,32},{32,48},{48,64},{64,80},{80,96},{96,112},{112,128},... | collective-permute-start | bytes 663560 | tf_op jit(solution)/shard_map/ppermute | solution.py:392
  8.8 12.7 %collective-permute-start.1 = (bf16[48,2304]{1,0:T(8,128)(2,1)S(1)}, bf16[48,2304]{1,0:T(8,128)(2,1)S(1)}, u32[]{:S(2)}, u32[]{:S(2)}) collective-permute-start(bf16[48,2304]{1,0:T(8,128)(2,1)S(1)} %get-tuple-element.39), channel_id=1, source_target_pairs={{0,240},{16,0},{32,16},{48,32},{64,48},{80,64},{96,80},{112,96},{1... | collective-permute-start | bytes 663560 | tf_op jit(solution)/shard_map/ppermute | solution.py:392
  12.7 8.8 %collective-permute-start.2 = (bf16[48,2304]{1,0:T(8,128)(2,1)S(1)}, bf16[48,2304]{1,0:T(8,128)(2,1)S(1)}, u32[]{:S(2)}, u32[]{:S(2)}) collective-permute-start(bf16[48,2304]{1,0:T(8,128)(2,1)S(1)} %get-tuple-element.40), channel_id=1, source_target_pairs={{0,1},{1,2},{2,3},{3,4},{4,5},{5,6},{6,7},{7,8},{8,9},{9,10},{10,1... | collective-permute-start | bytes 663560 | tf_op jit(solution)/shard_map/ppermute | solution.py:392
  15.2 6.3 %collective-permute-start.3 = (bf16[48,2304]{1,0:T(8,128)(2,1)S(1)}, bf16[48,2304]{1,0:T(8,128)(2,1)S(1)}, u32[]{:S(2)}, u32[]{:S(2)}) collective-permute-start(bf16[48,2304]{1,0:T(8,128)(2,1)S(1)} %get-tuple-element.41), channel_id=1, source_target_pairs={{0,15},{1,0},{2,1},{3,2},{4,3},{5,4},{6,5},{7,6},{8,7},{9,8},{10,9... | collective-permute-start | bytes 663560 | tf_op jit(solution)/shard_map/ppermute | solution.py:392
  28.0 10.2 %all-to-all-start = ((f32[16,16,128]{2,1,0:T(8,128)}), f32[16,16,128]{2,1,0:T(8,128)S(1)}, u32[]{:S(2)}, u32[]{:S(2)}) async-start(f32[16,16,128]{2,1,0:T(8,128)} %get-tuple-element.44._), calls=%async_computation | async-start | bytes 262144 | tf_op jit(solution)/shard_map/all_to_all | solution.py:486
  31.5 19.4 %copy-start.2 = (bf16[3,5,768]{2,0,1:T(4,128)(2,1)S(1)}, bf16[3,5,768]{2,0,1:T(4,128)(2,1)}, u32[]{:S(2)}) copy-start(bf16[3,5,768]{2,0,1:T(4,128)(2,1)} %param.29) | copy-start | bytes 69124
  31.5 27.6 %copy-start = (f32[6]{0:T(128)S(1)}, f32[6]{0:T(128)}, u32[]{:S(2)}) copy-start(f32[6]{0:T(128)} %om.1) | copy-start | bytes 76
  31.6 27.6 %copy-start.1 = (s32[1,96]{1,0:T(1,128)S(1)}, s32[1,96]{1,0:T(1,128)}, u32[]{:S(2)}) copy-start(s32[1,96]{1,0:T(1,128)} %wall) | copy-start | bytes 1156
  38.8 20.3 %all-to-all-start.1 = ((f32[16,16,128]{2,1,0:T(8,128)}), f32[16,16,128]{2,1,0:T(8,128)S(1)}, u32[]{:S(2)}, u32[]{:S(2)}) async-start(f32[16,16,128]{2,1,0:T(8,128)} %merge.1), calls=%async_computation.1 | async-start | bytes 262144 | tf_op jit(solution)/shard_map/all_to_all | solution.py:494
  50.6 15.5 %collective-permute-start.4 = (bf16[48,2304]{1,0:T(8,128)(2,1)}, bf16[48,2304]{1,0:T(8,128)(2,1)S(1)}, u32[]{:S(2)}, u32[]{:S(2)}) collective-permute-start(bf16[48,2304]{1,0:T(8,128)(2,1)} %get-tuple-element.47._), channel_id=1, source_target_pairs={{0,16},{16,32},{32,48},{48,64},{64,80},{80,96},{96,112},{112,128},... | collective-permute-start | bytes 663560 | tf_op jit(solution)/shard_map/ppermute | solution.py:392
  50.9 15.2 %collective-permute-start.5 = (bf16[48,2304]{1,0:T(8,128)(2,1)}, bf16[48,2304]{1,0:T(8,128)(2,1)S(1)}, u32[]{:S(2)}, u32[]{:S(2)}) collective-permute-start(bf16[48,2304]{1,0:T(8,128)(2,1)} %get-tuple-element.56), channel_id=1, source_target_pairs={{0,240},{16,0},{32,16},{48,32},{64,48},{80,64},{96,80},{112,96},{1... | collective-permute-start | bytes 663560 | tf_op jit(solution)/shard_map/ppermute | solution.py:392
  55.8 10.4 %collective-permute-start.6 = (bf16[48,2304]{1,0:T(8,128)(2,1)}, bf16[48,2304]{1,0:T(8,128)(2,1)S(1)}, u32[]{:S(2)}, u32[]{:S(2)}) collective-permute-start(bf16[48,2304]{1,0:T(8,128)(2,1)} %get-tuple-element.57), channel_id=1, source_target_pairs={{0,1},{1,2},{2,3},{3,4},{4,5},{5,6},{6,7},{7,8},{8,9},{9,10},{10,1... | collective-permute-start | bytes 663560 | tf_op jit(solution)/shard_map/ppermute | solution.py:392
  58.0 8.2 %collective-permute-start.7 = (bf16[48,2304]{1,0:T(8,128)(2,1)}, bf16[48,2304]{1,0:T(8,128)(2,1)S(1)}, u32[]{:S(2)}, u32[]{:S(2)}) collective-permute-start(bf16[48,2304]{1,0:T(8,128)(2,1)} %get-tuple-element.58), channel_id=1, source_target_pairs={{0,15},{1,0},{2,1},{3,2},{4,3},{5,4},{6,5},{7,6},{8,7},{9,8},{10,9... | collective-permute-start | bytes 663560 | tf_op jit(solution)/shard_map/ppermute | solution.py:392
  59.1 11.5 %copy-start.3 = (s32[6,4]{0,1:T(4,128)S(1)}, s32[6,4]{0,1:T(4,128)}, u32[]{:S(2)}) copy-start(s32[6,4]{0,1:T(4,128)} %param.30) | copy-start | bytes 292
  66.2 4.5 %copy-start.4 = (bf16[48,2304]{1,0:T(8,128)(2,1)}, bf16[48,2304]{1,0:T(8,128)(2,1)S(1)}, u32[]{:S(2)}) copy-start(bf16[48,2304]{1,0:T(8,128)(2,1)S(1)} %collective-permute-done.4.b0_h) | copy-start | bytes 663556
  66.2 4.5 %copy-start.5 = (bf16[48,2304]{1,0:T(8,128)(2,1)}, bf16[48,2304]{1,0:T(8,128)(2,1)S(1)}, u32[]{:S(2)}) copy-start(bf16[48,2304]{1,0:T(8,128)(2,1)S(1)} %collective-permute-done.5.b1_h) | copy-start | bytes 663556
  66.2 4.5 %copy-start.6 = (bf16[48,2304]{1,0:T(8,128)(2,1)}, bf16[48,2304]{1,0:T(8,128)(2,1)S(1)}, u32[]{:S(2)}) copy-start(bf16[48,2304]{1,0:T(8,128)(2,1)S(1)} %collective-permute-done.6.b2_h) | copy-start | bytes 663556
  66.2 4.5 %copy-start.7 = (bf16[48,2304]{1,0:T(8,128)(2,1)}, bf16[48,2304]{1,0:T(8,128)(2,1)S(1)}, u32[]{:S(2)}) copy-start(bf16[48,2304]{1,0:T(8,128)(2,1)S(1)} %collective-permute-done.7.b3_h) | copy-start | bytes 663556
  66.2 16.6 %all-to-all-start.2 = ((bf16[16,144,128]{2,1,0:T(8,128)(2,1)}), bf16[16,144,128]{2,1,0:T(8,128)(2,1)S(1)}, u32[]{:S(2)}, u32[]{:S(2)}) async-start(bf16[16,144,128]{2,1,0:T(8,128)(2,1)} %get-tuple-element.63._), calls=%async_computation.2 | async-start | bytes 1179648 | tf_op jit(solution)/shard_map/all_to_all | solution.py:517
